TPU v7x, 32 devices: a whole 2x2x4 slice. The times are simulated.
32 devices in a mesh: ta: 2 (over x), gx: 16 (over z, y, core).
Axes of the slice: x: 2, y: 2, z: 4, core: 2. Of those that a mesh axis runs over, the one named last changes fastest.
Arguments:
- gauge_links: float32 [3, 2, 3, 3, 32, 9216], P(None, None, None, None, ('ta', 'gx')), parts along dimension 4, may hold values from -1 to 1, as said below
Outputs:
- fixed_links: float32 [3, 2, 3, 3, 32, 9216], P(None, None, None, None, ('ta', 'gx')), parts along dimension 4
- drift_values: float32 [2], P('ta'), parts along dimension 0
There are 2 independent parts, one for each index of `ta`. A program takes and returns all parts, laid end to end along the dimension named above; each array names one. Nothing has to cross between parts.
Inputs may be any that keep to these rules, and one draw needn't show every extreme that they name: `gauge_links`: for every direction and site the complex matrix is unitary.
All inputs are finite; a program needn't handle non-finite values.
Results may differ from a plain program's by a relative error of at most 0.0003.
Values sent between devices are 32-bit elements; how exact they have to be, the bound alone decides.
No kernel may reach another device: no remote copies, remote signals or barrier semaphores. Data moves between devices by JAX's collectives and lax.ppermute only.
A program may use at most 128 MiB of HBM per device.

v0:
```python
import math

import jax
import jax.numpy as jnp
from jax import lax
from jax.sharding import PartitionSpec as P

SIDE = 96


step_size = 0.08
peak_square = 12.0


def passed_along(block, axis, distance):
    devices = range(lax.axis_size(axis))
    route = [((i - distance) % len(devices), i) for i in devices]
    return lax.ppermute(block, axis, route)


def matrix_mul(left, right):
    rows_list = []
    for i in range(3):
        line = []
        for j in range(3):
            line.append(
                left[i, 0] * right[0, j] + left[i, 1] * right[1, j] + left[i, 2] * right[2, j]
            )
        rows_list.append(jnp.stack(line))
    return jnp.stack(rows_list)


def complex_mul(left, right):
    real_part = matrix_mul(left[0], right[0]) - matrix_mul(left[1], right[1])
    imag_part = matrix_mul(left[0], right[1]) + matrix_mul(left[1], right[0])
    return (real_part, imag_part)


def dagger(matrix):
    return (jnp.swapaxes(matrix[0], 0, 1), -jnp.swapaxes(matrix[1], 0, 1))


def scalar_mul(left, right):
    return (left[0] * right[0] - left[1] * right[1], left[0] * right[1] + left[1] * right[0])


def inverse_three(real_part, imag_part):

    def entry(i, j):
        return (real_part[i % 3, j % 3], imag_part[i % 3, j % 3])

    cofactor = []
    for i in range(3):
        row_list = []
        for j in range(3):
            first = scalar_mul(entry(i + 1, j + 1), entry(i + 2, j + 2))
            second = scalar_mul(entry(i + 1, j + 2), entry(i + 2, j + 1))
            row_list.append((first[0] - second[0], first[1] - second[1]))
        cofactor.append(row_list)
    det_real = 0.0
    det_imag = 0.0
    for j in range(3):
        term = scalar_mul(entry(0, j), cofactor[0][j])
        det_real = det_real + term[0]
        det_imag = det_imag + term[1]
    denom = det_real * det_real + det_imag * det_imag
    recip = (det_real / denom, -det_imag / denom)
    rows_real = []
    rows_imag = []
    for i in range(3):
        line_real = []
        line_imag = []
        for j in range(3):
            value = scalar_mul(cofactor[j][i], recip)
            line_real.append(value[0])
            line_imag.append(value[1])
        rows_real.append(jnp.stack(line_real))
        rows_imag.append(jnp.stack(line_imag))
    return (jnp.stack(rows_real), jnp.stack(rows_imag))


def identity_like(array):
    return jnp.eye(3, dtype=jnp.float32).reshape((3, 3) + (1,) * (array.ndim - 2))


def cayley(matrix):
    eye_full = identity_like(matrix[0])
    lower_real, lower_imag = inverse_three(eye_full - 0.5 * matrix[0], -0.5 * matrix[1])
    upper = (eye_full + 0.5 * matrix[0], 0.5 * matrix[1])
    return complex_mul(upper, (lower_real, lower_imag))


def rebuild(fields):
    empty_part = jnp.zeros_like(fields[0])
    rows_real = [
        [empty_part, fields[2], fields[4]],
        [-fields[2], empty_part, fields[6]],
        [-fields[4], -fields[6], empty_part],
    ]
    rows_imag = [
        [fields[0], fields[3], fields[5]],
        [fields[3], fields[1], fields[7]],
        [fields[5], fields[7], -(fields[0] + fields[1])],
    ]
    return (
        jnp.stack([jnp.stack(r) for r in rows_real]),
        jnp.stack([jnp.stack(r) for r in rows_imag]),
    )


def traceless(div_real, div_imag):
    anti_real = 0.5 * (div_real - jnp.swapaxes(div_real, 0, 1))
    anti_imag = 0.5 * (div_imag + jnp.swapaxes(div_imag, 0, 1))
    trace_part = (anti_imag[0, 0] + anti_imag[1, 1] + anti_imag[2, 2]) / 3.0
    anti_imag = anti_imag - identity_like(anti_imag) * trace_part
    fields = jnp.stack(
        [
            anti_imag[0, 0],
            anti_imag[1, 1],
            anti_real[0, 1],
            anti_imag[0, 1],
            anti_real[0, 2],
            anti_imag[0, 2],
            anti_real[1, 2],
            anti_imag[1, 2],
        ]
    )
    return (anti_real, anti_imag, fields)


def sine_square(index, length):
    value = jnp.sin(index.astype(jnp.float32) * (math.pi / length))
    return 4.0 * value * value


def tables(length):
    index = jnp.arange(length, dtype=jnp.int32)
    phase = index[:, None] * index[None, :] % length
    angle = phase.astype(jnp.float32) * (2.0 * math.pi / length)
    return (jnp.cos(angle), jnp.sin(angle))


def transform(matrix, array, form):
    return jnp.einsum(form, matrix, array, precision=lax.Precision.HIGHEST)


def along(real_part, imag_part, cosine, sine, sign, form):
    new_real = transform(cosine, real_part, form) + sign * transform(sine, imag_part, form)
    new_imag = transform(cosine, imag_part, form) - sign * transform(sine, real_part, form)
    return (new_real, new_imag)


def smooth(fields, count_x, side):
    planes = fields.shape[1]
    cells = side * side
    cos_side, sin_side = tables(side)
    cos_x, sin_x = tables(count_x)
    real_part = transform(cos_side, fields, "kz,cxyz->cxyk")
    imag_part = -transform(sin_side, fields, "kz,cxyz->cxyk")
    real_part, imag_part = along(real_part, imag_part, cos_side, sin_side, 1.0, "ky,cxyz->cxkz")
    count = real_part.shape[0]
    real_part = real_part.reshape(count, planes, cells)
    imag_part = imag_part.reshape(count, planes, cells)
    pieces = (
        lax.all_to_all(real_part, "gx", split_axis=2, concat_axis=1, tiled=True),
        lax.all_to_all(imag_part, "gx", split_axis=2, concat_axis=1, tiled=True),
    )
    width = pieces[0].shape[2]
    start = lax.axis_index("gx") * width
    merged = start + jnp.arange(width, dtype=jnp.int32)
    square_x = sine_square(jnp.arange(count_x, dtype=jnp.int32), count_x)
    square_yz = sine_square(merged // side, side) + sine_square(merged % side, side)
    total = square_x[:, None] + square_yz[None, :]
    safe = jnp.where(total > 0, total, 1.0)
    kernel = jnp.where(total > 0, peak_square / safe, 0.0) / (count_x * cells)
    wave_real, wave_imag = along(pieces[0], pieces[1], cos_x, sin_x, 1.0, "kx,cxs->cks")
    wave_real = wave_real * kernel[None]
    wave_imag = wave_imag * kernel[None]
    wave_real, wave_imag = along(wave_real, wave_imag, cos_x, sin_x, -1.0, "kx,cxs->cks")
    real_part = lax.all_to_all(wave_real, "gx", split_axis=1, concat_axis=2, tiled=True)
    imag_part = lax.all_to_all(wave_imag, "gx", split_axis=1, concat_axis=2, tiled=True)
    real_part = real_part.reshape(count, planes, side, side)
    imag_part = imag_part.reshape(count, planes, side, side)
    real_part, imag_part = along(real_part, imag_part, cos_side, sin_side, -1.0, "ky,cxyz->cxkz")
    real_part, imag_part = along(real_part, imag_part, cos_side, sin_side, -1.0, "kz,cxyz->cxyk")
    return real_part


def local(gauge_links):
    planes = gauge_links.shape[4]
    count_x = planes * lax.axis_size("gx")
    side = SIDE
    cells = side * side
    state = gauge_links
    cube = state.reshape(3, 2, 3, 3, planes, side, side)
    edge_part = state[0, :, :, :, planes - 1 : planes, :]
    unused_real, unused_imag, edge_fields = traceless(edge_part[0], edge_part[1])
    lower_set = passed_along(edge_fields, "gx", 1)
    empty_plane = jnp.zeros_like(state[0, :, :, :, 0:1, :])
    back_x = jnp.concatenate([empty_plane, state[0, :, :, :, : planes - 1, :]], axis=3)
    diverge = back_x.reshape(2, 3, 3, planes, side, side) - cube[0]
    diverge = diverge + jnp.roll(cube[1], 1, axis=4) - cube[1]
    diverge = diverge + jnp.roll(cube[2], 1, axis=5) - cube[2]
    anti_real, anti_imag, fields = traceless(diverge[0], diverge[1])
    add_real, add_imag = rebuild(lower_set)
    anti_real = anti_real + add_real.reshape(3, 3, planes, side, side)
    anti_imag = anti_imag + add_imag.reshape(3, 3, planes, side, side)
    fields = fields + lower_set.reshape(8, planes, side, side)
    values = [jnp.sum(anti_real * anti_real + anti_imag * anti_imag) / (9.0 * count_x * cells)]
    filtered = smooth(fields, count_x, side)
    rotation = cayley(rebuild(step_size * filtered))
    stacked = jnp.stack(rotation).reshape(2, 3, 3, planes, cells)
    first_fields = filtered.reshape(8, 1, cells)
    upper_set = passed_along(first_fields, "gx", -1)
    upper = jnp.stack(cayley(rebuild(step_size * upper_set)))
    ahead_x = jnp.concatenate([stacked[:, :, :, 1:, :], upper], axis=3).reshape(
        2, 3, 3, planes, side, side
    )
    aheads = [(ahead_x[0], ahead_x[1])]
    for d in (1, 2):
        aheads.append(
            (jnp.roll(rotation[0], -1, axis=2 + d), jnp.roll(rotation[1], -1, axis=2 + d))
        )
    updated = []
    for d in range(3):
        moved = complex_mul(complex_mul(rotation, (cube[d, 0], cube[d, 1])), dagger(aheads[d]))
        updated.append(jnp.stack(moved))
    state = jnp.stack(updated).reshape(3, 2, 3, 3, planes, cells)
    drift = lax.psum(jnp.stack(values), "gx")
    return (state, drift)


def solution(mesh):
    in_specs = (P(None, None, None, None, ("ta", "gx"), None),)
    out_specs = (P(None, None, None, None, ("ta", "gx"), None), P("ta"))
    return jax.shard_map(local, mesh=mesh, in_specs=in_specs, out_specs=out_specs, check_vma=False)
```

profile of v0, /device:TPU:0, one launch (start us, length us, event | category | flops | bytes accessed | tf_op | source)
XLA Modules:
  0.0 409.5 jit_solution(10816750593789599451)
XLA Ops:
  3.5 7.0 %subtract_reduce_fusion = (f32[2,3,3,9216]{3,2,1,0:T(4,128)}, f32[2,3,3,9216]{3,2,1,0:T(4,128)}, f32[2,3,3,9216]{3,2,1,0:T(4,128)S(1)}) fusion(f32[3,2,3,3,1,9216]{5,4,3,2,1,0:T(1,128)S(1)} %copy-done), kind=kLoop, calls=%fused_computation.32 | loop fusion | flops 165888 | bytes 3981312 | tf_op jit(solution)/shard_map/sub | solution.py:201
  10.6 2.5 reshape.41993
  14.5 2.2 reshape.41996
  16.7 2.3 fusion.14
  24.6 2.6 maximum_reduce_fusion
  39.7 3.3 copy.989
  43.5 43.2 %reduce.166 = f32[9216,8]{1,0:T(8,128)} reduce(f32[9216,1,8]{2,1,0:T(1,128)} %bitcast.2640, f32[]{:T(128)} %broadcast.479), dimensions={1}, to_apply=%bitcast.2325.reduce_sub_computation | reduce | bytes 589828
  86.7 4.8 %reshape.42193 = f32[16,1,4608]{2,1,0:T(1,128)} reshape(f32[9216,8]{1,0:T(8,128)} %reduce.166) | data formatting | bytes 589824
  91.5 7.4 %all-to-all-start.1 = ((f32[16,1,4608]{2,1,0:T(1,128)}), f32[16,1,4608]{2,1,0:T(1,128)S(1)}, u32[]{:S(2)}, u32[]{:S(2)}) async-start(f32[16,1,4608]{2,1,0:T(1,128)} %reshape.42193), calls=%async_computation.1 | async-start | bytes 589824 | tf_op jit(solution)/shard_map/all_to_all | solution.py:166
  100.6 3.3 copy.987
  103.9 43.0 %reduce.164 = f32[9216,8]{1,0:T(8,128)} reduce(f32[9216,1,8]{2,1,0:T(1,128)} %bitcast.2641, f32[]{:T(128)} %broadcast.479), dimensions={1}, to_apply=%bitcast.2323.reduce_sub_computation | reduce | bytes 589828
  146.9 4.8 %reshape.42191 = f32[16,1,4608]{2,1,0:T(1,128)} reshape(f32[9216,8]{1,0:T(8,128)} %reduce.164) | data formatting | bytes 589824
  151.7 6.4 %all-to-all-start = ((f32[16,1,4608]{2,1,0:T(1,128)}), f32[16,1,4608]{2,1,0:T(1,128)S(1)}, u32[]{:S(2)}, u32[]{:S(2)}) async-start(f32[16,1,4608]{2,1,0:T(1,128)} %reshape.42191), calls=%async_computation | async-start | bytes 589824 | tf_op jit(solution)/shard_map/all_to_all | solution.py:165
  159.5 9.5 %reshape.42194 = f32[9216,1,8]{2,1,0:T(1,128)} reshape(f32[16,4608]{1,0:T(8,128)S(1)} %reduce.167) | data formatting | bytes 589824
  169.0 3.1 copy.990
  174.0 9.5 %reshape.42192 = f32[9216,1,8]{2,1,0:T(1,128)} reshape(f32[16,4608]{1,0:T(8,128)S(1)} %reduce.165) | data formatting | bytes 589824
  183.5 3.1 copy.988
  189.8 6.6 %all-to-all-start.3 = ((f32[8,16,576]{2,0,1:T(8,128)}), f32[8,16,576]{2,0,1:T(8,128)}, u32[]{:S(2)}, u32[]{:S(2)}) async-start(f32[8,16,576]{2,0,1:T(8,128)} %copy.802), calls=%async_computation.3 | async-start | bytes 655360 | tf_op jit(solution)/shard_map/all_to_all | solution.py:181
  196.4 7.3 %reduce.4 = f32[3,2,3,3,9216]{4,3,2,1,0:T(4,128)} reduce(f32[3,2,3,3,1,9216]{5,4,3,2,1,0:T(1,128)S(1)} %copy-done, f32[]{:T(128)} %constant.91), dimensions={4}, to_apply=%param.1.reduce_sub_computation | reduce | bytes 3981316 | tf_op args[0]
  203.8 3.4 reshape.41987
  208.9 6.1 %all-to-all-start.2 = ((f32[8,16,576]{2,0,1:T(8,128)}), f32[8,16,576]{2,0,1:T(8,128)}, u32[]{:S(2)}, u32[]{:S(2)}) async-start(f32[8,16,576]{2,0,1:T(8,128)} %copy.799), calls=%async_computation.2 | async-start | bytes 655360 | tf_op jit(solution)/shard_map/all_to_all | solution.py:180
  217.1 34.9 %psum.7 = f32[1]{0:T(128)} all-reduce(f32[1]{0:T(128)} %bitcast.467), channel_id=1, replica_groups=mesh['ta'=2,'gx'=16] {'gx'}, use_global_device_ids=true, to_apply=%region_1.2 | all-reduce | flops 1 | bytes 8 | tf_op jit(solution)/shard_map/psum | solution.py:229
  345.3 3.0 maximum_add_fusion.10
  405.8 3.1 maximum_maximum_fusion
  (730 shorter events, 181.6 us)
Async XLA Ops:
  3.0 16.2 %collective-permute-start = (f32[8,1,9216]{2,1,0:T(1,128)S(1)}, f32[8,1,9216]{2,1,0:T(1,128)S(1)}, u32[]{:S(2)}, u32[]{:S(2)}) collective-permute-start(f32[8,1,9216]{2,1,0:T(1,128)S(1)} %fusion.126), channel_id=1, source_target_pairs={{15,0},{0,1},{1,2},{2,3},{3,4},{4,5},{5,6},{6,7},{7,8},{8,9},{9,10... | collective-permute-start | bytes 884744 | tf_op jit(solution)/shard_map/ppermute | solution.py:18
  91.5 60.2 %all-to-all-start.1 = ((f32[16,1,4608]{2,1,0:T(1,128)}), f32[16,1,4608]{2,1,0:T(1,128)S(1)}, u32[]{:S(2)}, u32[]{:S(2)}) async-start(f32[16,1,4608]{2,1,0:T(1,128)} %reshape.42193), calls=%async_computation.1 | async-start | bytes 589824 | tf_op jit(solution)/shard_map/all_to_all | solution.py:166
  151.7 20.9 %all-to-all-start = ((f32[16,1,4608]{2,1,0:T(1,128)}), f32[16,1,4608]{2,1,0:T(1,128)S(1)}, u32[]{:S(2)}, u32[]{:S(2)}) async-start(f32[16,1,4608]{2,1,0:T(1,128)} %reshape.42191), calls=%async_computation | async-start | bytes 589824 | tf_op jit(solution)/shard_map/all_to_all | solution.py:165
  189.8 19.1 %all-to-all-start.3 = ((f32[8,16,576]{2,0,1:T(8,128)}), f32[8,16,576]{2,0,1:T(8,128)}, u32[]{:S(2)}, u32[]{:S(2)}) async-start(f32[8,16,576]{2,0,1:T(8,128)} %copy.802), calls=%async_computation.3 | async-start | bytes 655360 | tf_op jit(solution)/shard_map/all_to_all | solution.py:181
  208.9 45.3 %all-to-all-start.2 = ((f32[8,16,576]{2,0,1:T(8,128)}), f32[8,16,576]{2,0,1:T(8,128)}, u32[]{:S(2)}, u32[]{:S(2)}) async-start(f32[8,16,576]{2,0,1:T(8,128)} %copy.799), calls=%async_computation.2 | async-start | bytes 655360 | tf_op jit(solution)/shard_map/all_to_all | solution.py:180
  289.0 26.0 %copy-start.62 = (f32[1,1,1,96,96]{4,3,0,2,1:T(8,128)S(1)}, f32[1,1,1,96,96]{4,3,0,2,1:T(8,128)}, u32[]{:S(2)}) copy-start(f32[1,1,1,96,96]{4,3,0,2,1:T(8,128)} %get-tuple-element.277) | copy-start | bytes 110596
  289.1 26.7 %copy-start.61 = (f32[1,1,1,96,96]{4,3,0,2,1:T(8,128)S(1)}, f32[1,1,1,96,96]{4,3,0,2,1:T(8,128)}, u32[]{:S(2)}) copy-start(f32[1,1,1,96,96]{4,3,0,2,1:T(8,128)} %get-tuple-element.281) | copy-start | bytes 110596
  289.1 27.4 %copy-start.60 = (f32[1,1,1,96,96]{4,3,0,2,1:T(8,128)S(1)}, f32[1,1,1,96,96]{4,3,0,2,1:T(8,128)}, u32[]{:S(2)}) copy-start(f32[1,1,1,96,96]{4,3,0,2,1:T(8,128)} %get-tuple-element.282) | copy-start | bytes 110596
  289.1 28.1 %copy-start.59 = (f32[1,1,1,96,96]{4,3,0,2,1:T(8,128)S(1)}, f32[1,1,1,96,96]{4,3,0,2,1:T(8,128)}, u32[]{:S(2)}) copy-start(f32[1,1,1,96,96]{4,3,0,2,1:T(8,128)} %get-tuple-element.283) | copy-start | bytes 110596
  290.3 27.7 %copy-start.58 = (f32[1,1,1,96,96]{4,3,0,2,1:T(8,128)S(1)}, f32[1,1,1,96,96]{4,3,0,2,1:T(8,128)}, u32[]{:S(2)}) copy-start(f32[1,1,1,96,96]{4,3,0,2,1:T(8,128)} %get-tuple-element.278) | copy-start | bytes 110596
  290.3 28.4 %copy-start.57 = (f32[1,1,1,96,96]{4,3,0,2,1:T(8,128)S(1)}, f32[1,1,1,96,96]{4,3,0,2,1:T(8,128)}, u32[]{:S(2)}) copy-start(f32[1,1,1,96,96]{4,3,0,2,1:T(8,128)} %get-tuple-element.280) | copy-start | bytes 110596
  290.3 29.1 %copy-start.56 = (f32[1,1,1,96,96]{4,3,0,2,1:T(8,128)S(1)}, f32[1,1,1,96,96]{4,3,0,2,1:T(8,128)}, u32[]{:S(2)}) copy-start(f32[1,1,1,96,96]{4,3,0,2,1:T(8,128)} %get-tuple-element.279) | copy-start | bytes 110596
  290.3 58.2 %collective-permute-start.1 = (f32[8,1,9216]{2,1,0:T(1,128)}, f32[8,1,9216]{2,1,0:T(1,128)}, u32[]{:S(2)}, u32[]{:S(2)}) collective-permute-start(f32[8,1,9216]{2,1,0:T(1,128)} %reshape.41994), channel_id=1, source_target_pairs={{1,0},{2,1},{3,2},{4,3},{5,4},{6,5},{7,6},{8,7},{9,8},{10,9},{11,1... | collective-permute-start | bytes 884744 | tf_op jit(solution)/shard_map/ppermute | solution.py:18
  301.8 34.5 %copy-start.67 = (f32[1,1,1,96,96]{4,3,0,2,1:T(8,128)S(1)}, f32[1,1,1,96,96]{4,3,0,2,1:T(8,128)}, u32[]{:S(2)}) copy-start(f32[1,1,1,96,96]{4,3,0,2,1:T(8,128)} %get-tuple-element.328) | copy-start | bytes 110596
  302.6 34.5 %copy-start.66 = (f32[1,1,1,96,96]{4,3,0,2,1:T(8,128)S(1)}, f32[1,1,1,96,96]{4,3,0,2,1:T(8,128)}, u32[]{:S(2)}) copy-start(f32[1,1,1,96,96]{4,3,0,2,1:T(8,128)} %get-tuple-element.323) | copy-start | bytes 110596
  302.6 31.5 %copy-start.68 = (f32[1,1,1,96,96]{4,3,0,2,1:T(8,128)S(1)}, f32[1,1,1,96,96]{4,3,0,2,1:T(8,128)}, u32[]{:S(2)}) copy-start(f32[1,1,1,96,96]{4,3,0,2,1:T(8,128)} %get-tuple-element.301) | copy-start | bytes 110596
  303.3 34.5 %copy-start.65 = (f32[1,1,1,96,96]{4,3,0,2,1:T(8,128)S(1)}, f32[1,1,1,96,96]{4,3,0,2,1:T(8,128)}, u32[]{:S(2)}) copy-start(f32[1,1,1,96,96]{4,3,0,2,1:T(8,128)} %get-tuple-element.325) | copy-start | bytes 110596
  303.3 27.1 %copy-start.75 = (f32[1,1,1,96,96]{4,3,0,2,1:T(8,128)S(1)}, f32[1,1,1,96,96]{4,3,0,2,1:T(8,128)}, u32[]{:S(2)}) copy-start(f32[1,1,1,96,96]{4,3,0,2,1:T(8,128)} %get-tuple-element.296) | copy-start | bytes 110596
  303.3 29.3 %copy-start.72 = (f32[1,1,1,96,96]{4,3,0,2,1:T(8,128)S(1)}, f32[1,1,1,96,96]{4,3,0,2,1:T(8,128)}, u32[]{:S(2)}) copy-start(f32[1,1,1,96,96]{4,3,0,2,1:T(8,128)} %get-tuple-element.299) | copy-start | bytes 110596
  303.3 32.2 %copy-start.69 = (f32[1,1,1,96,96]{4,3,0,2,1:T(8,128)S(1)}, f32[1,1,1,96,96]{4,3,0,2,1:T(8,128)}, u32[]{:S(2)}) copy-start(f32[1,1,1,96,96]{4,3,0,2,1:T(8,128)} %get-tuple-element.327) | copy-start | bytes 110596
  304.1 27.8 %copy-start.73 = (f32[1,1,1,96,96]{4,3,0,2,1:T(8,128)S(1)}, f32[1,1,1,96,96]{4,3,0,2,1:T(8,128)}, u32[]{:S(2)}) copy-start(f32[1,1,1,96,96]{4,3,0,2,1:T(8,128)} %get-tuple-element.298) | copy-start | bytes 110596
  304.1 29.3 %copy-start.70 = (f32[1,1,1,96,96]{4,3,0,2,1:T(8,128)S(1)}, f32[1,1,1,96,96]{4,3,0,2,1:T(8,128)}, u32[]{:S(2)}) copy-start(f32[1,1,1,96,96]{4,3,0,2,1:T(8,128)} %get-tuple-element.300) | copy-start | bytes 110596
  304.8 26.3 %copy-start.74 = (f32[1,1,1,96,96]{4,3,0,2,1:T(8,128)S(1)}, f32[1,1,1,96,96]{4,3,0,2,1:T(8,128)}, u32[]{:S(2)}) copy-start(f32[1,1,1,96,96]{4,3,0,2,1:T(8,128)} %get-tuple-element.297) | copy-start | bytes 110596
  304.8 30.0 %copy-start.71 = (f32[1,1,1,96,96]{4,3,0,2,1:T(8,128)S(1)}, f32[1,1,1,96,96]{4,3,0,2,1:T(8,128)}, u32[]{:S(2)}) copy-start(f32[1,1,1,96,96]{4,3,0,2,1:T(8,128)} %get-tuple-element.326) | copy-start | bytes 110596
  (128 other events, 1097.4 us)
where the time goes:
time: 417 us; the launch traced here: 409 us
  other arithmetic  175 us (42%)
  local copies, waits for them, and re-layouts  152 us (36%)
  blocking collectives  34.9 us (8%)
  starting transfers between devices  27.1 us (6%)
  matrix products  14.9 us (4%)
  between operations  5.24 us (1%)
    unnamed x3, other arithmetic  93.5 us
    add x144, local copies, waits for them, and re-layouts, matrix_mul(): left[i, 0] * right[0, j] + left[i, 1] * right[1, j]  81.7 us
    add x98, other arithmetic, matrix_mul(): left[i, 0] * right[0, j] + left[i, 1] * right[1, j]  38.3 us
    psum x1, blocking collectives, local(): drift = lax.psum(jnp.stack(values), 'gx')  34.9 us
    unnamed x311, local copies, waits for them, and re-layouts  31.4 us
    dot_general x20, matrix products, transform(): return jnp.einsum(form, matrix, array, precision=lax.Precision.HIGHEST)  14.9 us
  transfers between devices with their start and end apart: 6, of which 0 were waited for; matrix products, arithmetic and copies ran while one was open for 38% of the time, Pallas kernels for 0%

commit v1 on v0

v1 whole, which is shorter than its diff:
```python
import functools
import math

import jax
import jax.numpy as jnp
import numpy as np
from jax import lax
from jax.experimental import pallas as pl
from jax.experimental.pallas import tpu as pltpu
from jax.sharding import PartitionSpec as P

SIDE = 96
LANES = 128

step_size = 0.08
peak_square = 12.0
gain = 0.5 * step_size * peak_square

params = functools.partial(pltpu.CompilerParams, vmem_limit_bytes=48 * 1024 * 1024)


class Plan:
    def __init__(self, count_x, side):
        self.count_x, self.side = count_x, side
        self.cells = side * side
        self.rows = self.cells // LANES
        self.period = side * LANES // math.gcd(side, LANES)
        self.wide = self.period // LANES
        self.folds = self.period // side
        self.groups = self.cells // self.period
        self.pairs = count_x // 2
        self.share = side // self.pairs
        self.full = self.share // 8 * 8
        self.rest = self.share - self.full
        self.tiles = 4 * side // LANES
        self.block = self.tiles * self.share
        self.sent = -(-3 * self.block // 8) * 8
        self.returned = -(-2 * self.block // 8) * 8 + 8


def fourier(length):
    site = np.arange(length)
    basis = np.zeros((length, length))
    for k in range(length):
        angle = 2.0 * math.pi * (k * site % length) / length
        if k == 0 or 2 * k == length:
            basis[k] = np.cos(angle) / math.sqrt(length)
        elif 2 * k < length:
            basis[k] = np.cos(angle) * math.sqrt(2.0 / length)
        else:
            basis[k] = np.sin(angle) * math.sqrt(2.0 / length)
    return basis


def eigen(length):
    return 4.0 * np.sin(math.pi * np.arange(length) / length) ** 2


def split_table(table):
    high = table.astype(jnp.bfloat16)
    low = (table - high.astype(np.float64)).astype(jnp.bfloat16)
    return np.stack([high, low])


def tables(plan):
    side, folds, groups = plan.side, plan.folds, plan.groups
    basis = fourier(side)
    last = np.zeros((folds, side, folds, LANES))
    for j in range(folds):
        last[j, :, j, :side] = basis.T
    last = last.reshape(folds * side, folds * LANES)
    order = [plan.share * j + i for j in range(plan.pairs) for i in range(plan.full)]
    order += [plan.share * j + plan.full + i for j in range(plan.pairs) for i in range(plan.rest)]
    columns = [folds * g + j for j in range(folds) for g in range(groups)]
    second = basis[order][:, columns]
    value = eigen(side)
    inverse_side = np.zeros((side, LANES))
    inverse_side[:, :side] = 1.0 / (2.0 + value[order][:, None] + value[None, :])
    lane = np.arange(plan.tiles * LANES).reshape(plan.tiles, 1, LANES)
    owner = np.zeros((plan.pairs, plan.block, LANES))
    for j in range(plan.pairs):
        parts = []
        for start, size in ((0, plan.full), (plan.full, plan.rest)):
            mode = plan.share * j + start + np.arange(size).reshape(1, size, 1)
            parts.append((value[mode] + value[lane % side]).reshape(plan.tiles * size, LANES))
        owner[j] = np.concatenate(parts)
    weights = np.zeros((2, plan.block, LANES))
    for quad, values in enumerate(((1.5, 0.5, 2.0, 2.0), (2.0, 2.0, 2.0, 2.0))):
        of_lane = np.array(values)[lane // side]
        parts = [
            np.broadcast_to(of_lane, (plan.tiles, size, LANES)).reshape(plan.tiles * size, LANES)
            for size in (plan.full, plan.rest)
        ]
        weights[quad] = np.concatenate(parts)
    return {
        "last": split_table(last),
        "last_back": split_table(last.T),
        "second": split_table(second),
        "second_back": split_table(second.T),
        "inverse_side": inverse_side.astype(np.float32),
        "owner": owner.astype(np.float32),
        "weights": weights.astype(np.float32),
    }


def halve(value):
    high = value.astype(jnp.bfloat16)
    low = (value - high.astype(jnp.float32)).astype(jnp.bfloat16)
    return high, low


def product(left, right):
    dot = functools.partial(jnp.dot, preferred_element_type=jnp.float32)
    return dot(left[0], right[0]) + (dot(left[0], right[1]) + dot(left[1], right[0]))


def lane_of(shape):
    return lax.broadcasted_iota(jnp.int32, shape, 1)


def moved(ref, field, start, size, distance):
    down, over = distance // LANES, distance % LANES
    here = ref[field, pl.ds(start + down, size), :]
    after = ref[field, pl.ds(start + down + 1, size), :]
    mixed = jnp.where(lane_of(here.shape) >= over, here, after)
    return pltpu.roll(mixed, LANES - over, 1)


def last_index(rows, side):
    row = lax.broadcasted_iota(jnp.int32, (rows, LANES), 0)
    return (row * LANES + lane_of((rows, LANES))) % side


def wrap(ref, field, rows):
    ref[field, pl.ds(0, 8), :] = ref[field, pl.ds(rows, 8), :]
    ref[field, pl.ds(8 + rows, 8), :] = ref[field, pl.ds(8, 8), :]


def projected(links, d):
    def entry(part, i, j):
        return links[((d * 2 + part) * 3 + i) * 3 + j]

    im00, im11, im22 = entry(1, 0, 0), entry(1, 1, 1), entry(1, 2, 2)
    fields = [(im00 + im11 - 2.0 * im22) * (1.0 / 3.0), im00 - im11]
    for i, j in ((0, 1), (0, 2), (1, 2)):
        fields.append(0.5 * (entry(0, i, j) - entry(0, j, i)))
        fields.append(0.5 * (entry(1, i, j) + entry(1, j, i)))
    return fields


def divergence_kernel(plan, steps, index_ref, links_ref, keep_ref, send_ref, first, second, third):
    rows, side = plan.rows, plan.side
    size = rows // steps
    step = pl.program_id(0)
    start = pl.multiple_of(step * size, 8)
    for d, target, lead in ((0, first, 0), (1, second, 8), (2, third, 8)):
        for f, value in enumerate(projected(links_ref, d)):
            target[f, pl.ds(start + lead, size), :] = value

    @pl.when(step == steps - 1)
    def _():
        odd = index_ref[0] % 2
        at_start = last_index(rows, side) == 0
        diverge, direct = [], []
        for f in range(8):
            wrap(second, f, rows)
            wrap(third, f, rows)
            behind = moved(second, f, 8, rows, -side)
            beside = jnp.where(
                at_start, moved(third, f, 8, rows, side - 1), moved(third, f, 8, rows, -1)
            )
            here = first[f]
            total = (behind - second[f, pl.ds(8, rows), :]) + (
                beside - third[f, pl.ds(8, rows), :]
            )
            diverge.append(total - here)
            direct.append(here)
        for f in range(4):
            for part, values in enumerate((diverge, direct)):
                place = pl.ds((part * 4 + f) * rows, rows)
                keep_ref[place, :] = jnp.where(odd == 0, values[f], values[4 + f])
                send_ref[place, :] = jnp.where(odd == 0, values[4 + f], values[f])


def forward_kernel(
    plan, index_ref, keep_ref, got_ref, last_ref, second_ref, inverse_ref, sent_ref, odd_ref, dense
):
    rows, groups, folds, side = plan.rows, plan.groups, plan.folds, plan.side
    odd = index_ref[0] % 2
    quad = 4 * rows
    for f in range(4):
        own_d, own_a = keep_ref[pl.ds(f * rows, rows), :], keep_ref[pl.ds(quad + f * rows, rows), :]
        got_d, got_a = got_ref[pl.ds(f * rows, rows), :], got_ref[pl.ds(quad + f * rows, rows), :]
        even_d, odd_d = jnp.where(odd == 0, own_d, got_d), jnp.where(odd == 0, got_d, own_d)
        even_a, odd_a = jnp.where(odd == 0, own_a, got_a), jnp.where(odd == 0, got_a, own_a)
        for q, value in enumerate((even_d, odd_d + even_a, odd_a)):
            dense[pl.ds((q * 4 + f) * rows, rows), :] = value
    count = 12 * groups
    wide = jnp.concatenate(
        [dense[pl.ds(s, count, stride=plan.wide), :] for s in range(plan.wide)], axis=1
    )
    waves = product(halve(wide), (last_ref[0], last_ref[1]))
    columns = []
    for pf in range(12):
        part = waves[pf * groups : (pf + 1) * groups]
        columns.append(
            jnp.concatenate([part[:, j * LANES : (j + 1) * LANES] for j in range(folds)], axis=0)
        )
    modes = product((second_ref[0], second_ref[1]), halve(jnp.concatenate(columns, axis=1)))
    inverse = inverse_ref[...]
    full, rest, pairs, tiles = plan.full, plan.rest, plan.pairs, plan.tiles
    lane = lane_of((side, LANES))
    for q in range(3):
        fields = [modes[:, (q * 4 + f) * LANES : (q * 4 + f + 1) * LANES] for f in range(4)]
        if q == 1:
            for f in range(4):
                odd_ref[:, f * LANES : (f + 1) * LANES] = fields[f] * (gain * inverse)
        for t, value in enumerate(pack(fields, lane, side)):
            at = q * tiles + t
            for j in range(pairs):
                if full:
                    sent_ref[j, pl.ds(at * full, full), :] = value[j * full : (j + 1) * full]
                if rest:
                    begin = pairs * full + j * rest
                    sent_ref[j, pl.ds(3 * tiles * full + at * rest, rest), :] = value[
                        begin : begin + rest
                    ]
    spare = plan.sent - 3 * plan.block
    if spare:
        sent_ref[:, pl.ds(3 * plan.block, spare), :] = jnp.zeros((pairs, spare, LANES), jnp.float32)


def pack(fields, lane, side):
    rolled = [
        value if f * side % LANES == 0 else pltpu.roll(value, f * side % LANES, 1)
        for f, value in enumerate(fields)
    ]
    packed = []
    for t in range(4 * side // LANES):
        value = None
        for f in range(4):
            if f * side < (t + 1) * LANES and (f + 1) * side > t * LANES:
                value = rolled[f] if value is None else jnp.where(lane >= f * side - t * LANES, rolled[f], value)
        packed.append(value)
    return packed


def unpack(packed, lane, side):
    fields = []
    for f in range(4):
        begin = f * side // LANES
        end = ((f + 1) * side - 1) // LANES
        offset = f * side % LANES
        value = packed[begin]
        if end != begin:
            value = jnp.where(lane >= offset, packed[begin], packed[end])
        if offset:
            value = pltpu.roll(value, LANES - offset, 1)
        fields.append(jnp.where(lane < side, value, 0.0))
    return fields


def filter_kernel(plan, index_ref, got_ref, owner_ref, weight_ref, back_ref):
    pairs, tiles, count_x = plan.pairs, plan.tiles, plan.count_x
    half = pairs // 2
    drift = 0.0
    for part, (size, first, second) in enumerate(
        ((plan.full, 0, 0), (plan.rest, 3 * tiles * plan.full, 2 * tiles * plan.full))
    ):
        if not size:
            continue
        length = tiles * size
        own = pl.ds(0 if part == 0 else tiles * plan.full, length)
        value = owner_ref[0, own, :]
        weight = weight_ref[0, own, :]

        def plane(p, q):
            return got_ref[p, pl.ds(first + q * length, length), :]

        inverse = 1.0 / (2.0 + value)
        odds = [plane(p, 1) for p in range(pairs)]
        evens = [plane(p, 0) + plane((p - 1) % pairs, 2) for p in range(pairs)]
        square = jnp.zeros_like(value)
        for p in range(pairs):
            square = square + (odds[p] * odds[p] + evens[p] * evens[p])
        drift = drift + jnp.sum(square * weight)
        rhs = [evens[p] + (odds[p] + odds[(p - 1) % pairs]) * inverse for p in range(pairs)]
        plus = [rhs[d] + rhs[pairs - d] for d in range(1, half)]
        minus = [rhs[d] - rhs[pairs - d] for d in range(1, half)]
        cosines, sines = [], []
        for k in range(half + 1):
            total = rhs[0] + rhs[half] if k % 2 == 0 else rhs[0] - rhs[half]
            for d in range(1, half):
                total = total + plus[d - 1] * math.cos(2 * math.pi * (k * d % pairs) / pairs)
            root = 4.0 * math.sin(math.pi * k / count_x) ** 2
            below = (value + root) * (value + (4.0 - root))
            scale = gain / pairs * (1.0 if k in (0, half) else 2.0)
            if k == 0:
                factor = jnp.where(value > 0, scale * (2.0 + value) / jnp.where(value > 0, below, 1.0), 0.0)
                whole = odds[0]
                for p in range(1, pairs):
                    whole = whole + odds[p]
                mean = jnp.where(value > 0, 0.0, whole * (-0.25 * gain / pairs))
                cosines.append(total * factor + mean)
            else:
                factor = scale * (2.0 + value) / below
                cosines.append(total * factor)
                if k < half:
                    wave = jnp.zeros_like(value)
                    for d in range(1, half):
                        wave = wave + minus[d - 1] * math.sin(2 * math.pi * (k * d % pairs) / pairs)
                    sines.append(wave * factor)
        results = [None] * pairs
        for d in range(half + 1):
            even = cosines[0]
            for k in range(1, half + 1):
                even = even + cosines[k] * math.cos(2 * math.pi * (k * d % pairs) / pairs)
            if d in (0, half):
                results[d] = even
            else:
                wave = jnp.zeros_like(value)
                for k in range(1, half):
                    wave = wave + sines[k - 1] * math.sin(2 * math.pi * (k * d % pairs) / pairs)
                results[d] = even + wave
                results[pairs - d] = even - wave
        for p in range(pairs):
            back_ref[p, pl.ds(second, length), :] = results[p]
            back_ref[p, pl.ds(second + length, length), :] = results[(p + 1) % pairs]
    spare = plan.returned - 2 * plan.block
    for p in range(pairs):
        back_ref[p, pl.ds(2 * plan.block, spare), :] = jnp.full((spare, LANES), drift, jnp.float32)


def backward_kernel(
    plan, index_ref, got_ref, odd_ref, last_ref, second_ref, inverse_ref, keep_ref, send_ref, packed, dense
):
    rows, groups, folds, side = plan.rows, plan.groups, plan.folds, plan.side
    full, rest, pairs, tiles = plan.full, plan.rest, plan.pairs, plan.tiles
    odd = index_ref[0] % 2
    for q in range(2):
        for t in range(tiles):
            at = q * tiles + t
            for j in range(pairs):
                if full:
                    packed[at, pl.ds(j * full, full), :] = got_ref[j, pl.ds(at * full, full), :]
                if rest:
                    packed[at, pl.ds(pairs * full + j * rest, rest), :] = got_ref[
                        j, pl.ds(2 * tiles * full + at * rest, rest), :
                    ]
    lane = lane_of((side, LANES))
    inverse = inverse_ref[...]
    even, after = [
        unpack([packed[q * tiles + t] for t in range(tiles)], lane, side) for q in range(2)
    ]
    between = [
        odd_ref[:, f * LANES : (f + 1) * LANES] + (even[f] + after[f]) * inverse for f in range(4)
    ]
    waves = product(
        (second_ref[0], second_ref[1]), halve(jnp.concatenate(even + between + after, axis=1))
    )
    blocks = []
    for pf in range(12):
        part = waves[:, pf * LANES : (pf + 1) * LANES]
        blocks.append(
            jnp.concatenate([part[j * groups : (j + 1) * groups] for j in range(folds)], axis=1)
        )
    wide = product(halve(jnp.concatenate(blocks, axis=0)), (last_ref[0], last_ref[1]))
    count = 12 * groups
    for s in range(plan.wide):
        dense[pl.ds(s, count, stride=plan.wide), :] = wide[:, s * LANES : (s + 1) * LANES]
    quad = 4 * rows
    low, middle, high = [dense[pl.ds(q * quad, quad), :] for q in range(3)]
    keep_ref[pl.ds(0, quad), :] = jnp.where(odd == 0, low, middle)
    keep_ref[pl.ds(quad, quad), :] = jnp.where(odd == 0, middle, high)
    send_ref[pl.ds(0, quad), :] = jnp.where(odd == 0, middle, low)
    send_ref[pl.ds(quad, quad), :] = jnp.where(odd == 0, high, middle)
    drift = got_ref[0, pl.ds(2 * plan.block, 8), :]
    for j in range(1, pairs):
        drift = drift + got_ref[j, pl.ds(2 * plan.block, 8), :]
    keep_ref[pl.ds(2 * quad, 8), :] = drift
    send_ref[pl.ds(2 * quad, 8), :] = drift


def times(left, right):
    return (left[0] * right[0] - left[1] * right[1], left[0] * right[1] + left[1] * right[0])


def times_conj(left, right):
    return (left[0] * right[0] + left[1] * right[1], left[1] * right[0] - left[0] * right[1])


def rotation(fields):
    both, apart = fields[0], fields[1]
    a, b, e = 0.5 * (both + apart), 0.5 * (both - apart), -both
    u, v, w = (fields[2], fields[3]), (fields[4], fields[5]), (fields[6], fields[7])
    square = [x[0] * x[0] + x[1] * x[1] for x in (u, v, w)]
    a00, a11, a22 = square[2] - b * e, square[1] - a * e, square[0] - a * b
    vw, uw, vu = times_conj(v, w), times(u, w), times_conj(v, u)
    a01 = (e * u[1] - vw[0], -(e * u[0]) - vw[1])
    a02 = (uw[0] + b * v[1], uw[1] - b * v[0])
    a12 = (a * w[1] - vu[0], -(a * w[0]) - vu[1])
    turn = a * a00 + times_conj(u, a01)[1] + times_conj(v, a02)[1]
    real = 1.0 + (a00 + a11 + a22)
    scale = 2.0 / (real * real + turn * turn)
    factor = (real * scale, turn * scale)
    entries = [[None] * 3 for _ in range(3)]
    for i, (up, imag) in enumerate(((a00, a), (a11, b), (a22, e))):
        value = times((1.0 + up, imag), factor)
        entries[i][i] = (value[0] - 1.0, value[1])
    for (i, j), up, off in (((0, 1), a01, u), ((0, 2), a02, v), ((1, 2), a12, w)):
        entries[i][j] = times((up[0] + off[0], up[1] + off[1]), factor)
        entries[j][i] = times((up[0] - off[0], off[1] - up[1]), factor)
    return [entries[i][j][part] for part in range(2) for i in range(3) for j in range(3)]


def update_kernel(
    plan, steps, index_ref, keep_ref, got_ref, links_ref, fixed_ref, drift_ref, here, along_x, along_y, along_z
):
    rows, side = plan.rows, plan.side
    quad = 4 * rows
    size = rows // steps
    step = pl.program_id(0)

    @pl.when(step == 0)
    def _():
        odd = index_ref[0] % 2

        def turn(i, _):
            begin = pl.multiple_of(i * 8, 8)
            for q, target, lead in ((0, here, 8), (1, along_x, 0)):
                fields = [None] * 8
                for f in range(4):
                    place = pl.ds(pl.multiple_of(q * quad + f * rows + begin, 8), 8)
                    own, other = keep_ref[place, :], got_ref[place, :]
                    fields[f] = jnp.where(odd == 0, own, other)
                    fields[4 + f] = jnp.where(odd == 0, other, own)
                for n, value in enumerate(rotation(fields)):
                    target[n, pl.ds(begin + lead, 8), :] = value
            return 0

        lax.fori_loop(0, rows // 8, turn, 0)
        at_end = last_index(rows, side) == side - 1
        for n in range(18):
            wrap(here, n, rows)
            along_y[n] = moved(here, n, 8, rows, side)
            along_z[n] = jnp.where(
                at_end, moved(here, n, 8, rows, 1 - side), moved(here, n, 8, rows, 1)
            )
        total = keep_ref[pl.ds(2 * quad, 8), :] + got_ref[pl.ds(2 * quad, 8), :]
        drift_ref[0] = total[0, 0] * (1.0 / (9.0 * plan.count_x * plan.cells))

    def update(i, _):
        begin = pl.multiple_of(i * 8, 8)
        place = pl.multiple_of(step * size + i * 8, 8)

        def matrix(ref, lead):
            value = [ref[n, pl.ds(place + lead, 8), :] for n in range(18)]
            return [[(value[3 * r + c], value[9 + 3 * r + c]) for c in range(3)] for r in range(3)]

        for d, ahead_ref in enumerate((along_x, along_y, along_z)):
            own = matrix(here, 8)
            links = [
                [
                    tuple(links_ref[((d * 2 + part) * 3 + r) * 3 + c, pl.ds(begin, 8), :] for part in range(2))
                    for c in range(3)
                ]
                for r in range(3)
            ]
            ahead = matrix(ahead_ref, 0)
            for r in range(3):
                line = [
                    add(times(own[r][0], links[0][c]), times(own[r][1], links[1][c]), times(own[r][2], links[2][c]))
                    for c in range(3)
                ]
                for c in range(3):
                    value = add(*[times_conj(line[k], ahead[c][k]) for k in range(3)])
                    for part in range(2):
                        fixed_ref[((d * 2 + part) * 3 + r) * 3 + c, pl.ds(begin, 8), :] = value[part]
        return 0

    lax.fori_loop(0, size // 8, update, 0)


def add(first, second, third):
    return (first[0] + second[0] + third[0], first[1] + second[1] + third[1])


def whole_spec():
    return pl.BlockSpec(memory_space=pltpu.VMEM)


def scalar_spec():
    return pl.BlockSpec(memory_space=pltpu.SMEM)


def shape_of(*shape):
    return jax.ShapeDtypeStruct(shape, jnp.float32)


def local(gauge_links):
    count_x = lax.axis_size("gx")
    plan = Plan(count_x, SIDE)
    rows, pairs = plan.rows, plan.pairs
    table = tables(plan)
    index = lax.axis_index("gx").astype(jnp.int32).reshape(1)
    links = gauge_links.reshape(54, rows, LANES)
    steps = 3
    block = pl.BlockSpec((54, rows // steps, LANES), lambda i: (0, i, 0))
    quads = 8 * rows
    swap = [(i, i ^ 1) for i in range(count_x)]
    same_core = [[c + 2 * p for p in range(pairs)] for c in range(2)]

    keep, send = pl.pallas_call(
        functools.partial(divergence_kernel, plan, steps),
        grid=(steps,),
        out_shape=(shape_of(quads, LANES), shape_of(quads, LANES)),
        in_specs=[scalar_spec(), block],
        out_specs=(whole_spec(), whole_spec()),
        scratch_shapes=[
            pltpu.VMEM((8, rows, LANES), jnp.float32),
            pltpu.VMEM((8, rows + 16, LANES), jnp.float32),
            pltpu.VMEM((8, rows + 16, LANES), jnp.float32),
        ],
        compiler_params=params(),
        name="divergence",
    )(index, links)
    got = lax.ppermute(send, "gx", swap)
    sent, odd_part = pl.pallas_call(
        functools.partial(forward_kernel, plan),
        out_shape=(shape_of(pairs, plan.sent, LANES), shape_of(SIDE, 4 * LANES)),
        in_specs=[scalar_spec()] + [whole_spec()] * 5,
        out_specs=(whole_spec(), whole_spec()),
        scratch_shapes=[pltpu.VMEM((12 * rows, LANES), jnp.float32)],
        compiler_params=params(),
        name="forward",
    )(index, keep, got, table["last"], table["second"], table["inverse_side"])
    arrived = lax.all_to_all(
        sent, "gx", split_axis=0, concat_axis=0, tiled=True, axis_index_groups=same_core
    )
    back = pl.pallas_call(
        functools.partial(filter_kernel, plan),
        grid_spec=pltpu.PrefetchScalarGridSpec(
            num_scalar_prefetch=1,
            grid=(1,),
            in_specs=[
                pl.BlockSpec((pairs, plan.sent, LANES), lambda i, at: (0, 0, 0)),
                pl.BlockSpec((1, plan.block, LANES), lambda i, at: (at[0] // 2, 0, 0)),
                pl.BlockSpec((1, plan.block, LANES), lambda i, at: (at[0] % 2, 0, 0)),
            ],
            out_specs=pl.BlockSpec((pairs, plan.returned, LANES), lambda i, at: (0, 0, 0)),
        ),
        out_shape=shape_of(pairs, plan.returned, LANES),
        compiler_params=params(),
        name="filter",
    )(index, arrived, table["owner"], table["weights"])
    returned = lax.all_to_all(
        back, "gx", split_axis=0, concat_axis=0, tiled=True, axis_index_groups=same_core
    )
    keep, send = pl.pallas_call(
        functools.partial(backward_kernel, plan),
        out_shape=(shape_of(quads + 8, LANES), shape_of(quads + 8, LANES)),
        in_specs=[scalar_spec()] + [whole_spec()] * 5,
        out_specs=(whole_spec(), whole_spec()),
        scratch_shapes=[
            pltpu.VMEM((2 * plan.tiles, SIDE, LANES), jnp.float32),
            pltpu.VMEM((12 * rows, LANES), jnp.float32),
        ],
        compiler_params=params(),
        name="backward",
    )(index, returned, odd_part, table["last_back"], table["second_back"], table["inverse_side"])
    got = lax.ppermute(send, "gx", swap)
    fixed, drift = pl.pallas_call(
        functools.partial(update_kernel, plan, steps),
        grid=(steps,),
        out_shape=(shape_of(54, rows, LANES), shape_of(1)),
        in_specs=[scalar_spec(), whole_spec(), whole_spec(), block],
        out_specs=(block, scalar_spec()),
        scratch_shapes=[
            pltpu.VMEM((18, rows + 16, LANES), jnp.float32),
            pltpu.VMEM((18, rows, LANES), jnp.float32),
            pltpu.VMEM((18, rows, LANES), jnp.float32),
            pltpu.VMEM((18, rows, LANES), jnp.float32),
        ],
        compiler_params=params(),
        name="update",
    )(index, keep, got, links)
    return fixed.reshape(gauge_links.shape), drift


def solution(mesh):
    in_specs = (P(None, None, None, None, ("ta", "gx"), None),)
    out_specs = (P(None, None, None, None, ("ta", "gx"), None), P("ta"))
    return jax.shard_map(local, mesh=mesh, in_specs=in_specs, out_specs=out_specs, check_vma=False)
```

time: 417 us -> 47.3 us (0.11); the launches traced: 409 us -> 47.1 us
  other arithmetic: 175 us -> 0 us
  local copies, waits for them, and re-layouts: 152 us -> 1.59 us
  starting transfers between devices: 27.1 us -> 0.59 us
  matrix products: 14.9 us -> 0 us
  Pallas kernels: 0 us -> 6.75 us
  between operations: 5.24 us -> 0.72 us
    unnamed x3 -> x0, other arithmetic: 93.5 us -> none
    add x145 -> x0, local copies, waits for them, and re-layouts: 82.6 us -> none  [the longest x144 81.7 us: matrix_mul(): left[i, 0] * right[0, j] + left[i, 1] * right[1, j]]
    add x113 -> x0, other arithmetic: 45.5 us -> none  [the longest x98 38.3 us: matrix_mul(): left[i, 0] * right[0, j] + left[i, 1] * right[1, j]]
    psum x1 -> x0, blocking collectives: 34.9 us -> none  [local(): drift = lax.psum(jnp.stack(values), 'gx')]
    all_to_all x0 -> x2, blocking collectives: none -> 34.6 us  [the longest x1 20.6 us: local(): lax.all_to_all(sent, 'gx', split_axis=0, concat_axis=0, tiled=True, axis_...]
    unnamed x311 -> x18, local copies, waits for them, and re-layouts: 31.4 us -> 1.59 us
    all_to_all x4 -> x0, starting transfers between devices: 26.5 us -> none  [the longest x1 7.43 us: smooth(): lax.all_to_all(imag_part, 'gx', split_axis=2, concat_axis=1, tiled=True)]
    sub x21 -> x0, other arithmetic: 15.5 us -> none  [the longest x1 7.03 us: local(): diverge = back_x.reshape(2, 3, 3, planes, side, side) - cube[0]]
  transfers between devices with their start and end apart: 6 -> 2, of which waited for: 0 -> 2; matrix products, arithmetic and copies ran while one was open for 38% -> 0% of each run, Pallas kernels for 0% -> 0%
where the time goes in v1:
time: 47.3 us; the launch traced here: 47.1 us
  blocking collectives  34.6 us (73%)
  Pallas kernels  6.75 us (14%)
  waiting for transfers between devices  2.78 us (6%)
  local copies, waits for them, and re-layouts  1.59 us (3%)
  between operations  0.72 us (2%)
  starting transfers between devices  0.59 us (1%)
    all_to_all x1, blocking collectives, local(): lax.all_to_all(sent, 'gx', split_axis=0, concat_axis=0, tiled=True, axis_...  20.6 us
    all_to_all x1, blocking collectives, local(): lax.all_to_all(back, 'gx', split_axis=0, concat_axis=0, tiled=True, axis_...  14 us
    pallas_call x1, Pallas kernels, local(): pl.pallas_call(functools.partial(update_kernel, plan, steps), grid=(steps...  3.85 us
    ppermute x2, waiting for transfers between devices, local(): got = lax.ppermute(send, 'gx', swap)  2.78 us
    unnamed x18, local copies, waits for them, and re-layouts  1.59 us
    pallas_call x1, Pallas kernels, local(): pl.pallas_call(functools.partial(forward_kernel, plan), out_shape=(shape_...  1.07 us
    pallas_call x1, Pallas kernels, local(): pl.pallas_call(functools.partial(backward_kernel, plan), out_shape=(shape...  1.05 us
  transfers between devices with their start and end apart: 2, of which 2 were waited for; matrix products, arithmetic and copies ran while one was open for 0% of the time, Pallas kernels for 0%

profile of v1, /device:TPU:0, one launch (start us, length us, event | category | flops | bytes accessed | tf_op | source)
XLA Modules:
  0.0 47.1 jit_solution(7819292672552562628)
XLA Ops:
  0.6 0.0 copy-start
  0.6 1.5 %copy-done = f32[3,2,3,3,1,9216]{5,4,3,2,1,0:T(1,128)S(1)} copy-done((f32[3,2,3,3,1,9216]{5,4,3,2,1,0:T(1,128)S(1)}, f32[3,2,3,3,1,9216]{5,4,3,2,1,0:T(1,128)}, u32[]{:S(2)}) %copy-start) | copy-done | bytes 1990680
  2.2 0.0 copy-start.8
  2.2 0.6 %divergence.1 = (f32[576,128]{1,0:T(8,128)S(1)}, f32[576,128]{1,0:T(8,128)S(1)}) custom-call(s32[1]{0:T(128)} %bitcast.index_ref, f32[54,72,128]{2,1,0:T(8,128)S(1)} %bitcast.3), custom_call_target="tpu_custom_call" | custom-call | tf_op jit(solution)/shard_map/divergence/pallas_call | solution.py:513
  2.8 0.5 %collective-permute-start = (f32[576,128]{1,0:T(8,128)S(1)}, f32[576,128]{1,0:T(8,128)S(1)}, u32[]{:S(2)}, u32[]{:S(2)}) collective-permute-start(f32[576,128]{1,0:T(8,128)S(1)} %get-tuple-element.11), channel_id=1, source_target_pairs={{0,1},{1,0},{2,3},{3,2},{4,5},{5,4},{6,7},{7,6},{8,9},{9,8},{10,11... | collective-permute-start | bytes 884744 | tf_op jit(solution)/shard_map/ppermute | solution.py:527
  3.3 1.2 %collective-permute-done.got_ref = f32[576,128]{1,0:T(8,128)S(1)} collective-permute-done((f32[576,128]{1,0:T(8,128)S(1)}, f32[576,128]{1,0:T(8,128)S(1)}, u32[]{:S(2)}, u32[]{:S(2)}) %collective-permute-start) | collective-permute-done | bytes 294944 | tf_op jit(solution)/shard_map/ppermute | solution.py:527
  4.6 0.0 copy-done.3
  4.6 0.0 copy-done.4
  4.6 0.0 copy-done.7
  4.6 0.0 copy-start.6
  4.6 1.1 %forward.1 = (f32[8,112,128]{2,1,0:T(8,128)S(1)}, f32[96,512]{1,0:T(8,128)S(1)}) custom-call(s32[1]{0:T(128)} %bitcast.index_ref, f32[576,128]{1,0:T(8,128)S(1)} %get-tuple-element.10.keep_ref, f32[576,128]{1,0:T(8,128)S(1)} %collective-permute-done.got_ref, bf16[2,384,512]{2,1,0:T(8,128)(2,1)S(1)} %copy-done.3, bf16[2,96,96]{2,1,0:T(8,128)(2,1)S(1)} %copy-done.7, ...), custom_call_target="tpu_custom_call" | custom-call | tf_op jit(solution)/shard_map/forward/pallas_call | solution.py:528
  5.7 0.0 copy-start.1
  5.7 20.6 %all_to_all.10.got_ref = f32[8,112,128]{2,1,0:T(8,128)S(1)} all-to-all(f32[8,112,128]{2,1,0:T(8,128)S(1)} %get-tuple-element.12), channel_id=1, replica_groups={{0,2,4,6,8,10,12,14},{1,3,5,7,9,11,13,15},{16,18,20,22,24,26,28,30},{17..., dimensions={0} | all-to-all | bytes 917504 | tf_op jit(solution)/shard_map/all_to_all | solution.py:537
  26.3 0.0 copy-done.5
  26.3 0.0 copy-done.8
  26.3 0.2 filter.1
  26.5 14.0 %all_to_all.11.got_ref = f32[8,80,128]{2,1,0:T(8,128)S(1)} all-to-all(f32[8,80,128]{2,1,0:T(8,128)S(1)} %filter.1), channel_id=1, replica_groups={{0,2,4,6,8,10,12,14},{1,3,5,7,9,11,13,15},{16,18,20,22,24,26,28,30},{17..., dimensions={0} | all-to-all | bytes 655360 | tf_op jit(solution)/shard_map/all_to_all | solution.py:556
  40.5 0.0 copy-done.2
  40.5 0.0 copy-done.6
  40.5 1.1 %backward.1 = (f32[584,128]{1,0:T(8,128)S(1)}, f32[584,128]{1,0:T(8,128)S(1)}) custom-call(s32[1]{0:T(128)} %bitcast.index_ref, f32[8,80,128]{2,1,0:T(8,128)S(1)} %all_to_all.11.got_ref, f32[96,512]{1,0:T(8,128)S(1)} %get-tuple-element.13.odd_ref, bf16[2,512,384]{2,1,0:T(8,128)(2,1)S(1)} %copy-done.2, bf16[2,96,96]{2,1,0:T(8,128)(2,1)S(1)} %copy-done.6, ...), custom_call_target="tpu_custom_call" | custom-call | tf_op jit(solution)/shard_map/backward/pallas_call | solution.py:559
  41.6 0.1 collective-permute-start.1
  41.6 1.6 %collective-permute-done.1.got_ref = f32[584,128]{1,0:T(8,128)S(1)} collective-permute-done((f32[584,128]{1,0:T(8,128)S(1)}, f32[584,128]{1,0:T(8,128)S(1)}, u32[]{:S(2)}, u32[]{:S(2)}) %collective-permute-start.1) | collective-permute-done | bytes 299040 | tf_op jit(solution)/shard_map/ppermute | solution.py:571
  43.2 0.0 copy-done.1
  43.2 3.9 %update.1 = (f32[54,72,128]{2,1,0:T(8,128)}, f32[1]{0:T(128)}) custom-call(s32[1]{0:T(128)} %bitcast.index_ref, f32[584,128]{1,0:T(8,128)S(1)} %get-tuple-element.14.keep_ref, f32[584,128]{1,0:T(8,128)S(1)} %collective-permute-done.1.got_ref, f32[54,72,128]{2,1,0:T(8,128)S(1)} %bitcast.4), custom_call_target="tpu_custom_call" | custom-call | tf_op jit(solution)/shard_map/update/pallas_call | solution.py:572
  (5 shorter events, 0.0 us)
Async XLA Ops:
  0.6 1.6 %copy-start = (f32[3,2,3,3,1,9216]{5,4,3,2,1,0:T(1,128)S(1)}, f32[3,2,3,3,1,9216]{5,4,3,2,1,0:T(1,128)}, u32[]{:S(2)}) copy-start(f32[3,2,3,3,1,9216]{5,4,3,2,1,0:T(1,128)} %param.8) | copy-start | bytes 5971972
  2.2 2.4 %copy-start.3 = (bf16[2,384,512]{2,1,0:T(8,128)(2,1)S(1)}, bf16[2,384,512]{2,1,0:T(8,128)(2,1)}, u32[]{:S(2)}) copy-start(bf16[2,384,512]{2,1,0:T(8,128)(2,1)} %constant.18.clone.last_ref) | copy-start | bytes 2359300
  2.2 2.4 %copy-start.4 = (f32[96,128]{1,0:T(8,128)S(1)}, f32[96,128]{1,0:T(8,128)}, u32[]{:S(2)}) copy-start(f32[96,128]{1,0:T(8,128)} %constant.20.clone.inverse_ref) | copy-start | bytes 147460
  2.2 2.4 %copy-start.7 = (bf16[2,96,96]{2,1,0:T(8,128)(2,1)S(1)}, bf16[2,96,96]{2,1,0:T(8,128)(2,1)}, u32[]{:S(2)}) copy-start(bf16[2,96,96]{2,1,0:T(8,128)(2,1)} %constant.19.clone.second_ref) | copy-start | bytes 110596
  2.2 24.1 %copy-start.5 = (f32[8,36,128]{2,1,0:T(8,128)S(1)}, f32[8,36,128]{2,1,0:T(8,128)}, u32[]{:S(2)}) copy-start(f32[8,36,128]{2,1,0:T(8,128)} %constant.21.clone.owner_ref) | copy-start | bytes 442372
  2.2 24.1 %copy-start.8 = (f32[2,36,128]{2,1,0:T(8,128)S(1)}, f32[2,36,128]{2,1,0:T(8,128)}, u32[]{:S(2)}) copy-start(f32[2,36,128]{2,1,0:T(8,128)} %constant.22.clone.weight_ref) | copy-start | bytes 110596
  2.8 1.7 %collective-permute-start = (f32[576,128]{1,0:T(8,128)S(1)}, f32[576,128]{1,0:T(8,128)S(1)}, u32[]{:S(2)}, u32[]{:S(2)}) collective-permute-start(f32[576,128]{1,0:T(8,128)S(1)} %get-tuple-element.11), channel_id=1, source_target_pairs={{0,1},{1,0},{2,3},{3,2},{4,5},{5,4},{6,7},{7,6},{8,9},{9,8},{10,11... | collective-permute-start | bytes 884744 | tf_op jit(solution)/shard_map/ppermute | solution.py:527
  4.6 35.9 %copy-start.2 = (bf16[2,512,384]{2,1,0:T(8,128)(2,1)S(1)}, bf16[2,512,384]{2,1,0:T(8,128)(2,1)}, u32[]{:S(2)}) copy-start(bf16[2,512,384]{2,1,0:T(8,128)(2,1)} %constant.23.clone.last_ref) | copy-start | bytes 2359300
  4.6 35.9 %copy-start.6 = (bf16[2,96,96]{2,1,0:T(8,128)(2,1)S(1)}, bf16[2,96,96]{2,1,0:T(8,128)(2,1)}, u32[]{:S(2)}) copy-start(bf16[2,96,96]{2,1,0:T(8,128)(2,1)} %constant.24.clone.second_ref) | copy-start | bytes 110596
  5.7 37.6 %copy-start.1 = (f32[3,2,3,3,1,9216]{5,4,3,2,1,0:T(1,128)S(1)}, f32[3,2,3,3,1,9216]{5,4,3,2,1,0:T(1,128)}, u32[]{:S(2)}) copy-start(f32[3,2,3,3,1,9216]{5,4,3,2,1,0:T(1,128)} %param.8) | copy-start | bytes 5971972
  41.6 1.7 %collective-permute-start.1 = (f32[584,128]{1,0:T(8,128)S(1)}, f32[584,128]{1,0:T(8,128)S(1)}, u32[]{:S(2)}, u32[]{:S(2)}) collective-permute-start(f32[584,128]{1,0:T(8,128)S(1)} %get-tuple-element.15), channel_id=1, source_target_pairs={{0,1},{1,0},{2,3},{3,2},{4,5},{5,4},{6,7},{7,6},{8,9},{9,8},{10,11... | collective-permute-start | bytes 897032 | tf_op jit(solution)/shard_map/ppermute | solution.py:571

commit v2 on v1

--- a/solution.py
+++ b/solution.py
@@ -17,6 +17,7 @@
 gain = 0.5 * step_size * peak_square
 
 params = functools.partial(pltpu.CompilerParams, vmem_limit_bytes=48 * 1024 * 1024)
+drift_weights = (1.5, 0.5, 2.0, 2.0, 2.0, 2.0, 2.0, 2.0)
 
 
 class Plan:
@@ -34,8 +35,9 @@
         self.rest = self.share - self.full
         self.tiles = 4 * side // LANES
         self.block = self.tiles * self.share
-        self.sent = -(-3 * self.block // 8) * 8
-        self.returned = -(-2 * self.block // 8) * 8 + 8
+        self.sent = -(-2 * self.block // 8) * 8
+        self.place = [(p + self.pairs // 2) % self.pairs for p in range(self.pairs)]
+        self.returned = -(-(2 * self.block + 8) // 8) * 8
 
 
 def fourier(length):
@@ -84,14 +86,6 @@
             mode = plan.share * j + start + np.arange(size).reshape(1, size, 1)
             parts.append((value[mode] + value[lane % side]).reshape(plan.tiles * size, LANES))
         owner[j] = np.concatenate(parts)
-    weights = np.zeros((2, plan.block, LANES))
-    for quad, values in enumerate(((1.5, 0.5, 2.0, 2.0), (2.0, 2.0, 2.0, 2.0))):
-        of_lane = np.array(values)[lane // side]
-        parts = [
-            np.broadcast_to(of_lane, (plan.tiles, size, LANES)).reshape(plan.tiles * size, LANES)
-            for size in (plan.full, plan.rest)
-        ]
-        weights[quad] = np.concatenate(parts)
     return {
         "last": split_table(last),
         "last_back": split_table(last.T),
@@ -99,7 +93,6 @@
         "second_back": split_table(second.T),
         "inverse_side": inverse_side.astype(np.float32),
         "owner": owner.astype(np.float32),
-        "weights": weights.astype(np.float32),
     }
 
 
@@ -148,53 +141,60 @@
     return fields
 
 
-def divergence_kernel(plan, steps, index_ref, links_ref, keep_ref, send_ref, first, second, third):
+def divergence_kernel(
+    plan, index_ref, links_ref, keep_ref, send_ref, ahead_ref, base_ref, second, third
+):
     rows, side = plan.rows, plan.side
-    size = rows // steps
-    step = pl.program_id(0)
-    start = pl.multiple_of(step * size, 8)
-    for d, target, lead in ((0, first, 0), (1, second, 8), (2, third, 8)):
-        for f, value in enumerate(projected(links_ref, d)):
-            target[f, pl.ds(start + lead, size), :] = value
-
-    @pl.when(step == steps - 1)
-    def _():
-        odd = index_ref[0] % 2
-        at_start = last_index(rows, side) == 0
-        diverge, direct = [], []
-        for f in range(8):
-            wrap(second, f, rows)
-            wrap(third, f, rows)
-            behind = moved(second, f, 8, rows, -side)
-            beside = jnp.where(
-                at_start, moved(third, f, 8, rows, side - 1), moved(third, f, 8, rows, -1)
-            )
-            here = first[f]
-            total = (behind - second[f, pl.ds(8, rows), :]) + (
-                beside - third[f, pl.ds(8, rows), :]
-            )
-            diverge.append(total - here)
-            direct.append(here)
-        for f in range(4):
-            for part, values in enumerate((diverge, direct)):
-                place = pl.ds((part * 4 + f) * rows, rows)
-                keep_ref[place, :] = jnp.where(odd == 0, values[f], values[4 + f])
-                send_ref[place, :] = jnp.where(odd == 0, values[4 + f], values[f])
+    odd = index_ref[0] % 2
+    at_start = last_index(rows, side) == 0
+    middle = pl.ds(8, rows)
+    for f, value in enumerate(projected(links_ref, 1)):
+        second[f, middle, :] = value
+        wrap(second, f, rows)
+    diverge = [moved(second, f, 8, rows, -side) - second[f, middle, :] for f in range(8)]
+    for f, value in enumerate(projected(links_ref, 2)):
+        third[f, middle, :] = value
+        wrap(third, f, rows)
+    for f in range(8):
+        beside = jnp.where(
+            at_start, moved(third, f, 8, rows, side - 1), moved(third, f, 8, rows, -1)
+        )
+        diverge[f] = diverge[f] + (beside - third[f, middle, :])
+        second[f, middle, :] = diverge[f]
+    direct = projected(links_ref, 0)
+    index = index_ref[0]
+    for f in range(8):
+        place = pl.ds(f * rows, rows)
+        total = second[f, middle, :] - direct[f]
+        ahead_ref[place, :] = jnp.where(index == plan.count_x - 1, direct[f], total)
+        base_ref[place, :] = jnp.where(index == 0, total, direct[f])
+    for f in range(4):
+        for part in range(2):
+            place = pl.ds((part * 4 + f) * rows, rows)
+            low, high = direct[f], direct[4 + f]
+            if part == 0:
+                low, high = second[f, middle, :] - low, second[4 + f, middle, :] - high
+            keep_ref[place, :] = jnp.where(odd == 0, low, high)
+            send_ref[place, :] = jnp.where(odd == 0, high, low)
 
 
 def forward_kernel(
-    plan, index_ref, keep_ref, got_ref, last_ref, second_ref, inverse_ref, sent_ref, odd_ref, dense
+    plan, index_ref, keep_ref, got_ref, last_ref, second_ref, inverse_ref, sent_ref, odd_ref, drift_ref, dense
 ):
     rows, groups, folds, side = plan.rows, plan.groups, plan.folds, plan.side
     odd = index_ref[0] % 2
     quad = 4 * rows
+    square = jnp.zeros((rows, LANES), jnp.float32)
     for f in range(4):
         own_d, own_a = keep_ref[pl.ds(f * rows, rows), :], keep_ref[pl.ds(quad + f * rows, rows), :]
         got_d, got_a = got_ref[pl.ds(f * rows, rows), :], got_ref[pl.ds(quad + f * rows, rows), :]
         even_d, odd_d = jnp.where(odd == 0, own_d, got_d), jnp.where(odd == 0, got_d, own_d)
         even_a, odd_a = jnp.where(odd == 0, own_a, got_a), jnp.where(odd == 0, got_a, own_a)
-        for q, value in enumerate((even_d, odd_d + even_a, odd_a)):
+        whole = odd_d + even_a
+        for q, value in enumerate((even_d, whole, odd_a)):
             dense[pl.ds((q * 4 + f) * rows, rows), :] = value
+        square = square + whole * whole * jnp.where(odd == 0, drift_weights[f], drift_weights[4 + f])
+    drift_ref[...] = sum_tiles(square)
     count = 12 * groups
     wide = jnp.concatenate(
         [dense[pl.ds(s, count, stride=plan.wide), :] for s in range(plan.wide)], axis=1
@@ -210,24 +210,36 @@
     inverse = inverse_ref[...]
     full, rest, pairs, tiles = plan.full, plan.rest, plan.pairs, plan.tiles
     lane = lane_of((side, LANES))
-    for q in range(3):
-        fields = [modes[:, (q * 4 + f) * LANES : (q * 4 + f + 1) * LANES] for f in range(4)]
-        if q == 1:
-            for f in range(4):
-                odd_ref[:, f * LANES : (f + 1) * LANES] = fields[f] * (gain * inverse)
+    zero = (lane == 0) & (lax.broadcasted_iota(jnp.int32, (side, LANES), 0) == 0)
+    even, between, after = [
+        [modes[:, (q * 4 + f) * LANES : (q * 4 + f + 1) * LANES] for f in range(4)] for q in range(3)
+    ]
+    shared = [value * inverse for value in between]
+    for f in range(4):
+        odd_ref[:, f * LANES : (f + 1) * LANES] = gain * shared[f]
+    below = [even[f] + shared[f] for f in range(4)]
+    above = [jnp.where(zero, between[f], after[f] + shared[f]) for f in range(4)]
+    for q, fields in enumerate((below, above)):
         for t, value in enumerate(pack(fields, lane, side)):
             at = q * tiles + t
             for j in range(pairs):
                 if full:
-                    sent_ref[j, pl.ds(at * full, full), :] = value[j * full : (j + 1) * full]
+                    sent_ref[plan.place[j], pl.ds(at * full, full), :] = value[j * full : (j + 1) * full]
                 if rest:
                     begin = pairs * full + j * rest
-                    sent_ref[j, pl.ds(3 * tiles * full + at * rest, rest), :] = value[
+                    sent_ref[plan.place[j], pl.ds(2 * tiles * full + at * rest, rest), :] = value[
                         begin : begin + rest
                     ]
-    spare = plan.sent - 3 * plan.block
+    spare = plan.sent - 2 * plan.block
     if spare:
-        sent_ref[:, pl.ds(3 * plan.block, spare), :] = jnp.zeros((pairs, spare, LANES), jnp.float32)
+        sent_ref[:, pl.ds(2 * plan.block, spare), :] = jnp.zeros((pairs, spare, LANES), jnp.float32)
+
+
+def sum_tiles(value):
+    total = value[:8]
+    for i in range(1, value.shape[0] // 8):
+        total = total + value[i * 8 : (i + 1) * 8]
+    return total
 
 
 def pack(fields, lane, side):
@@ -260,31 +272,35 @@
     return fields
 
 
-def filter_kernel(plan, index_ref, got_ref, owner_ref, weight_ref, back_ref):
+def drift_kernel(plan, index_ref, odd_ref, beside_ref, base_ref, drift_ref):
+    rows, count_x = plan.rows, plan.count_x
+    index = index_ref[0]
+    square = jnp.zeros((rows, LANES), jnp.float32)
+    for f in range(8):
+        place = pl.ds(f * rows, rows)
+        value = beside_ref[place, :] + base_ref[place, :]
+        square = square + value * value * drift_weights[f]
+    complete = (index == 0) | ((index % 2 == 1) & (index < count_x - 1))
+    drift_ref[...] = odd_ref[...] + jnp.where(complete, sum_tiles(square), 0.0)
+
+
+def filter_kernel(plan, index_ref, got_ref, owner_ref, drift_ref, back_ref):
     pairs, tiles, count_x = plan.pairs, plan.tiles, plan.count_x
     half = pairs // 2
-    drift = 0.0
-    for part, (size, first, second) in enumerate(
-        ((plan.full, 0, 0), (plan.rest, 3 * tiles * plan.full, 2 * tiles * plan.full))
-    ):
+    drift = drift_ref[...]
+    for part, (size, first) in enumerate(((plan.full, 0), (plan.rest, 2 * tiles * plan.full))):
         if not size:
             continue
         length = tiles * size
-        own = pl.ds(0 if part == 0 else tiles * plan.full, length)
-        value = owner_ref[0, own, :]
-        weight = weight_ref[0, own, :]
-
-        def plane(p, q):
-            return got_ref[p, pl.ds(first + q * length, length), :]
-
-        inverse = 1.0 / (2.0 + value)
-        odds = [plane(p, 1) for p in range(pairs)]
-        evens = [plane(p, 0) + plane((p - 1) % pairs, 2) for p in range(pairs)]
-        square = jnp.zeros_like(value)
-        for p in range(pairs):
-            square = square + (odds[p] * odds[p] + evens[p] * evens[p])
-        drift = drift + jnp.sum(square * weight)
-        rhs = [evens[p] + (odds[p] + odds[(p - 1) % pairs]) * inverse for p in range(pairs)]
+        value = owner_ref[0, pl.ds(0 if part == 0 else tiles * plan.full, length), :]
+        low, high = pl.ds(first, length), pl.ds(first + length, length)
+        inside = value > 0
+        below = [got_ref[plan.place[p], low, :] for p in range(pairs)]
+        above = [got_ref[plan.place[p], high, :] for p in range(pairs)]
+        rhs = [
+            below[p] + jnp.where(inside, above[(p - 1) % pairs], -below[(p - 1) % pairs])
+            for p in range(pairs)
+        ]
         plus = [rhs[d] + rhs[pairs - d] for d in range(1, half)]
         minus = [rhs[d] - rhs[pairs - d] for d in range(1, half)]
         cosines, sines = [], []
@@ -293,17 +309,17 @@
             for d in range(1, half):
                 total = total + plus[d - 1] * math.cos(2 * math.pi * (k * d % pairs) / pairs)
             root = 4.0 * math.sin(math.pi * k / count_x) ** 2
-            below = (value + root) * (value + (4.0 - root))
+            split = (value + root) * (value + (4.0 - root))
             scale = gain / pairs * (1.0 if k in (0, half) else 2.0)
             if k == 0:
-                factor = jnp.where(value > 0, scale * (2.0 + value) / jnp.where(value > 0, below, 1.0), 0.0)
-                whole = odds[0]
+                factor = jnp.where(inside, scale * (2.0 + value) / jnp.where(inside, split, 1.0), 0.0)
+                whole = above[0]
                 for p in range(1, pairs):
-                    whole = whole + odds[p]
-                mean = jnp.where(value > 0, 0.0, whole * (-0.25 * gain / pairs))
+                    whole = whole + above[p]
+                mean = jnp.where(inside, 0.0, whole * (-0.25 * gain / pairs))
                 cosines.append(total * factor + mean)
             else:
-                factor = scale * (2.0 + value) / below
+                factor = scale * (2.0 + value) / split
                 cosines.append(total * factor)
                 if k < half:
                     wave = jnp.zeros_like(value)
@@ -324,11 +340,10 @@
                 results[d] = even + wave
                 results[pairs - d] = even - wave
         for p in range(pairs):
-            back_ref[p, pl.ds(second, length), :] = results[p]
-            back_ref[p, pl.ds(second + length, length), :] = results[(p + 1) % pairs]
-    spare = plan.returned - 2 * plan.block
+            back_ref[plan.place[p], low, :] = results[p]
+            back_ref[plan.place[p], high, :] = results[(p + 1) % pairs]
     for p in range(pairs):
-        back_ref[p, pl.ds(2 * plan.block, spare), :] = jnp.full((spare, LANES), drift, jnp.float32)
+        back_ref[p, pl.ds(2 * plan.block, 8), :] = drift
 
 
 def backward_kernel(
@@ -342,10 +357,10 @@
             at = q * tiles + t
             for j in range(pairs):
                 if full:
-                    packed[at, pl.ds(j * full, full), :] = got_ref[j, pl.ds(at * full, full), :]
+                    packed[at, pl.ds(j * full, full), :] = got_ref[plan.place[j], pl.ds(at * full, full), :]
                 if rest:
                     packed[at, pl.ds(pairs * full + j * rest, rest), :] = got_ref[
-                        j, pl.ds(2 * tiles * full + at * rest, rest), :
+                        plan.place[j], pl.ds(2 * tiles * full + at * rest, rest), :
                     ]
     lane = lane_of((side, LANES))
     inverse = inverse_ref[...]
@@ -447,7 +462,7 @@
                 at_end, moved(here, n, 8, rows, 1 - side), moved(here, n, 8, rows, 1)
             )
         total = keep_ref[pl.ds(2 * quad, 8), :] + got_ref[pl.ds(2 * quad, 8), :]
-        drift_ref[0] = total[0, 0] * (1.0 / (9.0 * plan.count_x * plan.cells))
+        drift_ref[0] = jnp.sum(total) * (1.0 / (9.0 * plan.count_x * plan.cells))
 
     def update(i, _):
         begin = pl.multiple_of(i * 8, 8)
@@ -508,16 +523,15 @@
     block = pl.BlockSpec((54, rows // steps, LANES), lambda i: (0, i, 0))
     quads = 8 * rows
     swap = [(i, i ^ 1) for i in range(count_x)]
-    same_core = [[c + 2 * p for p in range(pairs)] for c in range(2)]
-
-    keep, send = pl.pallas_call(
-        functools.partial(divergence_kernel, plan, steps),
-        grid=(steps,),
-        out_shape=(shape_of(quads, LANES), shape_of(quads, LANES)),
-        in_specs=[scalar_spec(), block],
-        out_specs=(whole_spec(), whole_spec()),
+    halo = [(2 * p, 2 * p - 1) for p in range(1, pairs)] + [(count_x - 1, 0)]
+    same_core = [[c + 2 * p for p in sorted(range(pairs), key=plan.place.__getitem__)] for c in range(2)]
+
+    keep, send, ahead, base = pl.pallas_call(
+        functools.partial(divergence_kernel, plan),
+        out_shape=(shape_of(quads, LANES),) * 4,
+        in_specs=[scalar_spec(), whole_spec()],
+        out_specs=(whole_spec(),) * 4,
         scratch_shapes=[
-            pltpu.VMEM((8, rows, LANES), jnp.float32),
             pltpu.VMEM((8, rows + 16, LANES), jnp.float32),
             pltpu.VMEM((8, rows + 16, LANES), jnp.float32),
         ],
@@ -525,11 +539,16 @@
         name="divergence",
     )(index, links)
     got = lax.ppermute(send, "gx", swap)
-    sent, odd_part = pl.pallas_call(
+    beside = lax.ppermute(ahead, "gx", halo)
+    sent, odd_part, odd_drift = pl.pallas_call(
         functools.partial(forward_kernel, plan),
-        out_shape=(shape_of(pairs, plan.sent, LANES), shape_of(SIDE, 4 * LANES)),
+        out_shape=(
+            shape_of(pairs, plan.sent, LANES),
+            shape_of(SIDE, 4 * LANES),
+            shape_of(8, LANES),
+        ),
         in_specs=[scalar_spec()] + [whole_spec()] * 5,
-        out_specs=(whole_spec(), whole_spec()),
+        out_specs=(whole_spec(),) * 3,
         scratch_shapes=[pltpu.VMEM((12 * rows, LANES), jnp.float32)],
         compiler_params=params(),
         name="forward",
@@ -537,6 +556,15 @@
     arrived = lax.all_to_all(
         sent, "gx", split_axis=0, concat_axis=0, tiled=True, axis_index_groups=same_core
     )
+    drift_part = pl.pallas_call(
+        functools.partial(drift_kernel, plan),
+        out_shape=shape_of(8, LANES),
+        in_specs=[scalar_spec()] + [whole_spec()] * 3,
+        out_specs=whole_spec(),
+        compiler_params=params(),
+        cost_estimate=pl.CostEstimate(flops=5 * 10**10, bytes_accessed=5 * 10**7, transcendentals=0),
+        name="drift",
+    )(index, odd_drift, beside, base)
     back = pl.pallas_call(
         functools.partial(filter_kernel, plan),
         grid_spec=pltpu.PrefetchScalarGridSpec(
@@ -545,14 +573,14 @@
             in_specs=[
                 pl.BlockSpec((pairs, plan.sent, LANES), lambda i, at: (0, 0, 0)),
                 pl.BlockSpec((1, plan.block, LANES), lambda i, at: (at[0] // 2, 0, 0)),
-                pl.BlockSpec((1, plan.block, LANES), lambda i, at: (at[0] % 2, 0, 0)),
+                pl.BlockSpec((8, LANES), lambda i, at: (0, 0)),
             ],
             out_specs=pl.BlockSpec((pairs, plan.returned, LANES), lambda i, at: (0, 0, 0)),
         ),
         out_shape=shape_of(pairs, plan.returned, LANES),
         compiler_params=params(),
         name="filter",
-    )(index, arrived, table["owner"], table["weights"])
+    )(index, arrived, table["owner"], drift_part)
     returned = lax.all_to_all(
         back, "gx", split_axis=0, concat_axis=0, tiled=True, axis_index_groups=same_core
     )

time: 47.3 us -> 40.1 us (0.85)
  blocking collectives: 34.6 us -> 11.7 us
  starting transfers between devices: 0.59 us -> 10.9 us
  waiting for transfers between devices: 2.78 us -> 7.6 us
  Pallas kernels: 6.75 us -> 7.25 us
    all_to_all x1 -> x0, blocking collectives: 20.6 us -> none  [local(): lax.all_to_all(sent, 'gx', split_axis=0, concat_axis=0, tiled=True, axis_...]
    all_to_all x0 -> x1, starting transfers between devices: none -> 9.08 us  [local(): lax.all_to_all(sent, 'gx', split_axis=0, concat_axis=0, tiled=True, axis_...]
    all_to_all x0 -> x1, waiting for transfers between devices: none -> 6.02 us  [local(): lax.all_to_all(sent, 'gx', split_axis=0, concat_axis=0, tiled=True, axis_...]
    all_to_all x1, blocking collectives: 14 us -> 11.7 us  [local(): lax.all_to_all(back, 'gx', split_axis=0, concat_axis=0, tiled=True, axis_...]
    ppermute x0 -> x1, starting transfers between devices: none -> 1.28 us  [local(): beside = lax.ppermute(ahead, 'gx', halo)]
    ppermute x2, waiting for transfers between devices: 2.78 us -> 1.58 us  [local(): got = lax.ppermute(send, 'gx', swap)]
    pallas_call x1, Pallas kernels: 1.07 us -> 1.79 us  [local(): pl.pallas_call(functools.partial(forward_kernel, plan), out_shape=(shape_...]
    unnamed x18 -> x16, local copies, waits for them, and re-layouts: 1.59 us -> 1.58 us
  transfers between devices with their start and end apart: 2 -> 4, of which waited for: 2 -> 2; matrix products, arithmetic and copies ran while one was open for 0% -> 0% of each run, Pallas kernels for 0% -> 5%
where the time goes in v2:
time: 40.1 us; the launch traced here: 39.8 us
  blocking collectives  11.7 us (29%)
  starting transfers between devices  10.9 us (27%)
  waiting for transfers between devices  7.6 us (19%)
  Pallas kernels  7.25 us (18%)
  local copies, waits for them, and re-layouts  1.58 us (4%)
  between operations  0.75 us (2%)
    all_to_all x1, blocking collectives, local(): lax.all_to_all(back, 'gx', split_axis=0, concat_axis=0, tiled=True, axis_...  11.7 us
    all_to_all x1, starting transfers between devices, local(): lax.all_to_all(sent, 'gx', split_axis=0, concat_axis=0, tiled=True, axis_...  9.08 us
    all_to_all x1, waiting for transfers between devices, local(): lax.all_to_all(sent, 'gx', split_axis=0, concat_axis=0, tiled=True, axis_...  6.02 us
    pallas_call x1, Pallas kernels, local(): pl.pallas_call(functools.partial(update_kernel, plan, steps), grid=(steps...  3.87 us
    pallas_call x1, Pallas kernels, local(): pl.pallas_call(functools.partial(forward_kernel, plan), out_shape=(shape_...  1.79 us
    unnamed x16, local copies, waits for them, and re-layouts  1.58 us
    ppermute x2, waiting for transfers between devices, local(): got = lax.ppermute(send, 'gx', swap)  1.58 us
    ppermute x1, starting transfers between devices, local(): beside = lax.ppermute(ahead, 'gx', halo)  1.28 us
  transfers between devices with their start and end apart: 4, of which 2 were waited for; matrix products, arithmetic and copies ran while one was open for 0% of the time, Pallas kernels for 5%

profile of v2, /device:TPU:0, one launch (start us, length us, event | category | flops | bytes accessed | tf_op | source)
XLA Modules:
  0.0 39.8 jit_solution(11219157720122295665)
XLA Ops:
  0.6 0.0 copy-start
  0.6 1.5 %copy-done = f32[3,2,3,3,1,9216]{5,4,3,2,1,0:T(1,128)S(1)} copy-done((f32[3,2,3,3,1,9216]{5,4,3,2,1,0:T(1,128)S(1)}, f32[3,2,3,3,1,9216]{5,4,3,2,1,0:T(1,128)}, u32[]{:S(2)}) %copy-start) | copy-done | bytes 1990680
  2.2 0.4 divergence.1
  2.6 0.5 %collective-permute-start = (f32[576,128]{1,0:T(8,128)S(1)}, f32[576,128]{1,0:T(8,128)S(1)}, u32[]{:S(2)}, u32[]{:S(2)}) collective-permute-start(f32[576,128]{1,0:T(8,128)S(1)} %get-tuple-element.14), channel_id=1, source_target_pairs={{0,1},{1,0},{2,3},{3,2},{4,5},{5,4},{6,7},{7,6},{8,9},{9,8},{10,11... | collective-permute-start | bytes 884744 | tf_op jit(solution)/shard_map/ppermute | solution.py:541
  3.1 1.3 %collective-permute-start.1 = (f32[576,128]{1,0:T(8,128)S(1)}, f32[576,128]{1,0:T(8,128)S(1)}, u32[]{:S(2)}, u32[]{:S(2)}) collective-permute-start(f32[576,128]{1,0:T(8,128)S(1)} %get-tuple-element.17), channel_id=1, source_target_pairs={{2,1},{4,3},{6,5},{8,7},{10,9},{12,11},{14,13},{15,0},{18,17},{20,... | collective-permute-start | bytes 884744 | tf_op jit(solution)/shard_map/ppermute | solution.py:542
  4.4 0.0 collective-permute-done.got_ref
  4.4 0.0 copy-done.3
  4.4 0.0 copy-done.4
  4.4 0.0 copy-done.7
  4.4 1.8 %forward.1 = (f32[8,72,128]{2,1,0:T(8,128)}, f32[96,512]{1,0:T(8,128)S(1)}, f32[8,128]{1,0:T(8,128)S(1)}) custom-call(s32[1]{0:T(128)} %bitcast.index_ref, f32[576,128]{1,0:T(8,128)S(1)} %get-tuple-element.13.keep_ref, f32[576,128]{1,0:T(8,128)S(1)} %collective-permute-done.got_ref, bf16[2,384,512]{2,1,0:T(8,128)(2,1)S(1)} %copy-done.3, ...), custom_call_target="tpu_custom_call" | custom-call | tf_op jit(solution)/shard_map/forward/pallas_call | solution.py:543
  6.2 9.1 %all-to-all-start = ((f32[8,72,128]{2,1,0:T(8,128)}), f32[8,72,128]{2,1,0:T(8,128)S(1)}, u32[]{:S(2)}, u32[]{:S(2)}) async-start(f32[8,72,128]{2,1,0:T(8,128)} %get-tuple-element.15), calls=%async_computation | async-start | bytes 589824 | tf_op jit(solution)/shard_map/all_to_all | solution.py:556
  15.3 0.0 collective-permute-done.1.beside_ref
  15.3 0.0 copy-start.2
  15.3 0.0 copy-start.6
  15.3 0.1 drift.1.drift_ref
  15.4 0.0 copy-start.1
  15.4 6.0 %all-to-all-done.got_ref = f32[8,72,128]{2,1,0:T(8,128)S(1)} async-done(((f32[8,72,128]{2,1,0:T(8,128)}), f32[8,72,128]{2,1,0:T(8,128)S(1)}, u32[]{:S(2)}, u32[]{:S(2)}) %all-to-all-start) | async-done | bytes 294944 | tf_op jit(solution)/shard_map/all_to_all | solution.py:556
  21.4 0.0 copy-done.5
  21.4 0.1 filter.1
  21.5 11.7 %all_to_all.10.got_ref = f32[8,80,128]{2,1,0:T(8,128)S(1)} all-to-all(f32[8,80,128]{2,1,0:T(8,128)S(1)} %filter.1), channel_id=1, replica_groups={{8,10,12,14,0,2,4,6},{9,11,13,15,1,3,5,7},{24,26,28,30,16,18,20,22},{25..., dimensions={0} | all-to-all | bytes 655360 | tf_op jit(solution)/shard_map/all_to_all | solution.py:584
  33.2 1.0 %backward.1 = (f32[584,128]{1,0:T(8,128)S(1)}, f32[584,128]{1,0:T(8,128)S(1)}) custom-call(s32[1]{0:T(128)} %bitcast.index_ref, f32[8,80,128]{2,1,0:T(8,128)S(1)} %all_to_all.10.got_ref, f32[96,512]{1,0:T(8,128)S(1)} %get-tuple-element.19.odd_ref, bf16[2,512,384]{2,1,0:T(8,128)(2,1)S(1)} %copy-done.2, bf16[2,96,96]{2,1,0:T(8,128)(2,1)S(1)} %copy-done.6, ...), custom_call_target="tpu_custom_call" | custom-call | tf_op jit(solution)/shard_map/backward/pallas_call | solution.py:587
  34.3 0.1 collective-permute-start.2
  34.3 1.6 %collective-permute-done.2.got_ref = f32[584,128]{1,0:T(8,128)S(1)} collective-permute-done((f32[584,128]{1,0:T(8,128)S(1)}, f32[584,128]{1,0:T(8,128)S(1)}, u32[]{:S(2)}, u32[]{:S(2)}) %collective-permute-start.2) | collective-permute-done | bytes 299040 | tf_op jit(solution)/shard_map/ppermute | solution.py:599
  35.9 3.9 %update.1 = (f32[54,72,128]{2,1,0:T(8,128)}, f32[1]{0:T(128)}) custom-call(s32[1]{0:T(128)} %bitcast.index_ref, f32[584,128]{1,0:T(8,128)S(1)} %get-tuple-element.20.keep_ref, f32[584,128]{1,0:T(8,128)S(1)} %collective-permute-done.2.got_ref, f32[54,72,128]{2,1,0:T(8,128)S(1)} %bitcast.4), custom_call_target="tpu_custom_call" | custom-call | tf_op jit(solution)/shard_map/update/pallas_call | solution.py:600
  (7 shorter events, 0.0 us)
Async XLA Ops:
  0.6 1.6 %copy-start = (f32[3,2,3,3,1,9216]{5,4,3,2,1,0:T(1,128)S(1)}, f32[3,2,3,3,1,9216]{5,4,3,2,1,0:T(1,128)}, u32[]{:S(2)}) copy-start(f32[3,2,3,3,1,9216]{5,4,3,2,1,0:T(1,128)} %param.7) | copy-start | bytes 5971972
  2.2 2.2 %copy-start.3 = (bf16[2,384,512]{2,1,0:T(8,128)(2,1)S(1)}, bf16[2,384,512]{2,1,0:T(8,128)(2,1)}, u32[]{:S(2)}) copy-start(bf16[2,384,512]{2,1,0:T(8,128)(2,1)} %constant.16.clone.last_ref) | copy-start | bytes 2359300
  2.2 2.2 %copy-start.4 = (f32[96,128]{1,0:T(8,128)S(1)}, f32[96,128]{1,0:T(8,128)}, u32[]{:S(2)}) copy-start(f32[96,128]{1,0:T(8,128)} %constant.18.clone.inverse_ref) | copy-start | bytes 147460
  2.2 2.2 %copy-start.7 = (bf16[2,96,96]{2,1,0:T(8,128)(2,1)S(1)}, bf16[2,96,96]{2,1,0:T(8,128)(2,1)}, u32[]{:S(2)}) copy-start(bf16[2,96,96]{2,1,0:T(8,128)(2,1)} %constant.17.clone.second_ref) | copy-start | bytes 110596
  2.6 1.8 %collective-permute-start = (f32[576,128]{1,0:T(8,128)S(1)}, f32[576,128]{1,0:T(8,128)S(1)}, u32[]{:S(2)}, u32[]{:S(2)}) collective-permute-start(f32[576,128]{1,0:T(8,128)S(1)} %get-tuple-element.14), channel_id=1, source_target_pairs={{0,1},{1,0},{2,3},{3,2},{4,5},{5,4},{6,7},{7,6},{8,9},{9,8},{10,11... | collective-permute-start | bytes 884744 | tf_op jit(solution)/shard_map/ppermute | solution.py:541
  3.1 12.2 %collective-permute-start.1 = (f32[576,128]{1,0:T(8,128)S(1)}, f32[576,128]{1,0:T(8,128)S(1)}, u32[]{:S(2)}, u32[]{:S(2)}) collective-permute-start(f32[576,128]{1,0:T(8,128)S(1)} %get-tuple-element.17), channel_id=1, source_target_pairs={{2,1},{4,3},{6,5},{8,7},{10,9},{12,11},{14,13},{15,0},{18,17},{20,... | collective-permute-start | bytes 884744 | tf_op jit(solution)/shard_map/ppermute | solution.py:542
  6.2 15.2 %all-to-all-start = ((f32[8,72,128]{2,1,0:T(8,128)}), f32[8,72,128]{2,1,0:T(8,128)S(1)}, u32[]{:S(2)}, u32[]{:S(2)}) async-start(f32[8,72,128]{2,1,0:T(8,128)} %get-tuple-element.15), calls=%async_computation | async-start | bytes 589824 | tf_op jit(solution)/shard_map/all_to_all | solution.py:556
  15.3 6.1 %copy-start.5 = (f32[8,36,128]{2,1,0:T(8,128)S(1)}, f32[8,36,128]{2,1,0:T(8,128)}, u32[]{:S(2)}) copy-start(f32[8,36,128]{2,1,0:T(8,128)} %constant.19.clone.owner_ref) | copy-start | bytes 442372
  15.3 17.9 %copy-start.2 = (bf16[2,512,384]{2,1,0:T(8,128)(2,1)S(1)}, bf16[2,512,384]{2,1,0:T(8,128)(2,1)}, u32[]{:S(2)}) copy-start(bf16[2,512,384]{2,1,0:T(8,128)(2,1)} %constant.20.clone.last_ref) | copy-start | bytes 2359300
  15.3 17.9 %copy-start.6 = (bf16[2,96,96]{2,1,0:T(8,128)(2,1)S(1)}, bf16[2,96,96]{2,1,0:T(8,128)(2,1)}, u32[]{:S(2)}) copy-start(bf16[2,96,96]{2,1,0:T(8,128)(2,1)} %constant.21.clone.second_ref) | copy-start | bytes 110596
  15.4 20.5 %copy-start.1 = (f32[3,2,3,3,1,9216]{5,4,3,2,1,0:T(1,128)S(1)}, f32[3,2,3,3,1,9216]{5,4,3,2,1,0:T(1,128)}, u32[]{:S(2)}) copy-start(f32[3,2,3,3,1,9216]{5,4,3,2,1,0:T(1,128)} %param.7) | copy-start | bytes 5971972
  34.3 1.7 %collective-permute-start.2 = (f32[584,128]{1,0:T(8,128)S(1)}, f32[584,128]{1,0:T(8,128)S(1)}, u32[]{:S(2)}, u32[]{:S(2)}) collective-permute-start(f32[584,128]{1,0:T(8,128)S(1)} %get-tuple-element.21), channel_id=1, source_target_pairs={{0,1},{1,0},{2,3},{3,2},{4,5},{5,4},{6,7},{7,6},{8,9},{9,8},{10,11... | collective-permute-start | bytes 897032 | tf_op jit(solution)/shard_map/ppermute | solution.py:599

commit v3 on v2

--- a/solution.py
+++ b/solution.py
@@ -35,6 +35,7 @@
         self.rest = self.share - self.full
         self.tiles = 4 * side // LANES
         self.block = self.tiles * self.share
+        self.stride = -(-self.block // 8) * 8
         self.sent = -(-2 * self.block // 8) * 8
         self.place = [(p + self.pairs // 2) % self.pairs for p in range(self.pairs)]
         self.returned = -(-(2 * self.block + 8) // 8) * 8
@@ -62,6 +63,11 @@
     high = table.astype(jnp.bfloat16)
     low = (table - high.astype(np.float64)).astype(jnp.bfloat16)
     return np.stack([high, low])
+
+
+def stack_table(table):
+    high, low = split_table(table)
+    return np.block([[high, high], [low, np.zeros_like(low)]])
 
 
 def tables(plan):
@@ -79,20 +85,18 @@
     inverse_side = np.zeros((side, LANES))
     inverse_side[:, :side] = 1.0 / (2.0 + value[order][:, None] + value[None, :])
     lane = np.arange(plan.tiles * LANES).reshape(plan.tiles, 1, LANES)
-    owner = np.zeros((plan.pairs, plan.block, LANES))
+    owner = np.zeros((plan.pairs, plan.stride, LANES))
     for j in range(plan.pairs):
         parts = []
         for start, size in ((0, plan.full), (plan.full, plan.rest)):
             mode = plan.share * j + start + np.arange(size).reshape(1, size, 1)
             parts.append((value[mode] + value[lane % side]).reshape(plan.tiles * size, LANES))
-        owner[j] = np.concatenate(parts)
+        owner[j, : plan.block] = np.concatenate(parts)
     return {
-        "last": split_table(last),
-        "last_back": split_table(last.T),
-        "second": split_table(second),
-        "second_back": split_table(second.T),
-        "inverse_side": inverse_side.astype(np.float32),
-        "owner": owner.astype(np.float32),
+        "last": np.stack([split_table(last[a:b, c:d]) for a, b, c, d in bands(plan)]),
+        "last_back": np.stack([split_table(last[a:b, c:d].T) for a, b, c, d in bands(plan)]),
+        "second": np.stack([stack_table(second), stack_table(second.T)]),
+        "modes": np.concatenate([inverse_side, owner.reshape(-1, LANES)]).astype(np.float32),
     }
 
 
@@ -105,6 +109,19 @@
 def product(left, right):
     dot = functools.partial(jnp.dot, preferred_element_type=jnp.float32)
     return dot(left[0], right[0]) + (dot(left[0], right[1]) + dot(left[1], right[0]))
+
+
+def stacked(table, value):
+    both = jnp.dot(table, jnp.concatenate(halve(value), axis=0), preferred_element_type=jnp.float32)
+    size = both.shape[0] // 2
+    return both[:size] + both[size:]
+
+
+def bands(plan):
+    for j in range(0, plan.folds, 2):
+        rows = min(2, plan.folds - j)
+        begin, end = j * plan.side // LANES, -(-(j + rows) * plan.side // LANES)
+        yield begin * LANES, end * LANES, j * LANES, (j + rows) * LANES
 
 
 def lane_of(shape):
@@ -141,18 +158,36 @@
     return fields
 
 
+def link_copies(links_ref, staged, semaphores):
+    copies = []
+    for n, d in enumerate((1, 2, 0)):
+        for m, (begin, size) in enumerate(((1, 3), (5, 3), (9, 9))):
+            place = pl.ds(d * 18 + begin, size)
+            copies.append(
+                pltpu.make_async_copy(links_ref.at[place], staged.at[place], semaphores.at[n, m])
+            )
+    return copies
+
+
 def divergence_kernel(
-    plan, index_ref, links_ref, keep_ref, send_ref, ahead_ref, base_ref, second, third
+    plan, index_ref, links_ref, keep_ref, send_ref, ahead_ref, base_ref, staged, second, third, semaphores
 ):
     rows, side = plan.rows, plan.side
+    copies = link_copies(links_ref, staged, semaphores)
+    for copy in copies:
+        copy.start()
     odd = index_ref[0] % 2
     at_start = last_index(rows, side) == 0
     middle = pl.ds(8, rows)
-    for f, value in enumerate(projected(links_ref, 1)):
+    for copy in copies[:3]:
+        copy.wait()
+    for f, value in enumerate(projected(staged, 1)):
         second[f, middle, :] = value
         wrap(second, f, rows)
     diverge = [moved(second, f, 8, rows, -side) - second[f, middle, :] for f in range(8)]
-    for f, value in enumerate(projected(links_ref, 2)):
+    for copy in copies[3:6]:
+        copy.wait()
+    for f, value in enumerate(projected(staged, 2)):
         third[f, middle, :] = value
         wrap(third, f, rows)
     for f in range(8):
@@ -161,7 +196,9 @@
         )
         diverge[f] = diverge[f] + (beside - third[f, middle, :])
         second[f, middle, :] = diverge[f]
-    direct = projected(links_ref, 0)
+    for copy in copies[6:]:
+        copy.wait()
+    direct = projected(staged, 0)
     index = index_ref[0]
     for f in range(8):
         place = pl.ds(f * rows, rows)
@@ -179,7 +216,7 @@
 
 
 def forward_kernel(
-    plan, index_ref, keep_ref, got_ref, last_ref, second_ref, inverse_ref, sent_ref, odd_ref, drift_ref, dense
+    plan, index_ref, keep_ref, got_ref, last_ref, second_ref, modes_ref, sent_ref, odd_ref, drift_ref, dense
 ):
     rows, groups, folds, side = plan.rows, plan.groups, plan.folds, plan.side
     odd = index_ref[0] % 2
@@ -199,15 +236,25 @@
     wide = jnp.concatenate(
         [dense[pl.ds(s, count, stride=plan.wide), :] for s in range(plan.wide)], axis=1
     )
-    waves = product(halve(wide), (last_ref[0], last_ref[1]))
+    high, low = halve(wide)
+    waves = jnp.concatenate(
+        [
+            product(
+                (high[:, begin:end], low[:, begin:end]),
+                (last_ref[n, 0], last_ref[n, 1]),
+            )
+            for n, (begin, end, _, _) in enumerate(bands(plan))
+        ],
+        axis=1,
+    )
     columns = []
     for pf in range(12):
         part = waves[pf * groups : (pf + 1) * groups]
         columns.append(
             jnp.concatenate([part[:, j * LANES : (j + 1) * LANES] for j in range(folds)], axis=0)
         )
-    modes = product((second_ref[0], second_ref[1]), halve(jnp.concatenate(columns, axis=1)))
-    inverse = inverse_ref[...]
+    modes = stacked(second_ref[0], jnp.concatenate(columns, axis=1))
+    inverse = modes_ref[:side]
     full, rest, pairs, tiles = plan.full, plan.rest, plan.pairs, plan.tiles
     lane = lane_of((side, LANES))
     zero = (lane == 0) & (lax.broadcasted_iota(jnp.int32, (side, LANES), 0) == 0)
@@ -284,7 +331,7 @@
     drift_ref[...] = odd_ref[...] + jnp.where(complete, sum_tiles(square), 0.0)
 
 
-def filter_kernel(plan, index_ref, got_ref, owner_ref, drift_ref, back_ref):
+def filter_kernel(plan, index_ref, got_ref, modes_ref, drift_ref, back_ref):
     pairs, tiles, count_x = plan.pairs, plan.tiles, plan.count_x
     half = pairs // 2
     drift = drift_ref[...]
@@ -292,7 +339,8 @@
         if not size:
             continue
         length = tiles * size
-        value = owner_ref[0, pl.ds(0 if part == 0 else tiles * plan.full, length), :]
+        own = pl.multiple_of(plan.side + index_ref[0] // 2 * plan.stride, 8)
+        value = modes_ref[pl.ds(own, plan.stride), :][part * tiles * plan.full :][:length]
         low, high = pl.ds(first, length), pl.ds(first + length, length)
         inside = value > 0
         below = [got_ref[plan.place[p], low, :] for p in range(pairs)]
@@ -347,7 +395,7 @@
 
 
 def backward_kernel(
-    plan, index_ref, got_ref, odd_ref, last_ref, second_ref, inverse_ref, keep_ref, send_ref, packed, dense
+    plan, index_ref, got_ref, odd_ref, last_ref, second_ref, modes_ref, keep_ref, send_ref, packed, dense
 ):
     rows, groups, folds, side = plan.rows, plan.groups, plan.folds, plan.side
     full, rest, pairs, tiles = plan.full, plan.rest, plan.pairs, plan.tiles
@@ -363,26 +411,32 @@
                         plan.place[j], pl.ds(2 * tiles * full + at * rest, rest), :
                     ]
     lane = lane_of((side, LANES))
-    inverse = inverse_ref[...]
+    inverse = modes_ref[:side]
     even, after = [
         unpack([packed[q * tiles + t] for t in range(tiles)], lane, side) for q in range(2)
     ]
     between = [
         odd_ref[:, f * LANES : (f + 1) * LANES] + (even[f] + after[f]) * inverse for f in range(4)
     ]
-    waves = product(
-        (second_ref[0], second_ref[1]), halve(jnp.concatenate(even + between + after, axis=1))
-    )
+    waves = stacked(second_ref[1], jnp.concatenate(even + between + after, axis=1))
     blocks = []
     for pf in range(12):
         part = waves[:, pf * LANES : (pf + 1) * LANES]
         blocks.append(
             jnp.concatenate([part[j * groups : (j + 1) * groups] for j in range(folds)], axis=1)
         )
-    wide = product(halve(jnp.concatenate(blocks, axis=0)), (last_ref[0], last_ref[1]))
+    high, low = halve(jnp.concatenate(blocks, axis=0))
+    wide = [None] * plan.wide
+    for n, (begin, end, first, last) in enumerate(bands(plan)):
+        part = product(
+            (high[:, first:last], low[:, first:last]), (last_ref[n, 0], last_ref[n, 1])
+        )
+        for s in range(begin // LANES, end // LANES):
+            tile = part[:, s * LANES - begin : (s + 1) * LANES - begin]
+            wide[s] = tile if wide[s] is None else wide[s] + tile
     count = 12 * groups
     for s in range(plan.wide):
-        dense[pl.ds(s, count, stride=plan.wide), :] = wide[:, s * LANES : (s + 1) * LANES]
+        dense[pl.ds(s, count, stride=plan.wide), :] = wide[s]
     quad = 4 * rows
     low, middle, high = [dense[pl.ds(q * quad, quad), :] for q in range(3)]
     keep_ref[pl.ds(0, quad), :] = jnp.where(odd == 0, low, middle)
@@ -429,71 +483,85 @@
 
 
 def update_kernel(
-    plan, steps, index_ref, keep_ref, got_ref, links_ref, fixed_ref, drift_ref, here, along_x, along_y, along_z
+    plan, unroll, index_ref, keep_ref, got_ref, links_ref, fixed_ref, drift_ref, here, along, staged, semaphores
 ):
     rows, side = plan.rows, plan.side
     quad = 4 * rows
-    size = rows // steps
-    step = pl.program_id(0)
-
-    @pl.when(step == 0)
-    def _():
-        odd = index_ref[0] % 2
-
-        def turn(i, _):
-            begin = pl.multiple_of(i * 8, 8)
-            for q, target, lead in ((0, here, 8), (1, along_x, 0)):
-                fields = [None] * 8
-                for f in range(4):
-                    place = pl.ds(pl.multiple_of(q * quad + f * rows + begin, 8), 8)
-                    own, other = keep_ref[place, :], got_ref[place, :]
-                    fields[f] = jnp.where(odd == 0, own, other)
-                    fields[4 + f] = jnp.where(odd == 0, other, own)
-                for n, value in enumerate(rotation(fields)):
-                    target[n, pl.ds(begin + lead, 8), :] = value
-            return 0
-
-        lax.fori_loop(0, rows // 8, turn, 0)
-        at_end = last_index(rows, side) == side - 1
-        for n in range(18):
-            wrap(here, n, rows)
-            along_y[n] = moved(here, n, 8, rows, side)
-            along_z[n] = jnp.where(
-                at_end, moved(here, n, 8, rows, 1 - side), moved(here, n, 8, rows, 1)
-            )
-        total = keep_ref[pl.ds(2 * quad, 8), :] + got_ref[pl.ds(2 * quad, 8), :]
-        drift_ref[0] = jnp.sum(total) * (1.0 / (9.0 * plan.count_x * plan.cells))
-
-    def update(i, _):
+    odd = index_ref[0] % 2
+
+    def turn(i, _):
         begin = pl.multiple_of(i * 8, 8)
-        place = pl.multiple_of(step * size + i * 8, 8)
-
-        def matrix(ref, lead):
-            value = [ref[n, pl.ds(place + lead, 8), :] for n in range(18)]
+        for q, lead in ((0, 8), (1, 0)):
+            fields = [None] * 8
+            for f in range(4):
+                place = pl.ds(pl.multiple_of(q * quad + f * rows + begin, 8), 8)
+                own, other = keep_ref[place, :], got_ref[place, :]
+                fields[f] = jnp.where(odd == 0, own, other)
+                fields[4 + f] = jnp.where(odd == 0, other, own)
+            for n, value in enumerate(rotation(fields)):
+                if q == 0:
+                    here[n, pl.ds(begin + lead, 8), :] = value
+                else:
+                    along[0, n, pl.ds(begin, 8), :] = value
+        return 0
+
+    lax.fori_loop(0, rows // 8, turn, 0, unroll=unroll[0])
+
+    def update(d, i):
+        begin = pl.multiple_of(i * 8, 8)
+
+        def matrix(read):
+            value = [read(n) for n in range(18)]
             return [[(value[3 * r + c], value[9 + 3 * r + c]) for c in range(3)] for r in range(3)]
 
-        for d, ahead_ref in enumerate((along_x, along_y, along_z)):
-            own = matrix(here, 8)
-            links = [
-                [
-                    tuple(links_ref[((d * 2 + part) * 3 + r) * 3 + c, pl.ds(begin, 8), :] for part in range(2))
-                    for c in range(3)
-                ]
-                for r in range(3)
+        own = matrix(lambda n: here[n, pl.ds(begin + 8, 8), :])
+        links = matrix(lambda n: links_ref[d * 18 + n, pl.ds(begin, 8), :])
+        ahead = matrix(lambda n: along[d, n, pl.ds(begin, 8), :])
+        for r in range(3):
+            line = [
+                add(times(own[r][0], links[0][c]), times(own[r][1], links[1][c]), times(own[r][2], links[2][c]))
+                for c in range(3)
             ]
-            ahead = matrix(ahead_ref, 0)
-            for r in range(3):
-                line = [
-                    add(times(own[r][0], links[0][c]), times(own[r][1], links[1][c]), times(own[r][2], links[2][c]))
-                    for c in range(3)
-                ]
-                for c in range(3):
-                    value = add(*[times_conj(line[k], ahead[c][k]) for k in range(3)])
-                    for part in range(2):
-                        fixed_ref[((d * 2 + part) * 3 + r) * 3 + c, pl.ds(begin, 8), :] = value[part]
-        return 0
-
-    lax.fori_loop(0, size // 8, update, 0)
+            for c in range(3):
+                value = add(*[times_conj(line[k], ahead[c][k]) for k in range(3)])
+                for part in range(2):
+                    staged[d * 18 + part * 9 + r * 3 + c, pl.ds(begin, 8), :] = value[part]
+
+    tiles = rows // 8
+    copies = []
+
+    def write(place, rows_place, n):
+        copy = pltpu.make_async_copy(
+            staged.at[place, rows_place], fixed_ref.at[place, rows_place], semaphores.at[n]
+        )
+        copy.start()
+        copies.append(copy)
+
+    for d in (1, 2, 0):
+        if d == 1:
+            for n in range(18):
+                wrap(here, n, rows)
+                along[1, n] = moved(here, n, 8, rows, side)
+        if d == 2:
+            at_end = last_index(rows, side) == side - 1
+            for n in range(18):
+                along[2, n] = jnp.where(
+                    at_end, moved(here, n, 8, rows, 1 - side), moved(here, n, 8, rows, 1)
+                )
+        chunks = 1 if d else 3
+        for m in range(chunks):
+            part = tiles // chunks
+
+            def step(i, _, d=d):
+                update(d, i)
+                return 0
+
+            lax.fori_loop(m * part, (m + 1) * part, step, 0, unroll=unroll[1])
+            write(pl.ds(d * 18, 18), pl.ds(m * part * 8, part * 8), len(copies))
+    total = keep_ref[pl.ds(2 * quad, 8), :] + got_ref[pl.ds(2 * quad, 8), :]
+    drift_ref[0] = jnp.sum(total) * (1.0 / (9.0 * plan.count_x * plan.cells))
+    for copy in copies:
+        copy.wait()
 
 
 def add(first, second, third):
@@ -519,8 +587,6 @@
     table = tables(plan)
     index = lax.axis_index("gx").astype(jnp.int32).reshape(1)
     links = gauge_links.reshape(54, rows, LANES)
-    steps = 3
-    block = pl.BlockSpec((54, rows // steps, LANES), lambda i: (0, i, 0))
     quads = 8 * rows
     swap = [(i, i ^ 1) for i in range(count_x)]
     halo = [(2 * p, 2 * p - 1) for p in range(1, pairs)] + [(count_x - 1, 0)]
@@ -529,15 +595,17 @@
     keep, send, ahead, base = pl.pallas_call(
         functools.partial(divergence_kernel, plan),
         out_shape=(shape_of(quads, LANES),) * 4,
-        in_specs=[scalar_spec(), whole_spec()],
+        in_specs=[scalar_spec(), pl.BlockSpec(memory_space=pltpu.HBM)],
         out_specs=(whole_spec(),) * 4,
         scratch_shapes=[
+            pltpu.VMEM((54, rows, LANES), jnp.float32),
             pltpu.VMEM((8, rows + 16, LANES), jnp.float32),
             pltpu.VMEM((8, rows + 16, LANES), jnp.float32),
+            pltpu.SemaphoreType.DMA((3, 3)),
         ],
         compiler_params=params(),
         name="divergence",
-    )(index, links)
+    )(index, pltpu.with_memory_space_constraint(links, pltpu.HBM))
     got = lax.ppermute(send, "gx", swap)
     beside = lax.ppermute(ahead, "gx", halo)
     sent, odd_part, odd_drift = pl.pallas_call(
@@ -552,7 +620,7 @@
         scratch_shapes=[pltpu.VMEM((12 * rows, LANES), jnp.float32)],
         compiler_params=params(),
         name="forward",
-    )(index, keep, got, table["last"], table["second"], table["inverse_side"])
+    )(index, keep, got, table["last"], table["second"], table["modes"])
     arrived = lax.all_to_all(
         sent, "gx", split_axis=0, concat_axis=0, tiled=True, axis_index_groups=same_core
     )
@@ -567,20 +635,12 @@
     )(index, odd_drift, beside, base)
     back = pl.pallas_call(
         functools.partial(filter_kernel, plan),
-        grid_spec=pltpu.PrefetchScalarGridSpec(
-            num_scalar_prefetch=1,
-            grid=(1,),
-            in_specs=[
-                pl.BlockSpec((pairs, plan.sent, LANES), lambda i, at: (0, 0, 0)),
-                pl.BlockSpec((1, plan.block, LANES), lambda i, at: (at[0] // 2, 0, 0)),
-                pl.BlockSpec((8, LANES), lambda i, at: (0, 0)),
-            ],
-            out_specs=pl.BlockSpec((pairs, plan.returned, LANES), lambda i, at: (0, 0, 0)),
-        ),
         out_shape=shape_of(pairs, plan.returned, LANES),
+        in_specs=[scalar_spec()] + [whole_spec()] * 3,
+        out_specs=whole_spec(),
         compiler_params=params(),
         name="filter",
-    )(index, arrived, table["owner"], drift_part)
+    )(index, arrived, table["modes"], drift_part)
     returned = lax.all_to_all(
         back, "gx", split_axis=0, concat_axis=0, tiled=True, axis_index_groups=same_core
     )
@@ -595,19 +655,18 @@
         ],
         compiler_params=params(),
         name="backward",
-    )(index, returned, odd_part, table["last_back"], table["second_back"], table["inverse_side"])
+    )(index, returned, odd_part, table["last_back"], table["second"], table["modes"])
     got = lax.ppermute(send, "gx", swap)
     fixed, drift = pl.pallas_call(
-        functools.partial(update_kernel, plan, steps),
-        grid=(steps,),
+        functools.partial(update_kernel, plan, (3, 3)),
         out_shape=(shape_of(54, rows, LANES), shape_of(1)),
-        in_specs=[scalar_spec(), whole_spec(), whole_spec(), block],
-        out_specs=(block, scalar_spec()),
+        in_specs=[scalar_spec()] + [whole_spec()] * 3,
+        out_specs=(pl.BlockSpec(memory_space=pltpu.HBM), scalar_spec()),
         scratch_shapes=[
             pltpu.VMEM((18, rows + 16, LANES), jnp.float32),
-            pltpu.VMEM((18, rows, LANES), jnp.float32),
-            pltpu.VMEM((18, rows, LANES), jnp.float32),
-            pltpu.VMEM((18, rows, LANES), jnp.float32),
+            pltpu.VMEM((3, 18, rows, LANES), jnp.float32),
+            pltpu.VMEM((54, rows, LANES), jnp.float32),
+            pltpu.SemaphoreType.DMA((5,)),
         ],
         compiler_params=params(),
         name="update",

time: 40.1 us -> 39.3 us (0.980)
  local copies, waits for them, and re-layouts: 1.58 us -> 0.03 us
  Pallas kernels: 7.25 us -> 7.97 us
    unnamed x16 -> x10, local copies, waits for them, and re-layouts: 1.58 us -> 0.03 us
    pallas_call x1, Pallas kernels: 0.36 us -> 1.75 us  [local(): pl.pallas_call(functools.partial(divergence_kernel, plan), out_shape=(sha...]
  transfers between devices with their start and end apart: 4 -> 4, of which waited for: 2 -> 2; matrix products, arithmetic and copies ran while one was open for 0% -> 0% of each run, Pallas kernels for 5% -> 4%
where the time goes in v3:
time: 39.3 us; the launch traced here: 39 us
  blocking collectives  11.7 us (30%)
  starting transfers between devices  10.9 us (28%)
  Pallas kernels  7.97 us (20%)
  waiting for transfers between devices  7.63 us (19%)
  between operations  0.74 us (2%)
    all_to_all x1, blocking collectives, local(): lax.all_to_all(back, 'gx', split_axis=0, concat_axis=0, tiled=True, axis_...  11.7 us
    all_to_all x1, starting transfers between devices, local(): lax.all_to_all(sent, 'gx', split_axis=0, concat_axis=0, tiled=True, axis_...  9.07 us
    all_to_all x1, waiting for transfers between devices, local(): lax.all_to_all(sent, 'gx', split_axis=0, concat_axis=0, tiled=True, axis_...  6.05 us
    pallas_call x1, Pallas kernels, local(): pl.pallas_call(functools.partial(update_kernel, plan, (3, 3)), out_shape=...  3.77 us
    pallas_call x1, Pallas kernels, local(): pl.pallas_call(functools.partial(divergence_kernel, plan), out_shape=(sha...  1.75 us
    ppermute x2, waiting for transfers between devices, local(): got = lax.ppermute(send, 'gx', swap)  1.58 us
    pallas_call x1, Pallas kernels, local(): pl.pallas_call(functools.partial(forward_kernel, plan), out_shape=(shape_...  1.54 us
    ppermute x1, starting transfers between devices, local(): beside = lax.ppermute(ahead, 'gx', halo)  1.28 us
  transfers between devices with their start and end apart: 4, of which 2 were waited for; matrix products, arithmetic and copies ran while one was open for 0% of the time, Pallas kernels for 4%

profile of v3, /device:TPU:0, one launch (start us, length us, event | category | flops | bytes accessed | tf_op | source)
XLA Modules:
  0.0 39.0 jit_solution(13488183720773730547)
XLA Ops:
  0.6 0.0 copy-start.1
  0.6 0.0 copy-start.2
  0.7 0.0 copy-start.4
  0.7 1.8 %divergence.1 = (f32[576,128]{1,0:T(8,128)S(1)}, f32[576,128]{1,0:T(8,128)S(1)}, f32[576,128]{1,0:T(8,128)S(1)}, f32[576,128]{1,0:T(8,128)S(1)}) custom-call(s32[1]{0:T(128)} %bitcast.index_ref, f32[54,72,128]{2,1,0:T(8,128)} %bitcast.3), custom_call_target="tpu_custom_call" | custom-call | tf_op jit(solution)/shard_map/divergence/pallas_call | solution.py:595
  2.4 0.5 %collective-permute-start = (f32[576,128]{1,0:T(8,128)S(1)}, f32[576,128]{1,0:T(8,128)S(1)}, u32[]{:S(2)}, u32[]{:S(2)}) collective-permute-start(f32[576,128]{1,0:T(8,128)S(1)} %get-tuple-element.14), channel_id=1, source_target_pairs={{0,1},{1,0},{2,3},{3,2},{4,5},{5,4},{6,7},{7,6},{8,9},{9,8},{10,11... | collective-permute-start | bytes 884744 | tf_op jit(solution)/shard_map/ppermute | solution.py:609
  3.0 1.3 %collective-permute-start.1 = (f32[576,128]{1,0:T(8,128)S(1)}, f32[576,128]{1,0:T(8,128)S(1)}, u32[]{:S(2)}, u32[]{:S(2)}) collective-permute-start(f32[576,128]{1,0:T(8,128)S(1)} %get-tuple-element.17), channel_id=1, source_target_pairs={{2,1},{4,3},{6,5},{8,7},{10,9},{12,11},{14,13},{15,0},{18,17},{20,... | collective-permute-start | bytes 884744 | tf_op jit(solution)/shard_map/ppermute | solution.py:610
  4.2 0.0 collective-permute-done.got_ref
  4.2 0.0 copy-done.1
  4.3 0.0 copy-done.2
  4.3 0.0 copy-done.4
  4.3 1.5 %forward.1 = (f32[8,72,128]{2,1,0:T(8,128)}, f32[96,512]{1,0:T(8,128)S(1)}, f32[8,128]{1,0:T(8,128)S(1)}) custom-call(s32[1]{0:T(128)} %bitcast.index_ref, f32[576,128]{1,0:T(8,128)S(1)} %get-tuple-element.13.keep_ref, f32[576,128]{1,0:T(8,128)S(1)} %collective-permute-done.got_ref, bf16[2,2,256,256]{3,2,1,0:T(8,128)(2,1)S(1)} %copy-done.4, ...), custom_call_target="tpu_custom_call" | custom-call | tf_op jit(solution)/shard_map/forward/pallas_call | solution.py:611
  5.8 9.1 %all-to-all-start = ((f32[8,72,128]{2,1,0:T(8,128)}), f32[8,72,128]{2,1,0:T(8,128)S(1)}, u32[]{:S(2)}, u32[]{:S(2)}) async-start(f32[8,72,128]{2,1,0:T(8,128)} %get-tuple-element.15), calls=%async_computation | async-start | bytes 589824 | tf_op jit(solution)/shard_map/all_to_all | solution.py:624
  14.9 0.0 collective-permute-done.1.beside_ref
  14.9 0.1 drift.1.drift_ref
  15.0 0.0 copy-start
  15.0 6.0 %all-to-all-done.got_ref = f32[8,72,128]{2,1,0:T(8,128)S(1)} async-done(((f32[8,72,128]{2,1,0:T(8,128)}), f32[8,72,128]{2,1,0:T(8,128)S(1)}, u32[]{:S(2)}, u32[]{:S(2)}) %all-to-all-start) | async-done | bytes 294944 | tf_op jit(solution)/shard_map/all_to_all | solution.py:624
  21.0 0.1 filter.1
  21.1 11.7 %all_to_all.10.got_ref = f32[8,80,128]{2,1,0:T(8,128)S(1)} all-to-all(f32[8,80,128]{2,1,0:T(8,128)S(1)} %filter.1), channel_id=1, replica_groups={{8,10,12,14,0,2,4,6},{9,11,13,15,1,3,5,7},{24,26,28,30,16,18,20,22},{25..., dimensions={0} | all-to-all | bytes 655360 | tf_op jit(solution)/shard_map/all_to_all | solution.py:644
  32.8 0.0 copy-done.3
  32.8 0.7 %backward.1 = (f32[584,128]{1,0:T(8,128)S(1)}, f32[584,128]{1,0:T(8,128)S(1)}) custom-call(s32[1]{0:T(128)} %bitcast.index_ref, f32[8,80,128]{2,1,0:T(8,128)S(1)} %all_to_all.10.got_ref, f32[96,512]{1,0:T(8,128)S(1)} %get-tuple-element.19.odd_ref, bf16[2,2,256,256]{3,2,1,0:T(8,128)(2,1)S(1)} %copy-done.3, bf16[2,192,192]{2,1,0:T(8,128)(2,1)S(1)} %copy-done.2, ...), custom_call_target="tpu_custom_call" | custom-call | tf_op jit(solution)/shard_map/backward/pallas_call | solution.py:647
  33.5 0.1 collective-permute-start.2
  33.6 1.6 %collective-permute-done.2.got_ref = f32[584,128]{1,0:T(8,128)S(1)} collective-permute-done((f32[584,128]{1,0:T(8,128)S(1)}, f32[584,128]{1,0:T(8,128)S(1)}, u32[]{:S(2)}, u32[]{:S(2)}) %collective-permute-start.2) | collective-permute-done | bytes 299040 | tf_op jit(solution)/shard_map/ppermute | solution.py:659
  35.2 0.0 copy-done
  35.2 3.8 %update.1 = (f32[54,72,128]{2,1,0:T(8,128)}, f32[1]{0:T(128)}) custom-call(s32[1]{0:T(128)} %bitcast.index_ref, f32[584,128]{1,0:T(8,128)S(1)} %get-tuple-element.20.keep_ref, f32[584,128]{1,0:T(8,128)S(1)} %collective-permute-done.2.got_ref, f32[54,72,128]{2,1,0:T(8,128)S(1)} %bitcast.4), custom_call_target="tpu_custom_call" | custom-call | tf_op jit(solution)/shard_map/update/pallas_call | solution.py:660
  (1 shorter events, 0.0 us)
Async XLA Ops:
  0.6 3.6 %copy-start.1 = (f32[416,128]{1,0:T(8,128)S(1)}, f32[416,128]{1,0:T(8,128)}, u32[]{:S(2)}) copy-start(f32[416,128]{1,0:T(8,128)} %constant.14.clone.modes_ref) | copy-start | bytes 638980
  0.6 3.6 %copy-start.2 = (bf16[2,192,192]{2,1,0:T(8,128)(2,1)S(1)}, bf16[2,192,192]{2,1,0:T(8,128)(2,1)}, u32[]{:S(2)}) copy-start(bf16[2,192,192]{2,1,0:T(8,128)(2,1)} %constant.13.clone.second_ref) | copy-start | bytes 442372
  0.7 3.6 %copy-start.4 = (bf16[2,2,256,256]{3,2,1,0:T(8,128)(2,1)S(1)}, bf16[2,2,256,256]{3,2,1,0:T(8,128)(2,1)}, u32[]{:S(2)}) copy-start(bf16[2,2,256,256]{3,2,1,0:T(8,128)(2,1)} %constant.12.clone.last_ref) | copy-start | bytes 1572868
  2.4 1.8 %collective-permute-start = (f32[576,128]{1,0:T(8,128)S(1)}, f32[576,128]{1,0:T(8,128)S(1)}, u32[]{:S(2)}, u32[]{:S(2)}) collective-permute-start(f32[576,128]{1,0:T(8,128)S(1)} %get-tuple-element.14), channel_id=1, source_target_pairs={{0,1},{1,0},{2,3},{3,2},{4,5},{5,4},{6,7},{7,6},{8,9},{9,8},{10,11... | collective-permute-start | bytes 884744 | tf_op jit(solution)/shard_map/ppermute | solution.py:609
  3.0 12.0 %collective-permute-start.1 = (f32[576,128]{1,0:T(8,128)S(1)}, f32[576,128]{1,0:T(8,128)S(1)}, u32[]{:S(2)}, u32[]{:S(2)}) collective-permute-start(f32[576,128]{1,0:T(8,128)S(1)} %get-tuple-element.17), channel_id=1, source_target_pairs={{2,1},{4,3},{6,5},{8,7},{10,9},{12,11},{14,13},{15,0},{18,17},{20,... | collective-permute-start | bytes 884744 | tf_op jit(solution)/shard_map/ppermute | solution.py:610
  5.8 15.2 %all-to-all-start = ((f32[8,72,128]{2,1,0:T(8,128)}), f32[8,72,128]{2,1,0:T(8,128)S(1)}, u32[]{:S(2)}, u32[]{:S(2)}) async-start(f32[8,72,128]{2,1,0:T(8,128)} %get-tuple-element.15), calls=%async_computation | async-start | bytes 589824 | tf_op jit(solution)/shard_map/all_to_all | solution.py:624
  14.9 17.9 %copy-start.3 = (bf16[2,2,256,256]{3,2,1,0:T(8,128)(2,1)S(1)}, bf16[2,2,256,256]{3,2,1,0:T(8,128)(2,1)}, u32[]{:S(2)}) copy-start(bf16[2,2,256,256]{3,2,1,0:T(8,128)(2,1)} %constant.15.clone.last_ref) | copy-start | bytes 1572868
  15.0 20.2 %copy-start = (f32[3,2,3,3,1,9216]{5,4,3,2,1,0:T(1,128)S(1)}, f32[3,2,3,3,1,9216]{5,4,3,2,1,0:T(1,128)}, u32[]{:S(2)}) copy-start(f32[3,2,3,3,1,9216]{5,4,3,2,1,0:T(1,128)} %param.5) | copy-start | bytes 5971972
  33.5 1.7 %collective-permute-start.2 = (f32[584,128]{1,0:T(8,128)S(1)}, f32[584,128]{1,0:T(8,128)S(1)}, u32[]{:S(2)}, u32[]{:S(2)}) collective-permute-start(f32[584,128]{1,0:T(8,128)S(1)} %get-tuple-element.21), channel_id=1, source_target_pairs={{0,1},{1,0},{2,3},{3,2},{4,5},{5,4},{6,7},{7,6},{8,9},{9,8},{10,11... | collective-permute-start | bytes 897032 | tf_op jit(solution)/shard_map/ppermute | solution.py:659

commit v4 on v3

--- a/solution.py
+++ b/solution.py
@@ -38,6 +38,7 @@
         self.stride = -(-self.block // 8) * 8
         self.sent = -(-2 * self.block // 8) * 8
         self.place = [(p + self.pairs // 2) % self.pairs for p in range(self.pairs)]
+        self.back_place = [(p + self.pairs // 2 - 1) % self.pairs for p in range(self.pairs)]
         self.returned = -(-(2 * self.block + 8) // 8) * 8
 
 
@@ -170,7 +171,7 @@
 
 
 def divergence_kernel(
-    plan, index_ref, links_ref, keep_ref, send_ref, ahead_ref, base_ref, staged, second, third, semaphores
+    plan, index_ref, links_ref, keep_ref, send_ref, ahead_ref, staged, second, third, semaphores
 ):
     rows, side = plan.rows, plan.side
     copies = link_copies(links_ref, staged, semaphores)
@@ -204,7 +205,6 @@
         place = pl.ds(f * rows, rows)
         total = second[f, middle, :] - direct[f]
         ahead_ref[place, :] = jnp.where(index == plan.count_x - 1, direct[f], total)
-        base_ref[place, :] = jnp.where(index == 0, total, direct[f])
     for f in range(4):
         for part in range(2):
             place = pl.ds((part * 4 + f) * rows, rows)
@@ -319,14 +319,18 @@
     return fields
 
 
-def drift_kernel(plan, index_ref, odd_ref, beside_ref, base_ref, drift_ref):
+def drift_kernel(plan, index_ref, odd_ref, beside_ref, keep_ref, send_ref, drift_ref):
     rows, count_x = plan.rows, plan.count_x
     index = index_ref[0]
     square = jnp.zeros((rows, LANES), jnp.float32)
-    for f in range(8):
-        place = pl.ds(f * rows, rows)
-        value = beside_ref[place, :] + base_ref[place, :]
-        square = square + value * value * drift_weights[f]
+    part = jnp.where(index == 0, 0, 4 * rows)
+    for f in range(4):
+        place = pl.ds(pl.multiple_of(part + f * rows, 8), rows)
+        own, other = keep_ref[place, :], send_ref[place, :]
+        low, high = jnp.where(index % 2 == 0, own, other), jnp.where(index % 2 == 0, other, own)
+        for n, value in ((f, low), (4 + f, high)):
+            total = beside_ref[pl.ds(n * rows, rows), :] + value
+            square = square + total * total * drift_weights[n]
     complete = (index == 0) | ((index % 2 == 1) & (index < count_x - 1))
     drift_ref[...] = odd_ref[...] + jnp.where(complete, sum_tiles(square), 0.0)
 
@@ -388,8 +392,8 @@
                 results[d] = even + wave
                 results[pairs - d] = even - wave
         for p in range(pairs):
-            back_ref[plan.place[p], low, :] = results[p]
-            back_ref[plan.place[p], high, :] = results[(p + 1) % pairs]
+            back_ref[plan.back_place[p], low, :] = results[p]
+            back_ref[plan.back_place[p], high, :] = results[(p + 1) % pairs]
     for p in range(pairs):
         back_ref[p, pl.ds(2 * plan.block, 8), :] = drift
 
@@ -405,10 +409,10 @@
             at = q * tiles + t
             for j in range(pairs):
                 if full:
-                    packed[at, pl.ds(j * full, full), :] = got_ref[plan.place[j], pl.ds(at * full, full), :]
+                    packed[at, pl.ds(j * full, full), :] = got_ref[plan.back_place[j], pl.ds(at * full, full), :]
                 if rest:
                     packed[at, pl.ds(pairs * full + j * rest, rest), :] = got_ref[
-                        plan.place[j], pl.ds(2 * tiles * full + at * rest, rest), :
+                        plan.back_place[j], pl.ds(2 * tiles * full + at * rest, rest), :
                     ]
     lane = lane_of((side, LANES))
     inverse = modes_ref[:side]
@@ -483,7 +487,7 @@
 
 
 def update_kernel(
-    plan, unroll, index_ref, keep_ref, got_ref, links_ref, fixed_ref, drift_ref, here, along, staged, semaphores
+    plan, index_ref, keep_ref, got_ref, links_ref, fixed_ref, drift_ref, here, along, staged, semaphores
 ):
     rows, side = plan.rows, plan.side
     quad = 4 * rows
@@ -502,13 +506,13 @@
                 if q == 0:
                     here[n, pl.ds(begin + lead, 8), :] = value
                 else:
-                    along[0, n, pl.ds(begin, 8), :] = value
+                    along[n, pl.ds(begin, 8), :] = value
         return 0
 
-    lax.fori_loop(0, rows // 8, turn, 0, unroll=unroll[0])
+    lax.fori_loop(0, rows // 8, turn, 0, unroll=3)
 
     def update(d, i):
-        begin = pl.multiple_of(i * 8, 8)
+        begin = i * 8
 
         def matrix(read):
             value = [read(n) for n in range(18)]
@@ -516,7 +520,19 @@
 
         own = matrix(lambda n: here[n, pl.ds(begin + 8, 8), :])
         links = matrix(lambda n: links_ref[d * 18 + n, pl.ds(begin, 8), :])
-        ahead = matrix(lambda n: along[d, n, pl.ds(begin, 8), :])
+        if d == 0:
+            ahead = matrix(lambda n: along[n, pl.ds(begin, 8), :])
+        elif d == 1:
+            ahead = matrix(lambda n: moved(here, n, 8 + begin, 8, side))
+        else:
+            at_end = (last_index(8, side) + begin * LANES) % side == side - 1
+            ahead = matrix(
+                lambda n: jnp.where(
+                    at_end,
+                    moved(here, n, 8 + begin, 8, 1 - side),
+                    moved(here, n, 8 + begin, 8, 1),
+                )
+            )
         for r in range(3):
             line = [
                 add(times(own[r][0], links[0][c]), times(own[r][1], links[1][c]), times(own[r][2], links[2][c]))
@@ -537,26 +553,15 @@
         copy.start()
         copies.append(copy)
 
+    for n in range(18):
+        wrap(here, n, rows)
     for d in (1, 2, 0):
-        if d == 1:
-            for n in range(18):
-                wrap(here, n, rows)
-                along[1, n] = moved(here, n, 8, rows, side)
-        if d == 2:
-            at_end = last_index(rows, side) == side - 1
-            for n in range(18):
-                along[2, n] = jnp.where(
-                    at_end, moved(here, n, 8, rows, 1 - side), moved(here, n, 8, rows, 1)
-                )
         chunks = 1 if d else 3
         for m in range(chunks):
             part = tiles // chunks
 
-            def step(i, _, d=d):
+            for i in range(m * part, (m + 1) * part):
                 update(d, i)
-                return 0
-
-            lax.fori_loop(m * part, (m + 1) * part, step, 0, unroll=unroll[1])
             write(pl.ds(d * 18, 18), pl.ds(m * part * 8, part * 8), len(copies))
     total = keep_ref[pl.ds(2 * quad, 8), :] + got_ref[pl.ds(2 * quad, 8), :]
     drift_ref[0] = jnp.sum(total) * (1.0 / (9.0 * plan.count_x * plan.cells))
@@ -590,13 +595,16 @@
     quads = 8 * rows
     swap = [(i, i ^ 1) for i in range(count_x)]
     halo = [(2 * p, 2 * p - 1) for p in range(1, pairs)] + [(count_x - 1, 0)]
-    same_core = [[c + 2 * p for p in sorted(range(pairs), key=plan.place.__getitem__)] for c in range(2)]
-
-    keep, send, ahead, base = pl.pallas_call(
+    same_core, same_core_back = [
+        [[c + 2 * p for p in sorted(range(pairs), key=place.__getitem__)] for c in range(2)]
+        for place in (plan.place, plan.back_place)
+    ]
+
+    keep, send, ahead = pl.pallas_call(
         functools.partial(divergence_kernel, plan),
-        out_shape=(shape_of(quads, LANES),) * 4,
+        out_shape=(shape_of(quads, LANES),) * 3,
         in_specs=[scalar_spec(), pl.BlockSpec(memory_space=pltpu.HBM)],
-        out_specs=(whole_spec(),) * 4,
+        out_specs=(whole_spec(),) * 3,
         scratch_shapes=[
             pltpu.VMEM((54, rows, LANES), jnp.float32),
             pltpu.VMEM((8, rows + 16, LANES), jnp.float32),
@@ -627,12 +635,12 @@
     drift_part = pl.pallas_call(
         functools.partial(drift_kernel, plan),
         out_shape=shape_of(8, LANES),
-        in_specs=[scalar_spec()] + [whole_spec()] * 3,
+        in_specs=[scalar_spec()] + [whole_spec()] * 4,
         out_specs=whole_spec(),
         compiler_params=params(),
         cost_estimate=pl.CostEstimate(flops=5 * 10**10, bytes_accessed=5 * 10**7, transcendentals=0),
         name="drift",
-    )(index, odd_drift, beside, base)
+    )(index, odd_drift, beside, keep, send)
     back = pl.pallas_call(
         functools.partial(filter_kernel, plan),
         out_shape=shape_of(pairs, plan.returned, LANES),
@@ -642,7 +650,7 @@
         name="filter",
     )(index, arrived, table["modes"], drift_part)
     returned = lax.all_to_all(
-        back, "gx", split_axis=0, concat_axis=0, tiled=True, axis_index_groups=same_core
+        back, "gx", split_axis=0, concat_axis=0, tiled=True, axis_index_groups=same_core_back
     )
     keep, send = pl.pallas_call(
         functools.partial(backward_kernel, plan),
@@ -658,13 +666,13 @@
     )(index, returned, odd_part, table["last_back"], table["second"], table["modes"])
     got = lax.ppermute(send, "gx", swap)
     fixed, drift = pl.pallas_call(
-        functools.partial(update_kernel, plan, (3, 3)),
+        functools.partial(update_kernel, plan),
         out_shape=(shape_of(54, rows, LANES), shape_of(1)),
         in_specs=[scalar_spec()] + [whole_spec()] * 3,
         out_specs=(pl.BlockSpec(memory_space=pltpu.HBM), scalar_spec()),
         scratch_shapes=[
             pltpu.VMEM((18, rows + 16, LANES), jnp.float32),
-            pltpu.VMEM((3, 18, rows, LANES), jnp.float32),
+            pltpu.VMEM((18, rows, LANES), jnp.float32),
             pltpu.VMEM((54, rows, LANES), jnp.float32),
             pltpu.SemaphoreType.DMA((5,)),
         ],

time: 39.3 us -> 38.2 us (0.972)
  blocking collectives: 11.7 us -> 11 us
  Pallas kernels: 7.97 us -> 7.5 us
    all_to_all x1, blocking collectives: 11.7 us -> 11 us  [local(): lax.all_to_all(back, 'gx', split_axis=0, concat_axis=0, tiled=True, axis_...]
    pallas_call x1, Pallas kernels: 3.77 us -> 3.32 us  [local(): pl.pallas_call(functools.partial(update_kernel, plan), out_shape=(shape_o...]
where the time goes in v4:
time: 38.2 us; the launch traced here: 37.9 us
  starting transfers between devices  11 us (29%)
  blocking collectives  11 us (29%)
  waiting for transfers between devices  7.61 us (20%)
  Pallas kernels  7.5 us (20%)
  between operations  0.74 us (2%)
    all_to_all x1, blocking collectives, local(): lax.all_to_all(back, 'gx', split_axis=0, concat_axis=0, tiled=True, axis_...  11 us
    all_to_all x1, starting transfers between devices, local(): lax.all_to_all(sent, 'gx', split_axis=0, concat_axis=0, tiled=True, axis_...  9.09 us
    all_to_all x1, waiting for transfers between devices, local(): lax.all_to_all(sent, 'gx', split_axis=0, concat_axis=0, tiled=True, axis_...  6.03 us
    pallas_call x1, Pallas kernels, local(): pl.pallas_call(functools.partial(update_kernel, plan), out_shape=(shape_o...  3.32 us
    pallas_call x1, Pallas kernels, local(): pl.pallas_call(functools.partial(divergence_kernel, plan), out_shape=(sha...  1.73 us
    ppermute x2, waiting for transfers between devices, local(): got = lax.ppermute(send, 'gx', swap)  1.58 us
    pallas_call x1, Pallas kernels, local(): pl.pallas_call(functools.partial(forward_kernel, plan), out_shape=(shape_...  1.53 us
    ppermute x1, starting transfers between devices, local(): beside = lax.ppermute(ahead, 'gx', halo)  1.28 us
  transfers between devices with their start and end apart: 4, of which 2 were waited for; matrix products, arithmetic and copies ran while one was open for 0% of the time, Pallas kernels for 4%

profile of v4, /device:TPU:0, one launch (start us, length us, event | category | flops | bytes accessed | tf_op | source)
XLA Modules:
  0.0 37.9 jit_solution(16905446453431979022)
XLA Ops:
  0.6 0.0 copy-start.1
  0.6 0.0 copy-start.2
  0.7 0.0 copy-start.4
  0.7 1.7 %divergence.1 = (f32[576,128]{1,0:T(8,128)S(1)}, f32[576,128]{1,0:T(8,128)S(1)}, f32[576,128]{1,0:T(8,128)S(1)}) custom-call(s32[1]{0:T(128)} %bitcast.index_ref, f32[54,72,128]{2,1,0:T(8,128)} %bitcast.3), custom_call_target="tpu_custom_call" | custom-call | tf_op jit(solution)/shard_map/divergence/pallas_call | solution.py:603
  2.4 0.5 %collective-permute-start = (f32[576,128]{1,0:T(8,128)S(1)}, f32[576,128]{1,0:T(8,128)S(1)}, u32[]{:S(2)}, u32[]{:S(2)}) collective-permute-start(f32[576,128]{1,0:T(8,128)S(1)} %get-tuple-element.13.send_ref), channel_id=1, source_target_pairs={{0,1},{1,0},{2,3},{3,2},{4,5},{5,4},{6,7},{7,6},{8,9},{9,8},{10,11... | collective-permute-start | bytes 884744 | tf_op jit(solution)/shard_map/ppermute | solution.py:617
  2.9 1.3 %collective-permute-start.1 = (f32[576,128]{1,0:T(8,128)S(1)}, f32[576,128]{1,0:T(8,128)S(1)}, u32[]{:S(2)}, u32[]{:S(2)}) collective-permute-start(f32[576,128]{1,0:T(8,128)S(1)} %get-tuple-element.16), channel_id=1, source_target_pairs={{2,1},{4,3},{6,5},{8,7},{10,9},{12,11},{14,13},{15,0},{18,17},{20,... | collective-permute-start | bytes 884744 | tf_op jit(solution)/shard_map/ppermute | solution.py:618
  4.2 0.0 collective-permute-done.got_ref
  4.2 0.0 copy-done.1
  4.2 0.0 copy-done.2
  4.2 0.0 copy-done.4
  4.3 1.5 %forward.1 = (f32[8,72,128]{2,1,0:T(8,128)}, f32[96,512]{1,0:T(8,128)S(1)}, f32[8,128]{1,0:T(8,128)S(1)}) custom-call(s32[1]{0:T(128)} %bitcast.index_ref, f32[576,128]{1,0:T(8,128)S(1)} %get-tuple-element.12.keep_ref, f32[576,128]{1,0:T(8,128)S(1)} %collective-permute-done.got_ref, bf16[2,2,256,256]{3,2,1,0:T(8,128)(2,1)S(1)} %copy-done.4, ...), custom_call_target="tpu_custom_call" | custom-call | tf_op jit(solution)/shard_map/forward/pallas_call | solution.py:619
  5.8 9.1 %all-to-all-start = ((f32[8,72,128]{2,1,0:T(8,128)}), f32[8,72,128]{2,1,0:T(8,128)S(1)}, u32[]{:S(2)}, u32[]{:S(2)}) async-start(f32[8,72,128]{2,1,0:T(8,128)} %get-tuple-element.14), calls=%async_computation | async-start | bytes 589824 | tf_op jit(solution)/shard_map/all_to_all | solution.py:632
  14.9 0.0 collective-permute-done.1.beside_ref
  14.9 0.1 drift.1.drift_ref
  15.0 0.0 copy-start
  15.0 6.0 %all-to-all-done.got_ref = f32[8,72,128]{2,1,0:T(8,128)S(1)} async-done(((f32[8,72,128]{2,1,0:T(8,128)}), f32[8,72,128]{2,1,0:T(8,128)S(1)}, u32[]{:S(2)}, u32[]{:S(2)}) %all-to-all-start) | async-done | bytes 294944 | tf_op jit(solution)/shard_map/all_to_all | solution.py:632
  21.0 0.1 filter.1
  21.1 11.0 %all_to_all.10.got_ref = f32[8,80,128]{2,1,0:T(8,128)S(1)} all-to-all(f32[8,80,128]{2,1,0:T(8,128)S(1)} %filter.1), channel_id=1, replica_groups={{10,12,14,0,2,4,6,8},{11,13,15,1,3,5,7,9},{26,28,30,16,18,20,22,24},{27..., dimensions={0} | all-to-all | bytes 655360 | tf_op jit(solution)/shard_map/all_to_all | solution.py:652
  32.1 0.0 copy-done.3
  32.1 0.7 %backward.1 = (f32[584,128]{1,0:T(8,128)S(1)}, f32[584,128]{1,0:T(8,128)S(1)}) custom-call(s32[1]{0:T(128)} %bitcast.index_ref, f32[8,80,128]{2,1,0:T(8,128)S(1)} %all_to_all.10.got_ref, f32[96,512]{1,0:T(8,128)S(1)} %get-tuple-element.17.odd_ref, bf16[2,2,256,256]{3,2,1,0:T(8,128)(2,1)S(1)} %copy-done.3, bf16[2,192,192]{2,1,0:T(8,128)(2,1)S(1)} %copy-done.2, ...), custom_call_target="tpu_custom_call" | custom-call | tf_op jit(solution)/shard_map/backward/pallas_call | solution.py:655
  32.9 0.1 collective-permute-start.2
  33.0 1.6 %collective-permute-done.2.got_ref = f32[584,128]{1,0:T(8,128)S(1)} collective-permute-done((f32[584,128]{1,0:T(8,128)S(1)}, f32[584,128]{1,0:T(8,128)S(1)}, u32[]{:S(2)}, u32[]{:S(2)}) %collective-permute-start.2) | collective-permute-done | bytes 299040 | tf_op jit(solution)/shard_map/ppermute | solution.py:667
  34.5 0.0 copy-done
  34.5 3.3 %update.1 = (f32[54,72,128]{2,1,0:T(8,128)}, f32[1]{0:T(128)}) custom-call(s32[1]{0:T(128)} %bitcast.index_ref, f32[584,128]{1,0:T(8,128)S(1)} %get-tuple-element.18.keep_ref, f32[584,128]{1,0:T(8,128)S(1)} %collective-permute-done.2.got_ref, f32[54,72,128]{2,1,0:T(8,128)S(1)} %bitcast.4), custom_call_target="tpu_custom_call" | custom-call | tf_op jit(solution)/shard_map/update/pallas_call | solution.py:668
  (1 shorter events, 0.0 us)
Async XLA Ops:
  0.6 3.6 %copy-start.1 = (f32[416,128]{1,0:T(8,128)S(1)}, f32[416,128]{1,0:T(8,128)}, u32[]{:S(2)}) copy-start(f32[416,128]{1,0:T(8,128)} %constant.14.clone.modes_ref) | copy-start | bytes 638980
  0.6 3.6 %copy-start.2 = (bf16[2,192,192]{2,1,0:T(8,128)(2,1)S(1)}, bf16[2,192,192]{2,1,0:T(8,128)(2,1)}, u32[]{:S(2)}) copy-start(bf16[2,192,192]{2,1,0:T(8,128)(2,1)} %constant.13.clone.second_ref) | copy-start | bytes 442372
  0.7 3.6 %copy-start.4 = (bf16[2,2,256,256]{3,2,1,0:T(8,128)(2,1)S(1)}, bf16[2,2,256,256]{3,2,1,0:T(8,128)(2,1)}, u32[]{:S(2)}) copy-start(bf16[2,2,256,256]{3,2,1,0:T(8,128)(2,1)} %constant.12.clone.last_ref) | copy-start | bytes 1572868
  2.4 1.8 %collective-permute-start = (f32[576,128]{1,0:T(8,128)S(1)}, f32[576,128]{1,0:T(8,128)S(1)}, u32[]{:S(2)}, u32[]{:S(2)}) collective-permute-start(f32[576,128]{1,0:T(8,128)S(1)} %get-tuple-element.13.send_ref), channel_id=1, source_target_pairs={{0,1},{1,0},{2,3},{3,2},{4,5},{5,4},{6,7},{7,6},{8,9},{9,8},{10,11... | collective-permute-start | bytes 884744 | tf_op jit(solution)/shard_map/ppermute | solution.py:617
  2.9 11.9 %collective-permute-start.1 = (f32[576,128]{1,0:T(8,128)S(1)}, f32[576,128]{1,0:T(8,128)S(1)}, u32[]{:S(2)}, u32[]{:S(2)}) collective-permute-start(f32[576,128]{1,0:T(8,128)S(1)} %get-tuple-element.16), channel_id=1, source_target_pairs={{2,1},{4,3},{6,5},{8,7},{10,9},{12,11},{14,13},{15,0},{18,17},{20,... | collective-permute-start | bytes 884744 | tf_op jit(solution)/shard_map/ppermute | solution.py:618
  5.8 15.2 %all-to-all-start = ((f32[8,72,128]{2,1,0:T(8,128)}), f32[8,72,128]{2,1,0:T(8,128)S(1)}, u32[]{:S(2)}, u32[]{:S(2)}) async-start(f32[8,72,128]{2,1,0:T(8,128)} %get-tuple-element.14), calls=%async_computation | async-start | bytes 589824 | tf_op jit(solution)/shard_map/all_to_all | solution.py:632
  14.9 17.3 %copy-start.3 = (bf16[2,2,256,256]{3,2,1,0:T(8,128)(2,1)S(1)}, bf16[2,2,256,256]{3,2,1,0:T(8,128)(2,1)}, u32[]{:S(2)}) copy-start(bf16[2,2,256,256]{3,2,1,0:T(8,128)(2,1)} %constant.15.clone.last_ref) | copy-start | bytes 1572868
  15.0 19.6 %copy-start = (f32[3,2,3,3,1,9216]{5,4,3,2,1,0:T(1,128)S(1)}, f32[3,2,3,3,1,9216]{5,4,3,2,1,0:T(1,128)}, u32[]{:S(2)}) copy-start(f32[3,2,3,3,1,9216]{5,4,3,2,1,0:T(1,128)} %param.5) | copy-start | bytes 5971972
  32.9 1.7 %collective-permute-start.2 = (f32[584,128]{1,0:T(8,128)S(1)}, f32[584,128]{1,0:T(8,128)S(1)}, u32[]{:S(2)}, u32[]{:S(2)}) collective-permute-start(f32[584,128]{1,0:T(8,128)S(1)} %get-tuple-element.19), channel_id=1, source_target_pairs={{0,1},{1,0},{2,3},{3,2},{4,5},{5,4},{6,7},{7,6},{8,9},{9,8},{10,11... | collective-permute-start | bytes 897032 | tf_op jit(solution)/shard_map/ppermute | solution.py:667

commit v5 on v4

--- a/solution.py
+++ b/solution.py
@@ -37,8 +37,11 @@
         self.block = self.tiles * self.share
         self.stride = -(-self.block // 8) * 8
         self.sent = -(-2 * self.block // 8) * 8
-        self.place = [(p + self.pairs // 2) % self.pairs for p in range(self.pairs)]
-        self.back_place = [(p + self.pairs // 2 - 1) % self.pairs for p in range(self.pairs)]
+        half = self.pairs // 2
+        there = [(p + half) % self.pairs for p in range(self.pairs)]
+        back = [p ^ (1 - half % 2) for p in range(half, self.pairs)] + list(range(half))[::-1]
+        self.place = [there.index(p) for p in range(self.pairs)]
+        self.back_place = [back.index(p) for p in range(self.pairs)]
         self.returned = -(-(2 * self.block + 8) // 8) * 8
 
 
@@ -109,7 +112,9 @@
 
 def product(left, right):
     dot = functools.partial(jnp.dot, preferred_element_type=jnp.float32)
-    return dot(left[0], right[0]) + (dot(left[0], right[1]) + dot(left[1], right[0]))
+    both = dot(jnp.concatenate(left, axis=0), right[0])
+    size = left[0].shape[0]
+    return both[:size] + (both[size:] + dot(left[0], right[1]))
 
 
 def stacked(table, value):
@@ -216,26 +221,31 @@
 
 
 def forward_kernel(
-    plan, index_ref, keep_ref, got_ref, last_ref, second_ref, modes_ref, sent_ref, odd_ref, drift_ref, dense
+    plan, index_ref, keep_ref, got_ref, last_ref, second_ref, modes_ref, sent_ref, odd_ref, drift_ref
 ):
     rows, groups, folds, side = plan.rows, plan.groups, plan.folds, plan.side
     odd = index_ref[0] % 2
     quad = 4 * rows
-    square = jnp.zeros((rows, LANES), jnp.float32)
-    for f in range(4):
-        own_d, own_a = keep_ref[pl.ds(f * rows, rows), :], keep_ref[pl.ds(quad + f * rows, rows), :]
-        got_d, got_a = got_ref[pl.ds(f * rows, rows), :], got_ref[pl.ds(quad + f * rows, rows), :]
+    count = 4 * groups
+    square = jnp.zeros((8, LANES), jnp.float32)
+    wide = []
+    for s in range(plan.wide):
+        own_d, own_a, got_d, got_a = [
+            ref[pl.ds(begin + s, count, stride=plan.wide), :]
+            for ref in (keep_ref, got_ref)
+            for begin in (0, quad)
+        ]
         even_d, odd_d = jnp.where(odd == 0, own_d, got_d), jnp.where(odd == 0, got_d, own_d)
         even_a, odd_a = jnp.where(odd == 0, own_a, got_a), jnp.where(odd == 0, got_a, own_a)
         whole = odd_d + even_a
-        for q, value in enumerate((even_d, whole, odd_a)):
-            dense[pl.ds((q * 4 + f) * rows, rows), :] = value
-        square = square + whole * whole * jnp.where(odd == 0, drift_weights[f], drift_weights[4 + f])
-    drift_ref[...] = sum_tiles(square)
-    count = 12 * groups
-    wide = jnp.concatenate(
-        [dense[pl.ds(s, count, stride=plan.wide), :] for s in range(plan.wide)], axis=1
-    )
+        for f in range(4):
+            part = whole[f * groups : (f + 1) * groups]
+            square = square + sum_tiles(part * part) * jnp.where(
+                odd == 0, drift_weights[f], drift_weights[4 + f]
+            )
+        wide.append(jnp.concatenate([even_d, whole, odd_a], axis=0))
+    drift_ref[...] = square
+    wide = jnp.concatenate(wide, axis=1)
     high, low = halve(wide)
     waves = jnp.concatenate(
         [
@@ -399,7 +409,7 @@
 
 
 def backward_kernel(
-    plan, index_ref, got_ref, odd_ref, last_ref, second_ref, modes_ref, keep_ref, send_ref, packed, dense
+    plan, index_ref, got_ref, odd_ref, last_ref, second_ref, modes_ref, keep_ref, send_ref, packed
 ):
     rows, groups, folds, side = plan.rows, plan.groups, plan.folds, plan.side
     full, rest, pairs, tiles = plan.full, plan.rest, plan.pairs, plan.tiles
@@ -438,15 +448,14 @@
         for s in range(begin // LANES, end // LANES):
             tile = part[:, s * LANES - begin : (s + 1) * LANES - begin]
             wide[s] = tile if wide[s] is None else wide[s] + tile
-    count = 12 * groups
+    quad, count = 4 * rows, 4 * groups
     for s in range(plan.wide):
-        dense[pl.ds(s, count, stride=plan.wide), :] = wide[s]
-    quad = 4 * rows
-    low, middle, high = [dense[pl.ds(q * quad, quad), :] for q in range(3)]
-    keep_ref[pl.ds(0, quad), :] = jnp.where(odd == 0, low, middle)
-    keep_ref[pl.ds(quad, quad), :] = jnp.where(odd == 0, middle, high)
-    send_ref[pl.ds(0, quad), :] = jnp.where(odd == 0, middle, low)
-    send_ref[pl.ds(quad, quad), :] = jnp.where(odd == 0, high, middle)
+        low, middle, high = [wide[s][q * count : (q + 1) * count] for q in range(3)]
+        here, ahead = pl.ds(s, count, stride=plan.wide), pl.ds(quad + s, count, stride=plan.wide)
+        keep_ref[here, :] = jnp.where(odd == 0, low, middle)
+        keep_ref[ahead, :] = jnp.where(odd == 0, middle, high)
+        send_ref[here, :] = jnp.where(odd == 0, middle, low)
+        send_ref[ahead, :] = jnp.where(odd == 0, high, middle)
     drift = got_ref[0, pl.ds(2 * plan.block, 8), :]
     for j in range(1, pairs):
         drift = drift + got_ref[j, pl.ds(2 * plan.block, 8), :]
@@ -625,7 +634,6 @@
         ),
         in_specs=[scalar_spec()] + [whole_spec()] * 5,
         out_specs=(whole_spec(),) * 3,
-        scratch_shapes=[pltpu.VMEM((12 * rows, LANES), jnp.float32)],
         compiler_params=params(),
         name="forward",
     )(index, keep, got, table["last"], table["second"], table["modes"])
@@ -659,7 +667,6 @@
         out_specs=(whole_spec(), whole_spec()),
         scratch_shapes=[
             pltpu.VMEM((2 * plan.tiles, SIDE, LANES), jnp.float32),
-            pltpu.VMEM((12 * rows, LANES), jnp.float32),
         ],
         compiler_params=params(),
         name="backward",

time: 38.2 us -> 37.9 us (level)
  no operation moved by 1% of the time
where the time goes in v5:
time: 37.9 us; the launch traced here: 37.6 us
  starting transfers between devices  10.9 us (29%)
  blocking collectives  10.9 us (29%)
  waiting for transfers between devices  7.64 us (20%)
  Pallas kernels  7.41 us (20%)
  between operations  0.74 us (2%)
    all_to_all x1, blocking collectives, local(): lax.all_to_all(back, 'gx', split_axis=0, concat_axis=0, tiled=True, axis_...  10.9 us
    all_to_all x1, starting transfers between devices, local(): lax.all_to_all(sent, 'gx', split_axis=0, concat_axis=0, tiled=True, axis_...  9.08 us
    all_to_all x1, waiting for transfers between devices, local(): lax.all_to_all(sent, 'gx', split_axis=0, concat_axis=0, tiled=True, axis_...  6.06 us
    pallas_call x1, Pallas kernels, local(): pl.pallas_call(functools.partial(update_kernel, plan), out_shape=(shape_o...  3.32 us
    pallas_call x1, Pallas kernels, local(): pl.pallas_call(functools.partial(divergence_kernel, plan), out_shape=(sha...  1.73 us
    ppermute x2, waiting for transfers between devices, local(): got = lax.ppermute(send, 'gx', swap)  1.58 us
    pallas_call x1, Pallas kernels, local(): pl.pallas_call(functools.partial(forward_kernel, plan), out_shape=(shape_...  1.47 us
    ppermute x1, starting transfers between devices, local(): beside = lax.ppermute(ahead, 'gx', halo)  1.28 us
  transfers between devices with their start and end apart: 4, of which 2 were waited for; matrix products, arithmetic and copies ran while one was open for 0% of the time, Pallas kernels for 4%

profile of v5, /device:TPU:0, one launch (start us, length us, event | category | flops | bytes accessed | tf_op | source)
XLA Modules:
  0.0 37.6 jit_solution(1932223102816884155)
XLA Ops:
  0.6 0.0 copy-start.1
  0.6 0.0 copy-start.2
  0.7 0.0 copy-start.4
  0.7 1.7 %divergence.1 = (f32[576,128]{1,0:T(8,128)S(1)}, f32[576,128]{1,0:T(8,128)S(1)}, f32[576,128]{1,0:T(8,128)S(1)}) custom-call(s32[1]{0:T(128)} %bitcast.index_ref, f32[54,72,128]{2,1,0:T(8,128)} %bitcast.3), custom_call_target="tpu_custom_call" | custom-call | tf_op jit(solution)/shard_map/divergence/pallas_call | solution.py:612
  2.4 0.5 %collective-permute-start = (f32[576,128]{1,0:T(8,128)S(1)}, f32[576,128]{1,0:T(8,128)S(1)}, u32[]{:S(2)}, u32[]{:S(2)}) collective-permute-start(f32[576,128]{1,0:T(8,128)S(1)} %get-tuple-element.13.send_ref), channel_id=1, source_target_pairs={{0,1},{1,0},{2,3},{3,2},{4,5},{5,4},{6,7},{7,6},{8,9},{9,8},{10,11... | collective-permute-start | bytes 884744 | tf_op jit(solution)/shard_map/ppermute | solution.py:626
  2.9 1.3 %collective-permute-start.1 = (f32[576,128]{1,0:T(8,128)S(1)}, f32[576,128]{1,0:T(8,128)S(1)}, u32[]{:S(2)}, u32[]{:S(2)}) collective-permute-start(f32[576,128]{1,0:T(8,128)S(1)} %get-tuple-element.16), channel_id=1, source_target_pairs={{2,1},{4,3},{6,5},{8,7},{10,9},{12,11},{14,13},{15,0},{18,17},{20,... | collective-permute-start | bytes 884744 | tf_op jit(solution)/shard_map/ppermute | solution.py:627
  4.2 0.0 collective-permute-done.got_ref
  4.2 0.0 copy-done.1
  4.2 0.0 copy-done.2
  4.2 0.0 copy-done.4
  4.3 1.5 %forward.1 = (f32[8,72,128]{2,1,0:T(8,128)}, f32[96,512]{1,0:T(8,128)S(1)}, f32[8,128]{1,0:T(8,128)S(1)}) custom-call(s32[1]{0:T(128)} %bitcast.index_ref, f32[576,128]{1,0:T(8,128)S(1)} %get-tuple-element.12.keep_ref, f32[576,128]{1,0:T(8,128)S(1)} %collective-permute-done.got_ref, bf16[2,2,256,256]{3,2,1,0:T(8,128)(2,1)S(1)} %copy-done.4, ...), custom_call_target="tpu_custom_call" | custom-call | tf_op jit(solution)/shard_map/forward/pallas_call | solution.py:628
  5.7 9.1 %all-to-all-start = ((f32[8,72,128]{2,1,0:T(8,128)}), f32[8,72,128]{2,1,0:T(8,128)S(1)}, u32[]{:S(2)}, u32[]{:S(2)}) async-start(f32[8,72,128]{2,1,0:T(8,128)} %get-tuple-element.14), calls=%async_computation | async-start | bytes 589824 | tf_op jit(solution)/shard_map/all_to_all | solution.py:640
  14.8 0.0 collective-permute-done.1.beside_ref
  14.8 0.1 drift.1.drift_ref
  14.9 0.0 copy-start
  14.9 6.1 %all-to-all-done.got_ref = f32[8,72,128]{2,1,0:T(8,128)S(1)} async-done(((f32[8,72,128]{2,1,0:T(8,128)}), f32[8,72,128]{2,1,0:T(8,128)S(1)}, u32[]{:S(2)}, u32[]{:S(2)}) %all-to-all-start) | async-done | bytes 294944 | tf_op jit(solution)/shard_map/all_to_all | solution.py:640
  21.0 0.1 filter.1
  21.1 10.9 %all_to_all.10.got_ref = f32[8,80,128]{2,1,0:T(8,128)S(1)} all-to-all(f32[8,80,128]{2,1,0:T(8,128)S(1)} %filter.1), channel_id=1, replica_groups={{10,8,14,12,6,4,2,0},{11,9,15,13,7,5,3,1},{26,24,30,28,22,20,18,16},{27..., dimensions={0} | all-to-all | bytes 655360 | tf_op jit(solution)/shard_map/all_to_all | solution.py:660
  31.9 0.0 copy-done.3
  31.9 0.7 %backward.1 = (f32[584,128]{1,0:T(8,128)S(1)}, f32[584,128]{1,0:T(8,128)S(1)}) custom-call(s32[1]{0:T(128)} %bitcast.index_ref, f32[8,80,128]{2,1,0:T(8,128)S(1)} %all_to_all.10.got_ref, f32[96,512]{1,0:T(8,128)S(1)} %get-tuple-element.17.odd_ref, bf16[2,2,256,256]{3,2,1,0:T(8,128)(2,1)S(1)} %copy-done.3, bf16[2,192,192]{2,1,0:T(8,128)(2,1)S(1)} %copy-done.2, ...), custom_call_target="tpu_custom_call" | custom-call | tf_op jit(solution)/shard_map/backward/pallas_call | solution.py:663
  32.7 0.1 collective-permute-start.2
  32.7 1.6 %collective-permute-done.2.got_ref = f32[584,128]{1,0:T(8,128)S(1)} collective-permute-done((f32[584,128]{1,0:T(8,128)S(1)}, f32[584,128]{1,0:T(8,128)S(1)}, u32[]{:S(2)}, u32[]{:S(2)}) %collective-permute-start.2) | collective-permute-done | bytes 299040 | tf_op jit(solution)/shard_map/ppermute | solution.py:674
  34.3 0.0 copy-done
  34.3 3.3 %update.1 = (f32[54,72,128]{2,1,0:T(8,128)}, f32[1]{0:T(128)}) custom-call(s32[1]{0:T(128)} %bitcast.index_ref, f32[584,128]{1,0:T(8,128)S(1)} %get-tuple-element.18.keep_ref, f32[584,128]{1,0:T(8,128)S(1)} %collective-permute-done.2.got_ref, f32[54,72,128]{2,1,0:T(8,128)S(1)} %bitcast.4), custom_call_target="tpu_custom_call" | custom-call | tf_op jit(solution)/shard_map/update/pallas_call | solution.py:675
  (1 shorter events, 0.0 us)
Async XLA Ops:
  0.6 3.6 %copy-start.1 = (f32[416,128]{1,0:T(8,128)S(1)}, f32[416,128]{1,0:T(8,128)}, u32[]{:S(2)}) copy-start(f32[416,128]{1,0:T(8,128)} %constant.14.clone.modes_ref) | copy-start | bytes 638980
  0.6 3.6 %copy-start.2 = (bf16[2,192,192]{2,1,0:T(8,128)(2,1)S(1)}, bf16[2,192,192]{2,1,0:T(8,128)(2,1)}, u32[]{:S(2)}) copy-start(bf16[2,192,192]{2,1,0:T(8,128)(2,1)} %constant.13.clone.second_ref) | copy-start | bytes 442372
  0.7 3.6 %copy-start.4 = (bf16[2,2,256,256]{3,2,1,0:T(8,128)(2,1)S(1)}, bf16[2,2,256,256]{3,2,1,0:T(8,128)(2,1)}, u32[]{:S(2)}) copy-start(bf16[2,2,256,256]{3,2,1,0:T(8,128)(2,1)} %constant.12.clone.last_ref) | copy-start | bytes 1572868
  2.4 1.8 %collective-permute-start = (f32[576,128]{1,0:T(8,128)S(1)}, f32[576,128]{1,0:T(8,128)S(1)}, u32[]{:S(2)}, u32[]{:S(2)}) collective-permute-start(f32[576,128]{1,0:T(8,128)S(1)} %get-tuple-element.13.send_ref), channel_id=1, source_target_pairs={{0,1},{1,0},{2,3},{3,2},{4,5},{5,4},{6,7},{7,6},{8,9},{9,8},{10,11... | collective-permute-start | bytes 884744 | tf_op jit(solution)/shard_map/ppermute | solution.py:626
  2.9 11.9 %collective-permute-start.1 = (f32[576,128]{1,0:T(8,128)S(1)}, f32[576,128]{1,0:T(8,128)S(1)}, u32[]{:S(2)}, u32[]{:S(2)}) collective-permute-start(f32[576,128]{1,0:T(8,128)S(1)} %get-tuple-element.16), channel_id=1, source_target_pairs={{2,1},{4,3},{6,5},{8,7},{10,9},{12,11},{14,13},{15,0},{18,17},{20,... | collective-permute-start | bytes 884744 | tf_op jit(solution)/shard_map/ppermute | solution.py:627
  5.7 15.2 %all-to-all-start = ((f32[8,72,128]{2,1,0:T(8,128)}), f32[8,72,128]{2,1,0:T(8,128)S(1)}, u32[]{:S(2)}, u32[]{:S(2)}) async-start(f32[8,72,128]{2,1,0:T(8,128)} %get-tuple-element.14), calls=%async_computation | async-start | bytes 589824 | tf_op jit(solution)/shard_map/all_to_all | solution.py:640
  14.8 17.1 %copy-start.3 = (bf16[2,2,256,256]{3,2,1,0:T(8,128)(2,1)S(1)}, bf16[2,2,256,256]{3,2,1,0:T(8,128)(2,1)}, u32[]{:S(2)}) copy-start(bf16[2,2,256,256]{3,2,1,0:T(8,128)(2,1)} %constant.15.clone.last_ref) | copy-start | bytes 1572868
  14.9 19.4 %copy-start = (f32[3,2,3,3,1,9216]{5,4,3,2,1,0:T(1,128)S(1)}, f32[3,2,3,3,1,9216]{5,4,3,2,1,0:T(1,128)}, u32[]{:S(2)}) copy-start(f32[3,2,3,3,1,9216]{5,4,3,2,1,0:T(1,128)} %param.5) | copy-start | bytes 5971972
  32.7 1.7 %collective-permute-start.2 = (f32[584,128]{1,0:T(8,128)S(1)}, f32[584,128]{1,0:T(8,128)S(1)}, u32[]{:S(2)}, u32[]{:S(2)}) collective-permute-start(f32[584,128]{1,0:T(8,128)S(1)} %get-tuple-element.19), channel_id=1, source_target_pairs={{0,1},{1,0},{2,3},{3,2},{4,5},{5,4},{6,7},{7,6},{8,9},{9,8},{10,11... | collective-permute-start | bytes 897032 | tf_op jit(solution)/shard_map/ppermute | solution.py:674

commit v6 on v5

--- a/solution.py
+++ b/solution.py
@@ -35,7 +35,6 @@
         self.rest = self.share - self.full
         self.tiles = 4 * side // LANES
         self.block = self.tiles * self.share
-        self.stride = -(-self.block // 8) * 8
         self.sent = -(-2 * self.block // 8) * 8
         half = self.pairs // 2
         there = [(p + half) % self.pairs for p in range(self.pairs)]
@@ -88,19 +87,11 @@
     value = eigen(side)
     inverse_side = np.zeros((side, LANES))
     inverse_side[:, :side] = 1.0 / (2.0 + value[order][:, None] + value[None, :])
-    lane = np.arange(plan.tiles * LANES).reshape(plan.tiles, 1, LANES)
-    owner = np.zeros((plan.pairs, plan.stride, LANES))
-    for j in range(plan.pairs):
-        parts = []
-        for start, size in ((0, plan.full), (plan.full, plan.rest)):
-            mode = plan.share * j + start + np.arange(size).reshape(1, size, 1)
-            parts.append((value[mode] + value[lane % side]).reshape(plan.tiles * size, LANES))
-        owner[j, : plan.block] = np.concatenate(parts)
     return {
         "last": np.stack([split_table(last[a:b, c:d]) for a, b, c, d in bands(plan)]),
         "last_back": np.stack([split_table(last[a:b, c:d].T) for a, b, c, d in bands(plan)]),
         "second": np.stack([stack_table(second), stack_table(second.T)]),
-        "modes": np.concatenate([inverse_side, owner.reshape(-1, LANES)]).astype(np.float32),
+        "modes": inverse_side.astype(np.float32),
     }
 
 
@@ -329,8 +320,27 @@
     return fields
 
 
-def drift_kernel(plan, index_ref, odd_ref, beside_ref, keep_ref, send_ref, drift_ref):
+def eigenvalues(plan, first, size):
+    side = plan.side
+    row = lax.broadcasted_iota(jnp.int32, (plan.tiles * size, LANES), 0)
+    tile = row // size
+    total = 0.0
+    for mode in (first + row - tile * size, (tile * LANES + lane_of(row.shape)) % side):
+        near = jnp.minimum(mode, side - mode).astype(jnp.float32)
+        sine = jnp.sin(near * (math.pi / side))
+        total = total + 4.0 * sine * sine
+    return total
+
+
+def drift_kernel(
+    plan, index_ref, odd_ref, beside_ref, keep_ref, send_ref, links_ref, drift_ref, turns_ref, own_ref, loaded, arrivals
+):
     rows, count_x = plan.rows, plan.count_x
+    loads = []
+    for d in range(3):
+        place = pl.ds(d * 18, 18)
+        loads.append(pltpu.make_async_copy(links_ref.at[place], loaded.at[place], arrivals.at[d]))
+        loads[d].start()
     index = index_ref[0]
     square = jnp.zeros((rows, LANES), jnp.float32)
     part = jnp.where(index == 0, 0, 4 * rows)
@@ -343,9 +353,20 @@
             square = square + total * total * drift_weights[n]
     complete = (index == 0) | ((index % 2 == 1) & (index < count_x - 1))
     drift_ref[...] = odd_ref[...] + jnp.where(complete, sum_tiles(square), 0.0)
-
-
-def filter_kernel(plan, index_ref, got_ref, modes_ref, drift_ref, back_ref):
+    for start, size in ((0, plan.full), (plan.full, plan.rest)):
+        if size:
+            own_ref[pl.ds(plan.tiles * start, plan.tiles * size), :] = eigenvalues(
+                plan, index // 2 * plan.share + start, size
+            )
+    for d in range(3):
+        loads[d].wait()
+        link = [[tuple(loaded[((d * 2 + part) * 3 + r) * 3 + c] for part in range(2)) for c in range(3)] for r in range(3)]
+        value = add(*[times(link[0][c], cross(link[1], link[2], c)) for c in range(3)])
+        for part in range(2):
+            turns_ref[d * 2 + part] = value[part]
+
+
+def filter_kernel(plan, index_ref, got_ref, drift_ref, own_ref, back_ref):
     pairs, tiles, count_x = plan.pairs, plan.tiles, plan.count_x
     half = pairs // 2
     drift = drift_ref[...]
@@ -353,8 +374,7 @@
         if not size:
             continue
         length = tiles * size
-        own = pl.multiple_of(plan.side + index_ref[0] // 2 * plan.stride, 8)
-        value = modes_ref[pl.ds(own, plan.stride), :][part * tiles * plan.full :][:length]
+        value = own_ref[pl.ds(part * tiles * plan.full, length), :]
         low, high = pl.ds(first, length), pl.ds(first + length, length)
         inside = value > 0
         below = [got_ref[plan.place[p], low, :] for p in range(pairs)]
@@ -492,11 +512,12 @@
     for (i, j), up, off in (((0, 1), a01, u), ((0, 2), a02, v), ((1, 2), a12, w)):
         entries[i][j] = times((up[0] + off[0], up[1] + off[1]), factor)
         entries[j][i] = times((up[0] - off[0], off[1] - up[1]), factor)
-    return [entries[i][j][part] for part in range(2) for i in range(3) for j in range(3)]
+    whole = (0.5 * (real * factor[0] - turn * factor[1]), real * factor[1])
+    return [entries[i][j][part] for part in range(2) for i in range(3) for j in range(3)] + list(whole)
 
 
 def update_kernel(
-    plan, index_ref, keep_ref, got_ref, links_ref, fixed_ref, drift_ref, here, along, staged, semaphores
+    plan, index_ref, keep_ref, got_ref, links_ref, turns_ref, fixed_ref, drift_ref, here, along, staged, semaphores
 ):
     rows, side = plan.rows, plan.side
     quad = 4 * rows
@@ -527,30 +548,46 @@
             value = [read(n) for n in range(18)]
             return [[(value[3 * r + c], value[9 + 3 * r + c]) for c in range(3)] for r in range(3)]
 
-        own = matrix(lambda n: here[n, pl.ds(begin + 8, 8), :])
-        links = matrix(lambda n: links_ref[d * 18 + n, pl.ds(begin, 8), :])
         if d == 0:
-            ahead = matrix(lambda n: along[n, pl.ds(begin, 8), :])
+
+            def shifted(n):
+                return along[n, pl.ds(begin, 8), :]
+
         elif d == 1:
-            ahead = matrix(lambda n: moved(here, n, 8 + begin, 8, side))
+
+            def shifted(n):
+                return moved(here, n, 8 + begin, 8, side)
+
         else:
             at_end = (last_index(8, side) + begin * LANES) % side == side - 1
-            ahead = matrix(
-                lambda n: jnp.where(
+
+            def shifted(n):
+                return jnp.where(
                     at_end,
                     moved(here, n, 8 + begin, 8, 1 - side),
                     moved(here, n, 8 + begin, 8, 1),
                 )
+
+        def own(r, c):
+            return tuple(here[9 * part + 3 * r + c, pl.ds(begin + 8, 8), :] for part in range(2))
+
+        links = matrix(lambda n: links_ref[d * 18 + n, pl.ds(begin, 8), :])
+        ahead = matrix(shifted)
+        moved_rows = []
+        for r in range(2):
+            left = [own(r, k) for k in range(3)]
+            line = [add(*[times(left[k], links[k][c]) for k in range(3)]) for c in range(3)]
+            moved_rows.append(
+                [add(*[times_conj(line[k], ahead[c][k]) for k in range(3)]) for c in range(3)]
             )
+        whole = tuple(turns_ref[d * 2 + part, pl.ds(begin, 8), :] for part in range(2))
+        whole = times(whole, tuple(here[18 + part, pl.ds(begin + 8, 8), :] for part in range(2)))
+        whole = times_conj(whole, (shifted(18), shifted(19)))
+        moved_rows.append([times_conj(whole, cross(*moved_rows, c)) for c in range(3)])
         for r in range(3):
-            line = [
-                add(times(own[r][0], links[0][c]), times(own[r][1], links[1][c]), times(own[r][2], links[2][c]))
-                for c in range(3)
-            ]
             for c in range(3):
-                value = add(*[times_conj(line[k], ahead[c][k]) for k in range(3)])
                 for part in range(2):
-                    staged[d * 18 + part * 9 + r * 3 + c, pl.ds(begin, 8), :] = value[part]
+                    staged[d * 18 + part * 9 + r * 3 + c, pl.ds(begin, 8), :] = moved_rows[r][c][part]
 
     tiles = rows // 8
     copies = []
@@ -562,7 +599,7 @@
         copy.start()
         copies.append(copy)
 
-    for n in range(18):
+    for n in range(20):
         wrap(here, n, rows)
     for d in (1, 2, 0):
         chunks = 1 if d else 3
@@ -578,6 +615,12 @@
         copy.wait()
 
 
+def cross(first, second, c):
+    one = times(first[(c + 1) % 3], second[(c + 2) % 3])
+    two = times(first[(c + 2) % 3], second[(c + 1) % 3])
+    return (one[0] - two[0], one[1] - two[1])
+
+
 def add(first, second, third):
     return (first[0] + second[0] + third[0], first[1] + second[1] + third[1])
 
@@ -601,6 +644,7 @@
     table = tables(plan)
     index = lax.axis_index("gx").astype(jnp.int32).reshape(1)
     links = gauge_links.reshape(54, rows, LANES)
+    held = pltpu.with_memory_space_constraint(links, pltpu.HBM)
     quads = 8 * rows
     swap = [(i, i ^ 1) for i in range(count_x)]
     halo = [(2 * p, 2 * p - 1) for p in range(1, pairs)] + [(count_x - 1, 0)]
@@ -622,7 +666,7 @@
         ],
         compiler_params=params(),
         name="divergence",
-    )(index, pltpu.with_memory_space_constraint(links, pltpu.HBM))
+    )(index, held)
     got = lax.ppermute(send, "gx", swap)
     beside = lax.ppermute(ahead, "gx", halo)
     sent, odd_part, odd_drift = pl.pallas_call(
@@ -640,15 +684,16 @@
     arrived = lax.all_to_all(
         sent, "gx", split_axis=0, concat_axis=0, tiled=True, axis_index_groups=same_core
     )
-    drift_part = pl.pallas_call(
+    drift_part, turns, own_modes = pl.pallas_call(
         functools.partial(drift_kernel, plan),
-        out_shape=shape_of(8, LANES),
-        in_specs=[scalar_spec()] + [whole_spec()] * 4,
-        out_specs=whole_spec(),
+        out_shape=(shape_of(8, LANES), shape_of(6, rows, LANES), shape_of(plan.block, LANES)),
+        in_specs=[scalar_spec()] + [whole_spec()] * 4 + [pl.BlockSpec(memory_space=pltpu.HBM)],
+        out_specs=(whole_spec(),) * 3,
+        scratch_shapes=[pltpu.VMEM((54, rows, LANES), jnp.float32), pltpu.SemaphoreType.DMA((3,))],
         compiler_params=params(),
         cost_estimate=pl.CostEstimate(flops=5 * 10**10, bytes_accessed=5 * 10**7, transcendentals=0),
         name="drift",
-    )(index, odd_drift, beside, keep, send)
+    )(index, odd_drift, beside, keep, send, held)
     back = pl.pallas_call(
         functools.partial(filter_kernel, plan),
         out_shape=shape_of(pairs, plan.returned, LANES),
@@ -656,7 +701,7 @@
         out_specs=whole_spec(),
         compiler_params=params(),
         name="filter",
-    )(index, arrived, table["modes"], drift_part)
+    )(index, arrived, drift_part, own_modes)
     returned = lax.all_to_all(
         back, "gx", split_axis=0, concat_axis=0, tiled=True, axis_index_groups=same_core_back
     )
@@ -675,17 +720,17 @@
     fixed, drift = pl.pallas_call(
         functools.partial(update_kernel, plan),
         out_shape=(shape_of(54, rows, LANES), shape_of(1)),
-        in_specs=[scalar_spec()] + [whole_spec()] * 3,
+        in_specs=[scalar_spec()] + [whole_spec()] * 4,
         out_specs=(pl.BlockSpec(memory_space=pltpu.HBM), scalar_spec()),
         scratch_shapes=[
-            pltpu.VMEM((18, rows + 16, LANES), jnp.float32),
-            pltpu.VMEM((18, rows, LANES), jnp.float32),
+            pltpu.VMEM((20, rows + 16, LANES), jnp.float32),
+            pltpu.VMEM((20, rows, LANES), jnp.float32),
             pltpu.VMEM((54, rows, LANES), jnp.float32),
             pltpu.SemaphoreType.DMA((5,)),
         ],
         compiler_params=params(),
         name="update",
-    )(index, keep, got, links)
+    )(index, keep, got, links, turns)
     return fixed.reshape(gauge_links.shape), drift
 
 

time: 37.9 us -> 37.8 us (level)
  waiting for transfers between devices: 7.64 us -> 6.04 us
  Pallas kernels: 7.41 us -> 8.79 us
    all_to_all x1, waiting for transfers between devices: 6.06 us -> 4.46 us  [local(): lax.all_to_all(sent, 'gx', split_axis=0, concat_axis=0, tiled=True, axis_...]
    pallas_call x1, Pallas kernels: 0.07 us -> 1.66 us  [local(): pl.pallas_call(functools.partial(drift_kernel, plan), out_shape=(shape_of...]
  transfers between devices with their start and end apart: 4 -> 4, of which waited for: 2 -> 2; matrix products, arithmetic and copies ran while one was open for 0% -> 0% of each run, Pallas kernels for 4% -> 8%
where the time goes in v6:
time: 37.8 us; the launch traced here: 37.4 us
  starting transfers between devices  11 us (29%)
  blocking collectives  10.9 us (29%)
  Pallas kernels  8.79 us (23%)
  waiting for transfers between devices  6.04 us (16%)
  between operations  0.75 us (2%)
    all_to_all x1, blocking collectives, local(): lax.all_to_all(back, 'gx', split_axis=0, concat_axis=0, tiled=True, axis_...  10.9 us
    all_to_all x1, starting transfers between devices, local(): lax.all_to_all(sent, 'gx', split_axis=0, concat_axis=0, tiled=True, axis_...  9.08 us
    all_to_all x1, waiting for transfers between devices, local(): lax.all_to_all(sent, 'gx', split_axis=0, concat_axis=0, tiled=True, axis_...  4.46 us
    pallas_call x1, Pallas kernels, local(): pl.pallas_call(functools.partial(update_kernel, plan), out_shape=(shape_o...  3.13 us
    pallas_call x1, Pallas kernels, local(): pl.pallas_call(functools.partial(divergence_kernel, plan), out_shape=(sha...  1.72 us
    pallas_call x1, Pallas kernels, local(): pl.pallas_call(functools.partial(drift_kernel, plan), out_shape=(shape_of...  1.66 us
    ppermute x2, waiting for transfers between devices, local(): got = lax.ppermute(send, 'gx', swap)  1.58 us
    pallas_call x1, Pallas kernels, local(): pl.pallas_call(functools.partial(forward_kernel, plan), out_shape=(shape_...  1.47 us
  transfers between devices with their start and end apart: 4, of which 2 were waited for; matrix products, arithmetic and copies ran while one was open for 0% of the time, Pallas kernels for 8%

profile of v6, /device:TPU:0, one launch (start us, length us, event | category | flops | bytes accessed | tf_op | source)
XLA Modules:
  0.0 37.4 jit_solution(15207298369844738196)
XLA Ops:
  0.6 0.0 copy-start.4
  0.6 0.0 copy-start.1
  0.7 0.0 copy-start.3
  0.7 1.7 %divergence.1 = (f32[576,128]{1,0:T(8,128)S(1)}, f32[576,128]{1,0:T(8,128)S(1)}, f32[576,128]{1,0:T(8,128)S(1)}) custom-call(s32[1]{0:T(128)} %bitcast.index_ref, f32[54,72,128]{2,1,0:T(8,128)} %bitcast.3), custom_call_target="tpu_custom_call" | custom-call | tf_op jit(solution)/shard_map/divergence/pallas_call | solution.py:656
  2.4 0.5 %collective-permute-start = (f32[576,128]{1,0:T(8,128)S(1)}, f32[576,128]{1,0:T(8,128)S(1)}, u32[]{:S(2)}, u32[]{:S(2)}) collective-permute-start(f32[576,128]{1,0:T(8,128)S(1)} %get-tuple-element.16.send_ref), channel_id=1, source_target_pairs={{0,1},{1,0},{2,3},{3,2},{4,5},{5,4},{6,7},{7,6},{8,9},{9,8},{10,11... | collective-permute-start | bytes 884744 | tf_op jit(solution)/shard_map/ppermute | solution.py:670
  2.9 1.3 %collective-permute-start.1 = (f32[576,128]{1,0:T(8,128)S(1)}, f32[576,128]{1,0:T(8,128)S(1)}, u32[]{:S(2)}, u32[]{:S(2)}) collective-permute-start(f32[576,128]{1,0:T(8,128)S(1)} %get-tuple-element.19), channel_id=1, source_target_pairs={{2,1},{4,3},{6,5},{8,7},{10,9},{12,11},{14,13},{15,0},{18,17},{20,... | collective-permute-start | bytes 884744 | tf_op jit(solution)/shard_map/ppermute | solution.py:671
  4.2 0.0 collective-permute-done.got_ref
  4.2 0.0 copy-done.4
  4.2 0.0 copy-done.1
  4.2 0.0 copy-done.3
  4.2 1.5 %forward.1 = (f32[8,72,128]{2,1,0:T(8,128)}, f32[96,512]{1,0:T(8,128)S(1)}, f32[8,128]{1,0:T(8,128)S(1)}) custom-call(s32[1]{0:T(128)} %bitcast.index_ref, f32[576,128]{1,0:T(8,128)S(1)} %get-tuple-element.15.keep_ref, f32[576,128]{1,0:T(8,128)S(1)} %collective-permute-done.got_ref, bf16[2,2,256,256]{3,2,1,0:T(8,128)(2,1)S(1)} %copy-done.3, ...), custom_call_target="tpu_custom_call" | custom-call | tf_op jit(solution)/shard_map/forward/pallas_call | solution.py:672
  5.7 9.1 %all-to-all-start = ((f32[8,72,128]{2,1,0:T(8,128)}), f32[8,72,128]{2,1,0:T(8,128)S(1)}, u32[]{:S(2)}, u32[]{:S(2)}) async-start(f32[8,72,128]{2,1,0:T(8,128)} %get-tuple-element.17), calls=%async_computation | async-start | bytes 589824 | tf_op jit(solution)/shard_map/all_to_all | solution.py:684
  14.8 0.0 collective-permute-done.1.beside_ref
  14.8 1.7 %drift.1 = (f32[8,128]{1,0:T(8,128)S(1)}, f32[6,72,128]{2,1,0:T(8,128)S(1)}, f32[36,128]{1,0:T(8,128)S(1)}) custom-call(s32[1]{0:T(128)} %bitcast.index_ref, f32[8,128]{1,0:T(8,128)S(1)} %get-tuple-element.18.odd_ref, f32[576,128]{1,0:T(8,128)S(1)} %collective-permute-done.1.beside_ref, f32[576,128]{1,0:T(8,128)S(1)} %get-tuple-element.15.keep_ref, ...), custom_call_target="tpu_custom_call" | custom-call | flops 49999998976 | bytes 50000000 | tf_op jit(solution)/shard_map/drift/pallas_call | solution.py:687
  16.5 0.0 copy-start
  16.5 4.5 %all-to-all-done.got_ref = f32[8,72,128]{2,1,0:T(8,128)S(1)} async-done(((f32[8,72,128]{2,1,0:T(8,128)}), f32[8,72,128]{2,1,0:T(8,128)S(1)}, u32[]{:S(2)}, u32[]{:S(2)}) %all-to-all-start) | async-done | bytes 294944 | tf_op jit(solution)/shard_map/all_to_all | solution.py:684
  21.0 0.1 filter.1
  21.1 10.9 %all_to_all.10.got_ref = f32[8,80,128]{2,1,0:T(8,128)S(1)} all-to-all(f32[8,80,128]{2,1,0:T(8,128)S(1)} %filter.1), channel_id=1, replica_groups={{10,8,14,12,6,4,2,0},{11,9,15,13,7,5,3,1},{26,24,30,28,22,20,18,16},{27..., dimensions={0} | all-to-all | bytes 655360 | tf_op jit(solution)/shard_map/all_to_all | solution.py:705
  31.9 0.0 copy-done.2
  31.9 0.7 %backward.1 = (f32[584,128]{1,0:T(8,128)S(1)}, f32[584,128]{1,0:T(8,128)S(1)}) custom-call(s32[1]{0:T(128)} %bitcast.index_ref, f32[8,80,128]{2,1,0:T(8,128)S(1)} %all_to_all.10.got_ref, f32[96,512]{1,0:T(8,128)S(1)} %get-tuple-element.22.odd_ref, bf16[2,2,256,256]{3,2,1,0:T(8,128)(2,1)S(1)} %copy-done.2, bf16[2,192,192]{2,1,0:T(8,128)(2,1)S(1)} %copy-done.1, ...), custom_call_target="tpu_custom_call" | custom-call | tf_op jit(solution)/shard_map/backward/pallas_call | solution.py:708
  32.6 0.1 collective-permute-start.2
  32.7 1.6 %collective-permute-done.2.got_ref = f32[584,128]{1,0:T(8,128)S(1)} collective-permute-done((f32[584,128]{1,0:T(8,128)S(1)}, f32[584,128]{1,0:T(8,128)S(1)}, u32[]{:S(2)}, u32[]{:S(2)}) %collective-permute-start.2) | collective-permute-done | bytes 299040 | tf_op jit(solution)/shard_map/ppermute | solution.py:719
  34.3 0.0 copy-done
  34.3 3.1 %update.1 = (f32[54,72,128]{2,1,0:T(8,128)}, f32[1]{0:T(128)}) custom-call(s32[1]{0:T(128)} %bitcast.index_ref, f32[584,128]{1,0:T(8,128)S(1)} %get-tuple-element.23.keep_ref, f32[584,128]{1,0:T(8,128)S(1)} %collective-permute-done.2.got_ref, f32[54,72,128]{2,1,0:T(8,128)S(1)} %bitcast.5, f32[6,72,128]{2,1,0:T(8,128)S(1)} %get-tuple-element.25.turns_ref), custom_call_target="tpu_custom_call" | custom-call | tf_op jit(solution)/shard_map/update/pallas_call | solution.py:720
  (1 shorter events, 0.0 us)
Async XLA Ops:
  0.6 3.6 %copy-start.4 = (f32[96,128]{1,0:T(8,128)S(1)}, f32[96,128]{1,0:T(8,128)}, u32[]{:S(2)}) copy-start(f32[96,128]{1,0:T(8,128)} %constant.14.clone.modes_ref) | copy-start | bytes 147460
  0.6 3.6 %copy-start.1 = (bf16[2,192,192]{2,1,0:T(8,128)(2,1)S(1)}, bf16[2,192,192]{2,1,0:T(8,128)(2,1)}, u32[]{:S(2)}) copy-start(bf16[2,192,192]{2,1,0:T(8,128)(2,1)} %constant.13.clone.second_ref) | copy-start | bytes 442372
  0.7 3.6 %copy-start.3 = (bf16[2,2,256,256]{3,2,1,0:T(8,128)(2,1)S(1)}, bf16[2,2,256,256]{3,2,1,0:T(8,128)(2,1)}, u32[]{:S(2)}) copy-start(bf16[2,2,256,256]{3,2,1,0:T(8,128)(2,1)} %constant.12.clone.last_ref) | copy-start | bytes 1572868
  2.4 1.8 %collective-permute-start = (f32[576,128]{1,0:T(8,128)S(1)}, f32[576,128]{1,0:T(8,128)S(1)}, u32[]{:S(2)}, u32[]{:S(2)}) collective-permute-start(f32[576,128]{1,0:T(8,128)S(1)} %get-tuple-element.16.send_ref), channel_id=1, source_target_pairs={{0,1},{1,0},{2,3},{3,2},{4,5},{5,4},{6,7},{7,6},{8,9},{9,8},{10,11... | collective-permute-start | bytes 884744 | tf_op jit(solution)/shard_map/ppermute | solution.py:670
  2.9 11.9 %collective-permute-start.1 = (f32[576,128]{1,0:T(8,128)S(1)}, f32[576,128]{1,0:T(8,128)S(1)}, u32[]{:S(2)}, u32[]{:S(2)}) collective-permute-start(f32[576,128]{1,0:T(8,128)S(1)} %get-tuple-element.19), channel_id=1, source_target_pairs={{2,1},{4,3},{6,5},{8,7},{10,9},{12,11},{14,13},{15,0},{18,17},{20,... | collective-permute-start | bytes 884744 | tf_op jit(solution)/shard_map/ppermute | solution.py:671
  5.7 15.2 %all-to-all-start = ((f32[8,72,128]{2,1,0:T(8,128)}), f32[8,72,128]{2,1,0:T(8,128)S(1)}, u32[]{:S(2)}, u32[]{:S(2)}) async-start(f32[8,72,128]{2,1,0:T(8,128)} %get-tuple-element.17), calls=%async_computation | async-start | bytes 589824 | tf_op jit(solution)/shard_map/all_to_all | solution.py:684
  14.8 17.1 %copy-start.2 = (bf16[2,2,256,256]{3,2,1,0:T(8,128)(2,1)S(1)}, bf16[2,2,256,256]{3,2,1,0:T(8,128)(2,1)}, u32[]{:S(2)}) copy-start(bf16[2,2,256,256]{3,2,1,0:T(8,128)(2,1)} %constant.15.clone.last_ref) | copy-start | bytes 1572868
  16.5 17.8 %copy-start = (f32[3,2,3,3,1,9216]{5,4,3,2,1,0:T(1,128)S(1)}, f32[3,2,3,3,1,9216]{5,4,3,2,1,0:T(1,128)}, u32[]{:S(2)}) copy-start(f32[3,2,3,3,1,9216]{5,4,3,2,1,0:T(1,128)} %param.5) | copy-start | bytes 5971972
  32.6 1.7 %collective-permute-start.2 = (f32[584,128]{1,0:T(8,128)S(1)}, f32[584,128]{1,0:T(8,128)S(1)}, u32[]{:S(2)}, u32[]{:S(2)}) collective-permute-start(f32[584,128]{1,0:T(8,128)S(1)} %get-tuple-element.24), channel_id=1, source_target_pairs={{0,1},{1,0},{2,3},{3,2},{4,5},{5,4},{6,7},{7,6},{8,9},{9,8},{10,11... | collective-permute-start | bytes 897032 | tf_op jit(solution)/shard_map/ppermute | solution.py:719

commit v7 on v6

--- a/solution.py
+++ b/solution.py
@@ -212,7 +212,7 @@
 
 
 def forward_kernel(
-    plan, index_ref, keep_ref, got_ref, last_ref, second_ref, modes_ref, sent_ref, odd_ref, drift_ref
+    plan, index_ref, keep_ref, got_ref, last_ref, second_ref, modes_ref, sent_ref, odd_ref, drift_ref, staged, departures
 ):
     rows, groups, folds, side = plan.rows, plan.groups, plan.folds, plan.side
     odd = index_ref[0] % 2
@@ -267,20 +267,34 @@
         odd_ref[:, f * LANES : (f + 1) * LANES] = gain * shared[f]
     below = [even[f] + shared[f] for f in range(4)]
     above = [jnp.where(zero, between[f], after[f] + shared[f]) for f in range(4)]
+    early = tiles * full
+    copies = []
+
+    def leave(begin, size):
+        place = (slice(None), pl.ds(begin, size))
+        copy = pltpu.make_async_copy(staged.at[place], sent_ref.at[place], departures.at[len(copies)])
+        copy.start()
+        copies.append(copy)
+
     for q, fields in enumerate((below, above)):
         for t, value in enumerate(pack(fields, lane, side)):
             at = q * tiles + t
             for j in range(pairs):
                 if full:
-                    sent_ref[plan.place[j], pl.ds(at * full, full), :] = value[j * full : (j + 1) * full]
+                    staged[plan.place[j], pl.ds(at * full, full), :] = value[j * full : (j + 1) * full]
                 if rest:
                     begin = pairs * full + j * rest
-                    sent_ref[plan.place[j], pl.ds(2 * tiles * full + at * rest, rest), :] = value[
+                    staged[plan.place[j], pl.ds(2 * tiles * full + at * rest, rest), :] = value[
                         begin : begin + rest
                     ]
+        if q == 0 and early:
+            leave(0, early)
     spare = plan.sent - 2 * plan.block
     if spare:
-        sent_ref[:, pl.ds(2 * plan.block, spare), :] = jnp.zeros((pairs, spare, LANES), jnp.float32)
+        staged[:, pl.ds(2 * plan.block, spare), :] = jnp.zeros((pairs, spare, LANES), jnp.float32)
+    leave(early, plan.sent - early)
+    for copy in copies:
+        copy.wait()
 
 
 def sum_tiles(value):
@@ -677,7 +691,11 @@
             shape_of(8, LANES),
         ),
         in_specs=[scalar_spec()] + [whole_spec()] * 5,
-        out_specs=(whole_spec(),) * 3,
+        out_specs=(pl.BlockSpec(memory_space=pltpu.HBM), whole_spec(), whole_spec()),
+        scratch_shapes=[
+            pltpu.VMEM((pairs, plan.sent, LANES), jnp.float32),
+            pltpu.SemaphoreType.DMA((2,)),
+        ],
         compiler_params=params(),
         name="forward",
     )(index, keep, got, table["last"], table["second"], table["modes"])

time: 37.8 us -> 37.7 us (level)
  no operation moved by 1% of the time
where the time goes in v7:
time: 37.7 us; the launch traced here: 37.4 us
  starting transfers between devices  11 us (29%)
  blocking collectives  10.9 us (29%)
  Pallas kernels  8.76 us (23%)
  waiting for transfers between devices  6.05 us (16%)
  between operations  0.75 us (2%)
    all_to_all x1, blocking collectives, local(): lax.all_to_all(back, 'gx', split_axis=0, concat_axis=0, tiled=True, axis_...  10.9 us
    all_to_all x1, starting transfers between devices, local(): lax.all_to_all(sent, 'gx', split_axis=0, concat_axis=0, tiled=True, axis_...  9.09 us
    all_to_all x1, waiting for transfers between devices, local(): lax.all_to_all(sent, 'gx', split_axis=0, concat_axis=0, tiled=True, axis_...  4.47 us
    pallas_call x1, Pallas kernels, local(): pl.pallas_call(functools.partial(update_kernel, plan), out_shape=(shape_o...  3.13 us
    pallas_call x1, Pallas kernels, local(): pl.pallas_call(functools.partial(divergence_kernel, plan), out_shape=(sha...  1.72 us
    pallas_call x1, Pallas kernels, local(): pl.pallas_call(functools.partial(drift_kernel, plan), out_shape=(shape_of...  1.66 us
    ppermute x2, waiting for transfers between devices, local(): got = lax.ppermute(send, 'gx', swap)  1.58 us
    pallas_call x1, Pallas kernels, local(): pl.pallas_call(functools.partial(forward_kernel, plan), out_shape=(shape_...  1.44 us
  transfers between devices with their start and end apart: 4, of which 2 were waited for; matrix products, arithmetic and copies ran while one was open for 0% of the time, Pallas kernels for 8%

profile of v7, /device:TPU:0, one launch (start us, length us, event | category | flops | bytes accessed | tf_op | source)
XLA Modules:
  0.0 37.4 jit_solution(11518095668993053197)
XLA Ops:
  0.6 0.0 copy-start.4
  0.6 0.0 copy-start.1
  0.7 0.0 copy-start.3
  0.7 1.7 %divergence.1 = (f32[576,128]{1,0:T(8,128)S(1)}, f32[576,128]{1,0:T(8,128)S(1)}, f32[576,128]{1,0:T(8,128)S(1)}) custom-call(s32[1]{0:T(128)} %bitcast.index_ref, f32[54,72,128]{2,1,0:T(8,128)} %bitcast.3), custom_call_target="tpu_custom_call" | custom-call | tf_op jit(solution)/shard_map/divergence/pallas_call | solution.py:670
  2.4 0.5 %collective-permute-start = (f32[576,128]{1,0:T(8,128)S(1)}, f32[576,128]{1,0:T(8,128)S(1)}, u32[]{:S(2)}, u32[]{:S(2)}) collective-permute-start(f32[576,128]{1,0:T(8,128)S(1)} %get-tuple-element.16.send_ref), channel_id=1, source_target_pairs={{0,1},{1,0},{2,3},{3,2},{4,5},{5,4},{6,7},{7,6},{8,9},{9,8},{10,11... | collective-permute-start | bytes 884744 | tf_op jit(solution)/shard_map/ppermute | solution.py:684
  2.9 1.3 %collective-permute-start.1 = (f32[576,128]{1,0:T(8,128)S(1)}, f32[576,128]{1,0:T(8,128)S(1)}, u32[]{:S(2)}, u32[]{:S(2)}) collective-permute-start(f32[576,128]{1,0:T(8,128)S(1)} %get-tuple-element.19), channel_id=1, source_target_pairs={{2,1},{4,3},{6,5},{8,7},{10,9},{12,11},{14,13},{15,0},{18,17},{20,... | collective-permute-start | bytes 884744 | tf_op jit(solution)/shard_map/ppermute | solution.py:685
  4.2 0.0 collective-permute-done.got_ref
  4.2 0.0 copy-done.4
  4.2 0.0 copy-done.1
  4.2 0.0 copy-done.3
  4.2 1.4 %forward.1 = (f32[8,72,128]{2,1,0:T(8,128)}, f32[96,512]{1,0:T(8,128)S(1)}, f32[8,128]{1,0:T(8,128)S(1)}) custom-call(s32[1]{0:T(128)} %bitcast.index_ref, f32[576,128]{1,0:T(8,128)S(1)} %get-tuple-element.15.keep_ref, f32[576,128]{1,0:T(8,128)S(1)} %collective-permute-done.got_ref, bf16[2,2,256,256]{3,2,1,0:T(8,128)(2,1)S(1)} %copy-done.3, ...), custom_call_target="tpu_custom_call" | custom-call | tf_op jit(solution)/shard_map/forward/pallas_call | solution.py:686
  5.7 9.1 %all-to-all-start = ((f32[8,72,128]{2,1,0:T(8,128)}), f32[8,72,128]{2,1,0:T(8,128)S(1)}, u32[]{:S(2)}, u32[]{:S(2)}) async-start(f32[8,72,128]{2,1,0:T(8,128)} %get-tuple-element.17), calls=%async_computation | async-start | bytes 589824 | tf_op jit(solution)/shard_map/all_to_all | solution.py:702
  14.8 0.0 collective-permute-done.1.beside_ref
  14.8 1.7 %drift.1 = (f32[8,128]{1,0:T(8,128)S(1)}, f32[6,72,128]{2,1,0:T(8,128)S(1)}, f32[36,128]{1,0:T(8,128)S(1)}) custom-call(s32[1]{0:T(128)} %bitcast.index_ref, f32[8,128]{1,0:T(8,128)S(1)} %get-tuple-element.18.odd_ref, f32[576,128]{1,0:T(8,128)S(1)} %collective-permute-done.1.beside_ref, f32[576,128]{1,0:T(8,128)S(1)} %get-tuple-element.15.keep_ref, ...), custom_call_target="tpu_custom_call" | custom-call | flops 49999998976 | bytes 50000000 | tf_op jit(solution)/shard_map/drift/pallas_call | solution.py:705
  16.5 0.0 copy-start
  16.5 4.5 %all-to-all-done.got_ref = f32[8,72,128]{2,1,0:T(8,128)S(1)} async-done(((f32[8,72,128]{2,1,0:T(8,128)}), f32[8,72,128]{2,1,0:T(8,128)S(1)}, u32[]{:S(2)}, u32[]{:S(2)}) %all-to-all-start) | async-done | bytes 294944 | tf_op jit(solution)/shard_map/all_to_all | solution.py:702
  20.9 0.1 filter.1
  21.1 10.9 %all_to_all.10.got_ref = f32[8,80,128]{2,1,0:T(8,128)S(1)} all-to-all(f32[8,80,128]{2,1,0:T(8,128)S(1)} %filter.1), channel_id=1, replica_groups={{10,8,14,12,6,4,2,0},{11,9,15,13,7,5,3,1},{26,24,30,28,22,20,18,16},{27..., dimensions={0} | all-to-all | bytes 655360 | tf_op jit(solution)/shard_map/all_to_all | solution.py:723
  31.9 0.0 copy-done.2
  31.9 0.7 %backward.1 = (f32[584,128]{1,0:T(8,128)S(1)}, f32[584,128]{1,0:T(8,128)S(1)}) custom-call(s32[1]{0:T(128)} %bitcast.index_ref, f32[8,80,128]{2,1,0:T(8,128)S(1)} %all_to_all.10.got_ref, f32[96,512]{1,0:T(8,128)S(1)} %get-tuple-element.22.odd_ref, bf16[2,2,256,256]{3,2,1,0:T(8,128)(2,1)S(1)} %copy-done.2, bf16[2,192,192]{2,1,0:T(8,128)(2,1)S(1)} %copy-done.1, ...), custom_call_target="tpu_custom_call" | custom-call | tf_op jit(solution)/shard_map/backward/pallas_call | solution.py:726
  32.6 0.1 collective-permute-start.2
  32.7 1.6 %collective-permute-done.2.got_ref = f32[584,128]{1,0:T(8,128)S(1)} collective-permute-done((f32[584,128]{1,0:T(8,128)S(1)}, f32[584,128]{1,0:T(8,128)S(1)}, u32[]{:S(2)}, u32[]{:S(2)}) %collective-permute-start.2) | collective-permute-done | bytes 299040 | tf_op jit(solution)/shard_map/ppermute | solution.py:737
  34.3 0.0 copy-done
  34.3 3.1 %update.1 = (f32[54,72,128]{2,1,0:T(8,128)}, f32[1]{0:T(128)}) custom-call(s32[1]{0:T(128)} %bitcast.index_ref, f32[584,128]{1,0:T(8,128)S(1)} %get-tuple-element.23.keep_ref, f32[584,128]{1,0:T(8,128)S(1)} %collective-permute-done.2.got_ref, f32[54,72,128]{2,1,0:T(8,128)S(1)} %bitcast.5, f32[6,72,128]{2,1,0:T(8,128)S(1)} %get-tuple-element.25.turns_ref), custom_call_target="tpu_custom_call" | custom-call | tf_op jit(solution)/shard_map/update/pallas_call | solution.py:738
  (1 shorter events, 0.0 us)
Async XLA Ops:
  0.6 3.6 %copy-start.4 = (f32[96,128]{1,0:T(8,128)S(1)}, f32[96,128]{1,0:T(8,128)}, u32[]{:S(2)}) copy-start(f32[96,128]{1,0:T(8,128)} %constant.14.clone.modes_ref) | copy-start | bytes 147460
  0.6 3.6 %copy-start.1 = (bf16[2,192,192]{2,1,0:T(8,128)(2,1)S(1)}, bf16[2,192,192]{2,1,0:T(8,128)(2,1)}, u32[]{:S(2)}) copy-start(bf16[2,192,192]{2,1,0:T(8,128)(2,1)} %constant.13.clone.second_ref) | copy-start | bytes 442372
  0.7 3.6 %copy-start.3 = (bf16[2,2,256,256]{3,2,1,0:T(8,128)(2,1)S(1)}, bf16[2,2,256,256]{3,2,1,0:T(8,128)(2,1)}, u32[]{:S(2)}) copy-start(bf16[2,2,256,256]{3,2,1,0:T(8,128)(2,1)} %constant.12.clone.last_ref) | copy-start | bytes 1572868
  2.4 1.8 %collective-permute-start = (f32[576,128]{1,0:T(8,128)S(1)}, f32[576,128]{1,0:T(8,128)S(1)}, u32[]{:S(2)}, u32[]{:S(2)}) collective-permute-start(f32[576,128]{1,0:T(8,128)S(1)} %get-tuple-element.16.send_ref), channel_id=1, source_target_pairs={{0,1},{1,0},{2,3},{3,2},{4,5},{5,4},{6,7},{7,6},{8,9},{9,8},{10,11... | collective-permute-start | bytes 884744 | tf_op jit(solution)/shard_map/ppermute | solution.py:684
  2.9 11.9 %collective-permute-start.1 = (f32[576,128]{1,0:T(8,128)S(1)}, f32[576,128]{1,0:T(8,128)S(1)}, u32[]{:S(2)}, u32[]{:S(2)}) collective-permute-start(f32[576,128]{1,0:T(8,128)S(1)} %get-tuple-element.19), channel_id=1, source_target_pairs={{2,1},{4,3},{6,5},{8,7},{10,9},{12,11},{14,13},{15,0},{18,17},{20,... | collective-permute-start | bytes 884744 | tf_op jit(solution)/shard_map/ppermute | solution.py:685
  5.7 15.3 %all-to-all-start = ((f32[8,72,128]{2,1,0:T(8,128)}), f32[8,72,128]{2,1,0:T(8,128)S(1)}, u32[]{:S(2)}, u32[]{:S(2)}) async-start(f32[8,72,128]{2,1,0:T(8,128)} %get-tuple-element.17), calls=%async_computation | async-start | bytes 589824 | tf_op jit(solution)/shard_map/all_to_all | solution.py:702
  14.8 17.1 %copy-start.2 = (bf16[2,2,256,256]{3,2,1,0:T(8,128)(2,1)S(1)}, bf16[2,2,256,256]{3,2,1,0:T(8,128)(2,1)}, u32[]{:S(2)}) copy-start(bf16[2,2,256,256]{3,2,1,0:T(8,128)(2,1)} %constant.15.clone.last_ref) | copy-start | bytes 1572868
  16.5 17.8 %copy-start = (f32[3,2,3,3,1,9216]{5,4,3,2,1,0:T(1,128)S(1)}, f32[3,2,3,3,1,9216]{5,4,3,2,1,0:T(1,128)}, u32[]{:S(2)}) copy-start(f32[3,2,3,3,1,9216]{5,4,3,2,1,0:T(1,128)} %param.5) | copy-start | bytes 5971972
  32.6 1.7 %collective-permute-start.2 = (f32[584,128]{1,0:T(8,128)S(1)}, f32[584,128]{1,0:T(8,128)S(1)}, u32[]{:S(2)}, u32[]{:S(2)}) collective-permute-start(f32[584,128]{1,0:T(8,128)S(1)} %get-tuple-element.24), channel_id=1, source_target_pairs={{0,1},{1,0},{2,3},{3,2},{4,5},{5,4},{6,7},{7,6},{8,9},{9,8},{10,11... | collective-permute-start | bytes 897032 | tf_op jit(solution)/shard_map/ppermute | solution.py:737

commit v8 on v7

--- a/solution.py
+++ b/solution.py
@@ -616,7 +616,7 @@
     for n in range(20):
         wrap(here, n, rows)
     for d in (1, 2, 0):
-        chunks = 1 if d else 3
+        chunks = 1 if d == 1 else 3
         for m in range(chunks):
             part = tiles // chunks
 
@@ -744,7 +744,7 @@
             pltpu.VMEM((20, rows + 16, LANES), jnp.float32),
             pltpu.VMEM((20, rows, LANES), jnp.float32),
             pltpu.VMEM((54, rows, LANES), jnp.float32),
-            pltpu.SemaphoreType.DMA((5,)),
+            pltpu.SemaphoreType.DMA((7,)),
         ],
         compiler_params=params(),
         name="update",

time: 37.7 us -> 37.8 us (level)
  no operation moved by 1% of the time
where the time goes in v8:
time: 37.8 us; the launch traced here: 37.4 us
  starting transfers between devices  11 us (29%)
  blocking collectives  10.9 us (29%)
  Pallas kernels  8.78 us (23%)
  waiting for transfers between devices  6.05 us (16%)
  between operations  0.75 us (2%)
    all_to_all x1, blocking collectives, local(): lax.all_to_all(back, 'gx', split_axis=0, concat_axis=0, tiled=True, axis_...  10.9 us
    all_to_all x1, starting transfers between devices, local(): lax.all_to_all(sent, 'gx', split_axis=0, concat_axis=0, tiled=True, axis_...  9.09 us
    all_to_all x1, waiting for transfers between devices, local(): lax.all_to_all(sent, 'gx', split_axis=0, concat_axis=0, tiled=True, axis_...  4.47 us
    pallas_call x1, Pallas kernels, local(): pl.pallas_call(functools.partial(update_kernel, plan), out_shape=(shape_o...  3.15 us
    pallas_call x1, Pallas kernels, local(): pl.pallas_call(functools.partial(divergence_kernel, plan), out_shape=(sha...  1.72 us
    pallas_call x1, Pallas kernels, local(): pl.pallas_call(functools.partial(drift_kernel, plan), out_shape=(shape_of...  1.66 us
    ppermute x2, waiting for transfers between devices, local(): got = lax.ppermute(send, 'gx', swap)  1.58 us
    pallas_call x1, Pallas kernels, local(): pl.pallas_call(functools.partial(forward_kernel, plan), out_shape=(shape_...  1.44 us
  transfers between devices with their start and end apart: 4, of which 2 were waited for; matrix products, arithmetic and copies ran while one was open for 0% of the time, Pallas kernels for 8%

profile of v8, /device:TPU:0, one launch (start us, length us, event | category | flops | bytes accessed | tf_op | source)
XLA Modules:
  0.0 37.4 jit_solution(3783455093561600133)
XLA Ops:
  0.6 0.0 copy-start.4
  0.6 0.0 copy-start.1
  0.7 0.0 copy-start.3
  0.7 1.7 %divergence.1 = (f32[576,128]{1,0:T(8,128)S(1)}, f32[576,128]{1,0:T(8,128)S(1)}, f32[576,128]{1,0:T(8,128)S(1)}) custom-call(s32[1]{0:T(128)} %bitcast.index_ref, f32[54,72,128]{2,1,0:T(8,128)} %bitcast.3), custom_call_target="tpu_custom_call" | custom-call | tf_op jit(solution)/shard_map/divergence/pallas_call | solution.py:670
  2.4 0.5 %collective-permute-start = (f32[576,128]{1,0:T(8,128)S(1)}, f32[576,128]{1,0:T(8,128)S(1)}, u32[]{:S(2)}, u32[]{:S(2)}) collective-permute-start(f32[576,128]{1,0:T(8,128)S(1)} %get-tuple-element.16.send_ref), channel_id=1, source_target_pairs={{0,1},{1,0},{2,3},{3,2},{4,5},{5,4},{6,7},{7,6},{8,9},{9,8},{10,11... | collective-permute-start | bytes 884744 | tf_op jit(solution)/shard_map/ppermute | solution.py:684
  2.9 1.3 %collective-permute-start.1 = (f32[576,128]{1,0:T(8,128)S(1)}, f32[576,128]{1,0:T(8,128)S(1)}, u32[]{:S(2)}, u32[]{:S(2)}) collective-permute-start(f32[576,128]{1,0:T(8,128)S(1)} %get-tuple-element.19), channel_id=1, source_target_pairs={{2,1},{4,3},{6,5},{8,7},{10,9},{12,11},{14,13},{15,0},{18,17},{20,... | collective-permute-start | bytes 884744 | tf_op jit(solution)/shard_map/ppermute | solution.py:685
  4.2 0.0 collective-permute-done.got_ref
  4.2 0.0 copy-done.4
  4.2 0.0 copy-done.1
  4.2 0.0 copy-done.3
  4.2 1.4 %forward.1 = (f32[8,72,128]{2,1,0:T(8,128)}, f32[96,512]{1,0:T(8,128)S(1)}, f32[8,128]{1,0:T(8,128)S(1)}) custom-call(s32[1]{0:T(128)} %bitcast.index_ref, f32[576,128]{1,0:T(8,128)S(1)} %get-tuple-element.15.keep_ref, f32[576,128]{1,0:T(8,128)S(1)} %collective-permute-done.got_ref, bf16[2,2,256,256]{3,2,1,0:T(8,128)(2,1)S(1)} %copy-done.3, ...), custom_call_target="tpu_custom_call" | custom-call | tf_op jit(solution)/shard_map/forward/pallas_call | solution.py:686
  5.7 9.1 %all-to-all-start = ((f32[8,72,128]{2,1,0:T(8,128)}), f32[8,72,128]{2,1,0:T(8,128)S(1)}, u32[]{:S(2)}, u32[]{:S(2)}) async-start(f32[8,72,128]{2,1,0:T(8,128)} %get-tuple-element.17), calls=%async_computation | async-start | bytes 589824 | tf_op jit(solution)/shard_map/all_to_all | solution.py:702
  14.8 0.0 collective-permute-done.1.beside_ref
  14.8 1.7 %drift.1 = (f32[8,128]{1,0:T(8,128)S(1)}, f32[6,72,128]{2,1,0:T(8,128)S(1)}, f32[36,128]{1,0:T(8,128)S(1)}) custom-call(s32[1]{0:T(128)} %bitcast.index_ref, f32[8,128]{1,0:T(8,128)S(1)} %get-tuple-element.18.odd_ref, f32[576,128]{1,0:T(8,128)S(1)} %collective-permute-done.1.beside_ref, f32[576,128]{1,0:T(8,128)S(1)} %get-tuple-element.15.keep_ref, ...), custom_call_target="tpu_custom_call" | custom-call | flops 49999998976 | bytes 50000000 | tf_op jit(solution)/shard_map/drift/pallas_call | solution.py:705
  16.5 0.0 copy-start
  16.5 4.5 %all-to-all-done.got_ref = f32[8,72,128]{2,1,0:T(8,128)S(1)} async-done(((f32[8,72,128]{2,1,0:T(8,128)}), f32[8,72,128]{2,1,0:T(8,128)S(1)}, u32[]{:S(2)}, u32[]{:S(2)}) %all-to-all-start) | async-done | bytes 294944 | tf_op jit(solution)/shard_map/all_to_all | solution.py:702
  20.9 0.1 filter.1
  21.1 10.9 %all_to_all.10.got_ref = f32[8,80,128]{2,1,0:T(8,128)S(1)} all-to-all(f32[8,80,128]{2,1,0:T(8,128)S(1)} %filter.1), channel_id=1, replica_groups={{10,8,14,12,6,4,2,0},{11,9,15,13,7,5,3,1},{26,24,30,28,22,20,18,16},{27..., dimensions={0} | all-to-all | bytes 655360 | tf_op jit(solution)/shard_map/all_to_all | solution.py:723
  31.9 0.0 copy-done.2
  31.9 0.7 %backward.1 = (f32[584,128]{1,0:T(8,128)S(1)}, f32[584,128]{1,0:T(8,128)S(1)}) custom-call(s32[1]{0:T(128)} %bitcast.index_ref, f32[8,80,128]{2,1,0:T(8,128)S(1)} %all_to_all.10.got_ref, f32[96,512]{1,0:T(8,128)S(1)} %get-tuple-element.22.odd_ref, bf16[2,2,256,256]{3,2,1,0:T(8,128)(2,1)S(1)} %copy-done.2, bf16[2,192,192]{2,1,0:T(8,128)(2,1)S(1)} %copy-done.1, ...), custom_call_target="tpu_custom_call" | custom-call | tf_op jit(solution)/shard_map/backward/pallas_call | solution.py:726
  32.6 0.1 collective-permute-start.2
  32.7 1.6 %collective-permute-done.2.got_ref = f32[584,128]{1,0:T(8,128)S(1)} collective-permute-done((f32[584,128]{1,0:T(8,128)S(1)}, f32[584,128]{1,0:T(8,128)S(1)}, u32[]{:S(2)}, u32[]{:S(2)}) %collective-permute-start.2) | collective-permute-done | bytes 299040 | tf_op jit(solution)/shard_map/ppermute | solution.py:737
  34.3 0.0 copy-done
  34.3 3.1 %update.1 = (f32[54,72,128]{2,1,0:T(8,128)}, f32[1]{0:T(128)}) custom-call(s32[1]{0:T(128)} %bitcast.index_ref, f32[584,128]{1,0:T(8,128)S(1)} %get-tuple-element.23.keep_ref, f32[584,128]{1,0:T(8,128)S(1)} %collective-permute-done.2.got_ref, f32[54,72,128]{2,1,0:T(8,128)S(1)} %bitcast.5, f32[6,72,128]{2,1,0:T(8,128)S(1)} %get-tuple-element.25.turns_ref), custom_call_target="tpu_custom_call" | custom-call | tf_op jit(solution)/shard_map/update/pallas_call | solution.py:738
  (1 shorter events, 0.0 us)
Async XLA Ops:
  0.6 3.6 %copy-start.4 = (f32[96,128]{1,0:T(8,128)S(1)}, f32[96,128]{1,0:T(8,128)}, u32[]{:S(2)}) copy-start(f32[96,128]{1,0:T(8,128)} %constant.14.clone.modes_ref) | copy-start | bytes 147460
  0.6 3.6 %copy-start.1 = (bf16[2,192,192]{2,1,0:T(8,128)(2,1)S(1)}, bf16[2,192,192]{2,1,0:T(8,128)(2,1)}, u32[]{:S(2)}) copy-start(bf16[2,192,192]{2,1,0:T(8,128)(2,1)} %constant.13.clone.second_ref) | copy-start | bytes 442372
  0.7 3.6 %copy-start.3 = (bf16[2,2,256,256]{3,2,1,0:T(8,128)(2,1)S(1)}, bf16[2,2,256,256]{3,2,1,0:T(8,128)(2,1)}, u32[]{:S(2)}) copy-start(bf16[2,2,256,256]{3,2,1,0:T(8,128)(2,1)} %constant.12.clone.last_ref) | copy-start | bytes 1572868
  2.4 1.8 %collective-permute-start = (f32[576,128]{1,0:T(8,128)S(1)}, f32[576,128]{1,0:T(8,128)S(1)}, u32[]{:S(2)}, u32[]{:S(2)}) collective-permute-start(f32[576,128]{1,0:T(8,128)S(1)} %get-tuple-element.16.send_ref), channel_id=1, source_target_pairs={{0,1},{1,0},{2,3},{3,2},{4,5},{5,4},{6,7},{7,6},{8,9},{9,8},{10,11... | collective-permute-start | bytes 884744 | tf_op jit(solution)/shard_map/ppermute | solution.py:684
  2.9 11.9 %collective-permute-start.1 = (f32[576,128]{1,0:T(8,128)S(1)}, f32[576,128]{1,0:T(8,128)S(1)}, u32[]{:S(2)}, u32[]{:S(2)}) collective-permute-start(f32[576,128]{1,0:T(8,128)S(1)} %get-tuple-element.19), channel_id=1, source_target_pairs={{2,1},{4,3},{6,5},{8,7},{10,9},{12,11},{14,13},{15,0},{18,17},{20,... | collective-permute-start | bytes 884744 | tf_op jit(solution)/shard_map/ppermute | solution.py:685
  5.7 15.3 %all-to-all-start = ((f32[8,72,128]{2,1,0:T(8,128)}), f32[8,72,128]{2,1,0:T(8,128)S(1)}, u32[]{:S(2)}, u32[]{:S(2)}) async-start(f32[8,72,128]{2,1,0:T(8,128)} %get-tuple-element.17), calls=%async_computation | async-start | bytes 589824 | tf_op jit(solution)/shard_map/all_to_all | solution.py:702
  14.8 17.1 %copy-start.2 = (bf16[2,2,256,256]{3,2,1,0:T(8,128)(2,1)S(1)}, bf16[2,2,256,256]{3,2,1,0:T(8,128)(2,1)}, u32[]{:S(2)}) copy-start(bf16[2,2,256,256]{3,2,1,0:T(8,128)(2,1)} %constant.15.clone.last_ref) | copy-start | bytes 1572868
  16.5 17.8 %copy-start = (f32[3,2,3,3,1,9216]{5,4,3,2,1,0:T(1,128)S(1)}, f32[3,2,3,3,1,9216]{5,4,3,2,1,0:T(1,128)}, u32[]{:S(2)}) copy-start(f32[3,2,3,3,1,9216]{5,4,3,2,1,0:T(1,128)} %param.5) | copy-start | bytes 5971972
  32.6 1.7 %collective-permute-start.2 = (f32[584,128]{1,0:T(8,128)S(1)}, f32[584,128]{1,0:T(8,128)S(1)}, u32[]{:S(2)}, u32[]{:S(2)}) collective-permute-start(f32[584,128]{1,0:T(8,128)S(1)} %get-tuple-element.24), channel_id=1, source_target_pairs={{0,1},{1,0},{2,3},{3,2},{4,5},{5,4},{6,7},{7,6},{8,9},{9,8},{10,11... | collective-permute-start | bytes 897032 | tf_op jit(solution)/shard_map/ppermute | solution.py:737
